TPU v7x, 32 devices: a whole 2x2x4 slice. The times are simulated.
32 devices in a mesh: groups: 2 (over x), gx: 16 (over z, y, core).
Axes of the slice: x: 2, y: 2, z: 4, core: 2. Of those that a mesh axis runs over, the one named last changes fastest.
Arguments:
- right_side: float32 [3, 2048, 512], P(None, ('groups', 'gx')), parts along dimension 1, may hold values from -135 to 135
- masses: float32 [2048, 512], P(('groups', 'gx')), parts along dimension 0, may hold values from 0.5 to 2
- stiffness: float32 [2, 2048, 512], P(None, ('groups', 'gx')), parts along dimension 1, may hold values from 0.3 to 3
- hessian: bfloat16 [1152, 384, 384], P(('groups', 'gx')), parts along dimension 0, may hold values from -1 to 4, as said below
- send_list: int32 [32, 48], P(('groups', 'gx')), parts along dimension 0, may hold values from 0 to 255, as said below
- pair_refs: int32 [1152, 2], P(('groups', 'gx')), parts along dimension 0, may hold values from 0 to 47, as said below
- counts: int32 [32], P(('groups', 'gx')), parts along dimension 0, may hold values from 18 to 36, as said below
Outputs:
- solution: float32 [3, 2048, 512], P(None, ('groups', 'gx')), parts along dimension 1
- residual: float32 [3, 2048, 512], P(None, ('groups', 'gx')), parts along dimension 1
There are 2 independent parts, one for each index of `groups`. A program takes and returns all parts, laid end to end along the dimension named above; each array names one. Nothing has to cross between parts.
Inputs may be any that keep to these rules, and one draw needn't show every extreme that they name: `hessian`: every block is symmetric. `send_list`: row d names 48 different blocks of device d. `pair_refs`: the two positions of a row differ. `counts`: some device holds 36 live slots.
All inputs are finite; a program needn't handle non-finite values.
Results may differ from a plain program's by a relative error of at most 0.018.
Values may be sent and summed in bfloat16 or wider, within the bound.
No kernel may reach another device: no remote copies, remote signals or barrier semaphores. Data moves between devices by JAX's collectives and lax.ppermute only.
A program may use at most 64 MiB of HBM per device.

v0:
```python
import jax
import jax.numpy as jnp
from jax import lax
from jax.sharding import PartitionSpec as P

ITERS = 3


HIGH = lax.Precision.HIGHEST


def shifted(value, axis, steps):
    count = lax.axis_size(axis)
    initial, last = (max(0, -steps), min(count, count - steps))
    return lax.ppermute(value, axis, [(source, source + steps) for source in range(initial, last)])


def extended(block, sides, width):
    for axis, dim in sides:
        count = lax.axis_size(axis)
        forward = [(i, i + 1) for i in range(count - 1)]
        backward = [(target, source) for source, target in forward]
        low = lax.ppermute(
            lax.slice_in_dim(block, block.shape[dim] - width, None, axis=dim), axis, forward
        )
        high = lax.ppermute(lax.slice_in_dim(block, 0, width, axis=dim), axis, backward)
        block = jnp.concatenate([low, block, high], axis=dim)
    return block


def to_blocks(grid_vals, block_len):
    comp_count, row_count, col_count = grid_vals.shape
    shaped = grid_vals.reshape(comp_count, row_count, col_count // block_len, block_len)
    return shaped.transpose(1, 2, 0, 3).reshape(
        row_count * (col_count // block_len), comp_count * block_len
    )


def from_blocks(blocks, row_count, col_count, block_len):
    shaped = blocks.reshape(row_count, col_count // block_len, 3, block_len)
    return shaped.transpose(2, 0, 1, 3).reshape(3, row_count, col_count)


def membrane(padded, kx_here, kx_prev, ky_here, ky_prev):
    centre = padded[:, 1:-1, :]
    next_row = padded[:, 2:, :]
    prev_row = padded[:, :-2, :]
    zero_col = jnp.zeros_like(centre[:, :, :1])
    next_col = jnp.concatenate([centre[:, :, 1:], zero_col], axis=2)
    prev_col = jnp.concatenate([zero_col, centre[:, :, :-1]], axis=2)
    return (
        kx_here * (centre - next_row)
        + kx_prev * (centre - prev_row)
        + ky_here * (centre - next_col)
        + ky_prev * (centre - prev_col)
    )


def owner_products(received, hessian, pair_refs, live_mask):
    first_x = received[pair_refs[:, 0]]
    second = received[pair_refs[:, 1]]
    stacked = jnp.stack([first_x, second], axis=1)
    products = jnp.einsum("hij,hkj->hki", hessian, stacked, preferred_element_type=jnp.float32)
    pushes = (products[:, 0] - products[:, 1]) * live_mask[:, None]
    slots_all = jnp.arange(received.shape[0], dtype=jnp.int32)
    signs_map = (pair_refs[:, 0:1] == slots_all[None, :]).astype(jnp.float32) - (
        pair_refs[:, 1:2] == slots_all[None, :]
    ).astype(jnp.float32)
    return jnp.einsum("hp,hi->pi", signs_map, pushes, precision=HIGH)


def per_device(right_side, masses, stiffness, hessian, send_list, pair_refs, counts):
    comp_count, row_count, col_count = right_side.shape
    block_width = hessian.shape[1]
    block_len = block_width // 3
    slot_count = hessian.shape[0]
    peer_count = lax.axis_size("gx")
    my_index = lax.axis_index("gx")
    send_order = send_list[0]
    send_count = send_order.shape[0]
    cap_slots = send_count // peer_count
    global_row = my_index * row_count + jnp.arange(row_count, dtype=jnp.int32)
    kx_here = jnp.where((global_row < row_count * peer_count - 1)[:, None], stiffness[0], 0.0)
    rim_row = shifted(kx_here[-1:], "gx", 1)
    kx_prev = jnp.concatenate([rim_row, kx_here[:-1]], axis=0)
    col_ids = jnp.arange(col_count, dtype=jnp.int32)
    ky_here = jnp.where((col_ids < col_count - 1)[None, :], stiffness[1], 0.0)
    ky_prev = jnp.concatenate([jnp.zeros_like(ky_here[:, :1]), ky_here[:, :-1]], axis=1)
    live_mask = (jnp.arange(slot_count, dtype=jnp.int32) < counts[0]).astype(jnp.float32)

    def squares(vector):
        return lax.psum(jnp.sum(vector * vector), "gx")

    solution = jnp.zeros_like(right_side)
    residual = right_side
    direction = right_side
    norm_now = squares(residual)
    for step_index in range(ITERS):
        block_rows = to_blocks(direction, block_len)
        outgoing = block_rows[send_order]
        arrived = lax.all_to_all(
            outgoing.astype(jnp.bfloat16).reshape(peer_count, cap_slots, block_width),
            "gx",
            split_axis=0,
            concat_axis=0,
            tiled=True,
        )
        received = arrived.reshape(send_count, block_width)
        padded = extended(direction.astype(jnp.bfloat16), (("gx", 1),), 1).astype(direction.dtype)
        pushes = owner_products(received, hessian, pair_refs, live_mask)
        returned = lax.all_to_all(
            pushes.reshape(peer_count, cap_slots, block_width).astype(jnp.bfloat16),
            "gx",
            split_axis=0,
            concat_axis=0,
            tiled=True,
        ).astype(jnp.float32)
        contact = (
            jnp.zeros_like(block_rows).at[send_order].add(returned.reshape(send_count, block_width))
        )
        image_vec = (
            masses[None] * direction
            + membrane(padded, kx_here, kx_prev, ky_here, ky_prev)
            + from_blocks(contact, row_count, col_count, block_len)
        )
        step_len = norm_now / lax.psum(jnp.sum(direction * image_vec), "gx")
        solution = solution + step_len * direction
        residual = residual - step_len * image_vec
        norm_next = squares(residual)
        direction = residual + norm_next / norm_now * direction
        norm_now = norm_next
    return (solution, residual)


def solution(mesh):
    placed = (
        P(None, ("groups", "gx"), None),
        P(("groups", "gx"), None),
        P(None, ("groups", "gx"), None),
        P(("groups", "gx"), None, None),
        P(("groups", "gx"), None),
        P(("groups", "gx"), None),
        P(("groups", "gx")),
    )
    return jax.shard_map(
        per_device,
        mesh=mesh,
        in_specs=placed,
        out_specs=(P(None, ("groups", "gx"), None), P(None, ("groups", "gx"), None)),
        check_vma=False,
    )
```

profile of v0, /device:TPU:0, one launch (start us, length us, event | category | flops | bytes accessed | tf_op | source)
XLA Modules:
  0.0 296.2 jit_solution(9662415191437659834)
XLA Ops:
  1.6 2.4 collective-permute-start.2
  5.1 4.7 %collective-permute-start = (bf16[3,1,512]{2,1,0:T(2,128)(2,1)S(1)}, bf16[3,1,512]{2,1,0:T(2,128)(2,1)S(1)}, u32[]{:S(2)}, u32[]{:S(2)}) collective-permute-start(bf16[3,1,512]{2,1,0:T(2,128)(2,1)S(1)} %get-tuple-element.30), channel_id=1, source_target_pairs={{0,1},{1,2},{2,3},{3,4},{4,5},{5,6},{6,7},{7,8},{8,9},{9,10},{10,1... | collective-permute-start | bytes 9224 | tf_op jit(solution)/shard_map/ppermute | solution.py:23
  9.8 1.3 collective-permute-start.1
  14.3 6.7 %all-to-all-start = ((bf16[16,3,384]{2,1,0:T(4,128)(2,1)}), bf16[16,3,384]{2,1,0:T(4,128)(2,1)S(1)}, u32[]{:S(2)}, u32[]{:S(2)}) async-start(bf16[16,3,384]{2,1,0:T(4,128)(2,1)} %convert_element_type.89), calls=%async_computation | async-start | bytes 98304 | tf_op jit(solution)/shard_map/all_to_all | solution.py:101
  23.8 4.0 %all-to-all-done = bf16[16,3,384]{2,1,0:T(4,128)(2,1)S(1)} async-done(((bf16[16,3,384]{2,1,0:T(4,128)(2,1)}), bf16[16,3,384]{2,1,0:T(4,128)(2,1)S(1)}, u32[]{:S(2)}, u32[]{:S(2)}) %all-to-all-start) | async-done | bytes 36896 | tf_op jit(solution)/shard_map/all_to_all | solution.py:101
  29.2 7.1 %fusion.36 = f32[36,2,384]{2,1,0:T(2,128)S(1)} fusion(bf16[36,384,384]{2,1,0:T(8,128)(2,1)} %param.10, bf16[36,1,384]{2,1,0:T(2,128)(2,1)S(1)} %copy.41, bf16[36,1,384]{2,1,0:T(2,128)(2,1)S(1)} %copy.40), kind=kOutput, calls=%fused_computation.84 | convolution fusion | flops 21344256 | bytes 10782720 | tf_op jit(solution)/shard_map/hij,hkj->hki/dot_general | solution.py:63
  37.4 3.5 %all-to-all-start.1 = ((bf16[16,3,384]{2,1,0:T(4,128)(2,1)}), bf16[16,3,384]{2,1,0:T(4,128)(2,1)S(1)}, u32[]{:S(2)}, u32[]{:S(2)}) async-start(bf16[16,3,384]{2,1,0:T(4,128)(2,1)} %copy.42), calls=%async_computation.1 | async-start | bytes 98304 | tf_op jit(solution)/shard_map/all_to_all | solution.py:111
  41.1 6.5 %all-to-all-done.1 = bf16[16,3,384]{2,1,0:T(4,128)(2,1)S(1)} async-done(((bf16[16,3,384]{2,1,0:T(4,128)(2,1)}), bf16[16,3,384]{2,1,0:T(4,128)(2,1)S(1)}, u32[]{:S(2)}, u32[]{:S(2)}) %all-to-all-start.1) | async-done | bytes 36896 | tf_op jit(solution)/shard_map/all_to_all | solution.py:111
  50.0 30.3 %all-reduce.7 = (f32[]{:T(128)}, f32[]{:T(128)}) all-reduce(f32[]{:T(128)} %get-tuple-element.3, f32[]{:T(128)} %get-tuple-element.2), channel_id=1, replica_groups=mesh['groups'=2,'gx'=16] {'gx'}, use_global_device_ids=true, to_apply=%region_1.2 | all-reduce | flops 2 | bytes 16 | tf_op jit(solution)/shard_map/psum | solution.py:92
  82.4 30.2 %psum.44 = f32[]{:T(128)} all-reduce(f32[]{:T(128)} %multiply_reduce_fusion.3), channel_id=1, replica_groups=mesh['groups'=2,'gx'=16] {'gx'}, use_global_device_ids=true, to_apply=%region_6.7 | all-reduce | flops 1 | bytes 8 | tf_op jit(solution)/shard_map/psum | solution.py:92
  114.1 1.8 collective-permute-start.3
  115.8 1.3 collective-permute-start.4
  118.7 3.6 %all-to-all-start.2 = ((bf16[16,3,384]{2,1,0:T(4,128)(2,1)}), bf16[16,3,384]{2,1,0:T(4,128)(2,1)S(1)}, u32[]{:S(2)}, u32[]{:S(2)}) async-start(bf16[16,3,384]{2,1,0:T(4,128)(2,1)} %convert_element_type.95), calls=%async_computation.2 | async-start | bytes 98304 | tf_op jit(solution)/shard_map/all_to_all | solution.py:101
  122.5 6.7 %all-to-all-done.2 = bf16[16,3,384]{2,1,0:T(4,128)(2,1)S(1)} async-done(((bf16[16,3,384]{2,1,0:T(4,128)(2,1)}), bf16[16,3,384]{2,1,0:T(4,128)(2,1)S(1)}, u32[]{:S(2)}, u32[]{:S(2)}) %all-to-all-start.2) | async-done | bytes 36896 | tf_op jit(solution)/shard_map/all_to_all | solution.py:101
  130.6 7.1 %fusion.40 = f32[36,2,384]{2,1,0:T(2,128)S(1)} fusion(bf16[36,384,384]{2,1,0:T(8,128)(2,1)} %param.10, bf16[36,1,384]{2,1,0:T(2,128)(2,1)S(1)} %copy.46, bf16[36,1,384]{2,1,0:T(2,128)(2,1)S(1)} %copy.45), kind=kOutput, calls=%fused_computation.88 | convolution fusion | flops 21344256 | bytes 10782720 | tf_op jit(solution)/shard_map/hij,hkj->hki/dot_general | solution.py:63
  138.7 3.5 %all-to-all-start.3 = ((bf16[16,3,384]{2,1,0:T(4,128)(2,1)}), bf16[16,3,384]{2,1,0:T(4,128)(2,1)S(1)}, u32[]{:S(2)}, u32[]{:S(2)}) async-start(bf16[16,3,384]{2,1,0:T(4,128)(2,1)} %copy.47), calls=%async_computation.3 | async-start | bytes 98304 | tf_op jit(solution)/shard_map/all_to_all | solution.py:111
  142.4 6.5 %all-to-all-done.3 = bf16[16,3,384]{2,1,0:T(4,128)(2,1)S(1)} async-done(((bf16[16,3,384]{2,1,0:T(4,128)(2,1)}), bf16[16,3,384]{2,1,0:T(4,128)(2,1)S(1)}, u32[]{:S(2)}, u32[]{:S(2)}) %all-to-all-start.3) | async-done | bytes 36896 | tf_op jit(solution)/shard_map/all_to_all | solution.py:111
  149.0 1.6 scatter_custom_fusion.1
  152.6 1.9 reshape.206
  154.5 1.9 multiply_reduce_fusion.2
  156.4 30.3 %psum.45 = f32[]{:T(128)} all-reduce(f32[]{:T(128)} %get-tuple-element.12), channel_id=1, replica_groups=mesh['groups'=2,'gx'=16] {'gx'}, use_global_device_ids=true, to_apply=%region_9.10 | all-reduce | flops 1 | bytes 8 | tf_op jit(solution)/shard_map/psum | solution.py:126
  188.8 30.2 %psum.46 = f32[]{:T(128)} all-reduce(f32[]{:T(128)} %get-tuple-element.10), channel_id=1, replica_groups=mesh['groups'=2,'gx'=16] {'gx'}, use_global_device_ids=true, to_apply=%region_11.12 | all-reduce | flops 1 | bytes 8 | tf_op jit(solution)/shard_map/psum | solution.py:92
  220.5 1.8 collective-permute-start.5
  225.1 3.7 %all-to-all-start.4 = ((bf16[16,3,384]{2,1,0:T(4,128)(2,1)}), bf16[16,3,384]{2,1,0:T(4,128)(2,1)S(1)}, u32[]{:S(2)}, u32[]{:S(2)}) async-start(bf16[16,3,384]{2,1,0:T(4,128)(2,1)} %convert_element_type.100), calls=%async_computation.4 | async-start | bytes 98304 | tf_op jit(solution)/shard_map/all_to_all | solution.py:101
  228.9 6.6 %all-to-all-done.4 = bf16[16,3,384]{2,1,0:T(4,128)(2,1)S(1)} async-done(((bf16[16,3,384]{2,1,0:T(4,128)(2,1)}), bf16[16,3,384]{2,1,0:T(4,128)(2,1)S(1)}, u32[]{:S(2)}, u32[]{:S(2)}) %all-to-all-start.4) | async-done | bytes 36896 | tf_op jit(solution)/shard_map/all_to_all | solution.py:101
  237.0 7.1 %fusion.44 = f32[36,2,384]{2,1,0:T(2,128)S(1)} fusion(bf16[36,384,384]{2,1,0:T(8,128)(2,1)} %param.10, bf16[36,1,384]{2,1,0:T(2,128)(2,1)S(1)} %copy.51, bf16[36,1,384]{2,1,0:T(2,128)(2,1)S(1)} %copy.50), kind=kOutput, calls=%fused_computation.92 | convolution fusion | flops 21344256 | bytes 10782720 | tf_op jit(solution)/shard_map/hij,hkj->hki/dot_general | solution.py:63
  245.2 3.5 %all-to-all-start.5 = ((bf16[16,3,384]{2,1,0:T(4,128)(2,1)}), bf16[16,3,384]{2,1,0:T(4,128)(2,1)S(1)}, u32[]{:S(2)}, u32[]{:S(2)}) async-start(bf16[16,3,384]{2,1,0:T(4,128)(2,1)} %copy.52), calls=%async_computation.5 | async-start | bytes 98304 | tf_op jit(solution)/shard_map/all_to_all | solution.py:111
  249.5 5.8 %all-to-all-done.5 = bf16[16,3,384]{2,1,0:T(4,128)(2,1)S(1)} async-done(((bf16[16,3,384]{2,1,0:T(4,128)(2,1)}), bf16[16,3,384]{2,1,0:T(4,128)(2,1)S(1)}, u32[]{:S(2)}, u32[]{:S(2)}) %all-to-all-start.5) | async-done | bytes 36896 | tf_op jit(solution)/shard_map/all_to_all | solution.py:111
  255.4 1.6 scatter_custom_fusion.2
  259.0 1.9 reshape.213
  260.9 2.0 multiply_reduce_fusion
  263.0 30.3 %psum.47 = f32[]{:T(128)} all-reduce(f32[]{:T(128)} %get-tuple-element.6), channel_id=1, replica_groups=mesh['groups'=2,'gx'=16] {'gx'}, use_global_device_ids=true, to_apply=%region_14.15 | all-reduce | flops 1 | bytes 8 | tf_op jit(solution)/shard_map/psum | solution.py:126
  (93 shorter events, 30.1 us)
Async XLA Ops:
  1.6 22.0 %collective-permute-start.2 = (f32[1,512]{1,0:T(1,128)S(1)}, f32[1,512]{1,0:T(1,128)S(1)}, u32[]{:S(2)}, u32[]{:S(2)}) collective-permute-start(f32[1,512]{1,0:T(1,128)S(1)} %slice.174), channel_id=1, source_target_pairs={{0,1},{1,2},{2,3},{3,4},{4,5},{5,6},{6,7},{7,8},{8,9},{9,10},{10,1... | collective-permute-start | bytes 6152 | tf_op jit(solution)/shard_map/ppermute | solution.py:15
  5.0 44.0 %copy-start = (f32[3,64,512]{2,1,0:T(8,128)S(1)}, f32[3,64,512]{2,1,0:T(8,128)}, u32[]{:S(2)}) copy-start(f32[3,64,512]{2,1,0:T(8,128)} %param.7) | copy-start | bytes 1179652
  5.0 44.0 %copy-start.1 = (f32[64,512]{1,0:T(8,128)S(1)}, f32[64,512]{1,0:T(8,128)}, u32[]{:S(2)}) copy-start(f32[64,512]{1,0:T(8,128)} %param.8) | copy-start | bytes 393220
  5.1 18.6 %collective-permute-start = (bf16[3,1,512]{2,1,0:T(2,128)(2,1)S(1)}, bf16[3,1,512]{2,1,0:T(2,128)(2,1)S(1)}, u32[]{:S(2)}, u32[]{:S(2)}) collective-permute-start(bf16[3,1,512]{2,1,0:T(2,128)(2,1)S(1)} %get-tuple-element.30), channel_id=1, source_target_pairs={{0,1},{1,2},{2,3},{3,4},{4,5},{5,6},{6,7},{7,8},{8,9},{9,10},{10,1... | collective-permute-start | bytes 9224 | tf_op jit(solution)/shard_map/ppermute | solution.py:23
  9.8 13.9 %collective-permute-start.1 = (bf16[3,1,512]{2,1,0:T(2,128)(2,1)S(1)}, bf16[3,1,512]{2,1,0:T(2,128)(2,1)S(1)}, u32[]{:S(2)}, u32[]{:S(2)}) collective-permute-start(bf16[3,1,512]{2,1,0:T(2,128)(2,1)S(1)} %get-tuple-element.31), channel_id=1, source_target_pairs={{1,0},{2,1},{3,2},{4,3},{5,4},{6,5},{7,6},{8,7},{9,8},{10,9},{11,1... | collective-permute-start | bytes 9224 | tf_op jit(solution)/shard_map/ppermute | solution.py:26
  14.3 13.5 %all-to-all-start = ((bf16[16,3,384]{2,1,0:T(4,128)(2,1)}), bf16[16,3,384]{2,1,0:T(4,128)(2,1)S(1)}, u32[]{:S(2)}, u32[]{:S(2)}) async-start(bf16[16,3,384]{2,1,0:T(4,128)(2,1)} %convert_element_type.89), calls=%async_computation | async-start | bytes 98304 | tf_op jit(solution)/shard_map/all_to_all | solution.py:101
  37.4 10.2 %all-to-all-start.1 = ((bf16[16,3,384]{2,1,0:T(4,128)(2,1)}), bf16[16,3,384]{2,1,0:T(4,128)(2,1)S(1)}, u32[]{:S(2)}, u32[]{:S(2)}) async-start(bf16[16,3,384]{2,1,0:T(4,128)(2,1)} %copy.42), calls=%async_computation.1 | async-start | bytes 98304 | tf_op jit(solution)/shard_map/all_to_all | solution.py:111
  114.1 8.3 %collective-permute-start.3 = (bf16[3,1,512]{2,1,0:T(2,128)(2,1)S(1)}, bf16[3,1,512]{2,1,0:T(2,128)(2,1)S(1)}, u32[]{:S(2)}, u32[]{:S(2)}) collective-permute-start(bf16[3,1,512]{2,1,0:T(2,128)(2,1)S(1)} %get-tuple-element.28), channel_id=1, source_target_pairs={{0,1},{1,2},{2,3},{3,4},{4,5},{5,6},{6,7},{7,8},{8,9},{9,10},{10,1... | collective-permute-start | bytes 9224 | tf_op jit(solution)/shard_map/ppermute | solution.py:23
  115.8 6.6 %collective-permute-start.4 = (bf16[3,1,512]{2,1,0:T(2,128)(2,1)S(1)}, bf16[3,1,512]{2,1,0:T(2,128)(2,1)S(1)}, u32[]{:S(2)}, u32[]{:S(2)}) collective-permute-start(bf16[3,1,512]{2,1,0:T(2,128)(2,1)S(1)} %get-tuple-element.29), channel_id=1, source_target_pairs={{1,0},{2,1},{3,2},{4,3},{5,4},{6,5},{7,6},{8,7},{9,8},{10,9},{11,1... | collective-permute-start | bytes 9224 | tf_op jit(solution)/shard_map/ppermute | solution.py:26
  118.7 10.4 %all-to-all-start.2 = ((bf16[16,3,384]{2,1,0:T(4,128)(2,1)}), bf16[16,3,384]{2,1,0:T(4,128)(2,1)S(1)}, u32[]{:S(2)}, u32[]{:S(2)}) async-start(bf16[16,3,384]{2,1,0:T(4,128)(2,1)} %convert_element_type.95), calls=%async_computation.2 | async-start | bytes 98304 | tf_op jit(solution)/shard_map/all_to_all | solution.py:101
  138.7 10.2 %all-to-all-start.3 = ((bf16[16,3,384]{2,1,0:T(4,128)(2,1)}), bf16[16,3,384]{2,1,0:T(4,128)(2,1)S(1)}, u32[]{:S(2)}, u32[]{:S(2)}) async-start(bf16[16,3,384]{2,1,0:T(4,128)(2,1)} %copy.47), calls=%async_computation.3 | async-start | bytes 98304 | tf_op jit(solution)/shard_map/all_to_all | solution.py:111
  220.5 8.4 %collective-permute-start.5 = (bf16[3,1,512]{2,1,0:T(2,128)(2,1)S(1)}, bf16[3,1,512]{2,1,0:T(2,128)(2,1)S(1)}, u32[]{:S(2)}, u32[]{:S(2)}) collective-permute-start(bf16[3,1,512]{2,1,0:T(2,128)(2,1)S(1)} %get-tuple-element.26), channel_id=1, source_target_pairs={{0,1},{1,2},{2,3},{3,4},{4,5},{5,6},{6,7},{7,8},{8,9},{9,10},{10,1... | collective-permute-start | bytes 9224 | tf_op jit(solution)/shard_map/ppermute | solution.py:23
  222.2 6.6 %collective-permute-start.6 = (bf16[3,1,512]{2,1,0:T(2,128)(2,1)S(1)}, bf16[3,1,512]{2,1,0:T(2,128)(2,1)S(1)}, u32[]{:S(2)}, u32[]{:S(2)}) collective-permute-start(bf16[3,1,512]{2,1,0:T(2,128)(2,1)S(1)} %get-tuple-element.27), channel_id=1, source_target_pairs={{1,0},{2,1},{3,2},{4,3},{5,4},{6,5},{7,6},{8,7},{9,8},{10,9},{11,1... | collective-permute-start | bytes 9224 | tf_op jit(solution)/shard_map/ppermute | solution.py:26
  225.1 10.4 %all-to-all-start.4 = ((bf16[16,3,384]{2,1,0:T(4,128)(2,1)}), bf16[16,3,384]{2,1,0:T(4,128)(2,1)S(1)}, u32[]{:S(2)}, u32[]{:S(2)}) async-start(bf16[16,3,384]{2,1,0:T(4,128)(2,1)} %convert_element_type.100), calls=%async_computation.4 | async-start | bytes 98304 | tf_op jit(solution)/shard_map/all_to_all | solution.py:101
  245.2 10.2 %all-to-all-start.5 = ((bf16[16,3,384]{2,1,0:T(4,128)(2,1)}), bf16[16,3,384]{2,1,0:T(4,128)(2,1)S(1)}, u32[]{:S(2)}, u32[]{:S(2)}) async-start(bf16[16,3,384]{2,1,0:T(4,128)(2,1)} %copy.52), calls=%async_computation.5 | async-start | bytes 98304 | tf_op jit(solution)/shard_map/all_to_all | solution.py:111
where the time goes:
time: 298 us; the launch traced here: 296 us
  blocking collectives  151 us (51%)
  starting transfers between devices  39 us (13%)
  waiting for transfers between devices  36.2 us (12%)
  matrix products  22.2 us (7%)
  local copies, waits for them, and re-layouts  21.5 us (7%)
  other arithmetic  17.5 us (6%)
  between operations  8.63 us (3%)
    psum x3, blocking collectives, squares(): return lax.psum(jnp.sum(vector * vector), 'gx')  90.6 us
    psum x2, blocking collectives, per_device(): step_len = norm_now / lax.psum(jnp.sum(direction * image_vec), 'gx')  60.6 us
    dot_general x3, matrix products, owner_products(): jnp.einsum('hij,hkj->hki', hessian, stacked, preferred_element_type=jnp.f...  21.4 us
    all_to_all x3, waiting for transfers between devices, per_device(): lax.all_to_all(pushes.reshape(peer_count, cap_slots, block_width).astype(...  18.9 us
    all_to_all x3, waiting for transfers between devices, per_device(): lax.all_to_all(outgoing.astype(jnp.bfloat16).reshape(peer_count, cap_slot...  17.3 us
    all_to_all x3, starting transfers between devices, per_device(): lax.all_to_all(outgoing.astype(jnp.bfloat16).reshape(peer_count, cap_slot...  14 us
    all_to_all x3, starting transfers between devices, per_device(): lax.all_to_all(pushes.reshape(peer_count, cap_slots, block_width).astype(...  10.5 us
    ppermute x3, starting transfers between devices, extended(): lax.ppermute(lax.slice_in_dim(block, block.shape[dim] - width, None, axis...  8.2 us
  transfers between devices with their start and end apart: 13, of which 6 were waited for; matrix products, arithmetic and copies ran while one was open for 4% of the time, Pallas kernels for 0%

commit v1 on v0

v1 whole, which is shorter than its diff:
```python
import jax
import jax.numpy as jnp
from jax import lax
from jax.sharding import PartitionSpec as P

HIGH = lax.Precision.HIGHEST


def to_blocks(grid_vals, block_len):
    comp_count, row_count, col_count = grid_vals.shape
    shaped = grid_vals.reshape(comp_count, row_count, col_count // block_len, block_len)
    return shaped.transpose(1, 2, 0, 3).reshape(
        row_count * (col_count // block_len), comp_count * block_len
    )


def from_blocks(blocks, row_count, col_count, block_len):
    shaped = blocks.reshape(row_count, col_count // block_len, 3, block_len)
    return shaped.transpose(2, 0, 1, 3).reshape(3, row_count, col_count)


def local_apply(padded, mass, kx_here, kx_prev, ky_here):
    centre = padded[:, 1:-1, :]
    next_row = padded[:, 2:, :]
    prev_row = padded[:, :-2, :]
    zero_col = jnp.zeros_like(centre[:, :, :1])
    next_col = jnp.concatenate([centre[:, :, 1:], zero_col], axis=2)
    prev_col = jnp.concatenate([zero_col, centre[:, :, :-1]], axis=2)
    ky_prev = jnp.concatenate([jnp.zeros_like(ky_here[:, :1]), ky_here[:, :-1]], axis=1)
    return (
        mass * centre
        + kx_here * (centre - next_row)
        + kx_prev * (centre - prev_row)
        + ky_here * (centre - next_col)
        + ky_prev * (centre - prev_col)
    )


def per_device(right_side, masses, stiffness, hessian, send_list, pair_refs, counts):
    comp_count, row_count, col_count = right_side.shape
    width = hessian.shape[1]
    block_len = width // 3
    slot_count = hessian.shape[0]
    peers = lax.axis_size("gx")
    me = lax.axis_index("gx")
    order = send_list[0]
    cap = order.shape[0] // peers
    f32 = jnp.float32

    up = [(i, i + 1) for i in range(peers - 1)]
    down = [(i + 1, i) for i in range(peers - 1)]

    global_row = me * row_count + jnp.arange(row_count, dtype=jnp.int32)
    kx = jnp.where((global_row < row_count * peers - 1)[:, None], stiffness[0], 0.0)
    col_ids = jnp.arange(col_count, dtype=jnp.int32)
    ky = jnp.where((col_ids < col_count - 1)[None, :], stiffness[1], 0.0)

    low = lax.ppermute(
        jnp.concatenate([right_side[:, -1], kx[-2:], ky[-1:], masses[-1:]], axis=0), "gx", up
    )
    high = lax.ppermute(
        jnp.concatenate([right_side[:, 0], kx[:1], ky[:1], masses[:1]], axis=0), "gx", down
    )
    b_ext = jnp.concatenate([low[:3, None], right_side, high[:3, None]], axis=1)
    kxh_ext = jnp.concatenate([low[4:5], kx, high[3:4]], axis=0)
    kxp_ext = jnp.concatenate([low[3:5], kx], axis=0)
    ky_ext = jnp.concatenate([low[5:6], ky, high[4:5]], axis=0)
    m_ext = jnp.concatenate([low[6:7], masses, high[5:6]], axis=0)

    def own_apply(ext):
        return local_apply(ext, masses, kx, kxp_ext[1:-1], ky)

    live = (jnp.arange(slot_count, dtype=jnp.int32) < counts[0]).astype(f32)
    slots_all = jnp.arange(peers * cap, dtype=jnp.int32)
    signs = (
        (pair_refs[:, 0:1] == slots_all[None, :]).astype(f32)
        - (pair_refs[:, 1:2] == slots_all[None, :]).astype(f32)
    ) * live[:, None]

    def contact(held):
        delta = held[pair_refs[:, 0]] - held[pair_refs[:, 1]]
        coarse = delta.astype(jnp.bfloat16)
        fine = (delta - coarse.astype(f32)).astype(jnp.bfloat16)
        both = jnp.stack([coarse, fine], axis=1)
        products = jnp.einsum("hij,hkj->hki", hessian, both, preferred_element_type=f32)
        return jnp.einsum(
            "hp,hi->pi", signs, products[:, 0] + products[:, 1], precision=HIGH
        )

    def exchange(fields, scalars):
        rows = jnp.stack(fields, axis=1).reshape(peers, cap * len(fields), width)
        line = jnp.zeros((width,), f32).at[: len(scalars)].set(jnp.stack(scalars))
        line = jnp.broadcast_to(line, (peers, 1, width))
        got = lax.all_to_all(
            jnp.concatenate([rows, line], axis=1), "gx", split_axis=0, concat_axis=0, tiled=True
        )
        blocks = got[:, :-1].reshape(peers * cap, len(fields), width)
        sums = jnp.sum(got[:, -1, : len(scalars)], axis=0)
        return [blocks[:, k] for k in range(len(fields))], [sums[k] for k in range(len(scalars))]

    def gathered(field):
        return to_blocks(field, block_len)[order]

    def spread(blocks):
        dense = jnp.zeros((row_count * col_count // block_len, width), f32).at[order].set(blocks)
        return from_blocks(dense, row_count, col_count, block_len)

    db = own_apply(b_ext)
    (b_o, db_o), (rr0, dad0) = exchange(
        [gathered(right_side), gathered(db)],
        [jnp.sum(right_side * right_side), jnp.sum(right_side * db)],
    )
    cb_o = contact(b_o)
    v1_o = db_o + cb_o
    cv1_o = contact(v1_o)
    (cb, cv1), (bcb,) = exchange([cb_o, cv1_o], [jnp.sum(b_o * cb_o)])
    alpha0 = rr0 / (dad0 + bcb)
    v1 = db + spread(cb)
    cv1 = spread(cv1)

    low1 = lax.ppermute(
        jnp.concatenate([v1[:, -2:], cv1[:, -1:]], axis=1), "gx", up
    )
    high1 = lax.ppermute(
        jnp.concatenate([v1[:, :2], cv1[:, :1]], axis=1), "gx", down
    )
    v1_wide = jnp.concatenate([low1[:, :2], v1, high1[:, :2]], axis=1)
    v1_ext = v1_wide[:, 1:-1]
    cv1_ext = jnp.concatenate([low1[:, 2:], cv1, high1[:, 2:]], axis=1)
    dv1_ext = local_apply(v1_wide, m_ext, kxh_ext, kxp_ext, ky_ext)
    v2_ext = dv1_ext + cv1_ext
    r1_ext = b_ext - alpha0 * v1_ext
    w_ext = v1_ext - alpha0 * v2_ext
    r1, w = (r1_ext[:, 1:-1], w_ext[:, 1:-1])

    (dv1_o,), sums = exchange(
        [gathered(dv1_ext[:, 1:-1])],
        [
            jnp.sum(r1 * r1),
            jnp.sum(r1 * w),
            jnp.sum(r1 * v1),
            jnp.sum(right_side * w),
            jnp.sum(right_side * v1),
            jnp.sum(w * w),
            jnp.sum(w * v1),
            jnp.sum(v1 * v1),
        ],
    )
    rr1, r1w, r1v1, bw, bv1, ww, wv1, v1v1 = sums
    beta0 = rr1 / rr0
    dad1 = r1w + beta0 * (r1v1 + bw) + beta0 * beta0 * bv1
    alpha1 = rr1 / dad1
    r1_image = r1w + beta0 * r1v1
    image_sq = ww + 2.0 * beta0 * wv1 + beta0 * beta0 * v1v1
    beta1 = (rr1 - 2.0 * alpha1 * r1_image + alpha1 * alpha1 * image_sq) / rr1

    def advance(b, v1, v2):
        r1 = b - alpha0 * v1
        d1 = r1 + beta0 * b
        r2 = r1 - alpha1 * (v1 - alpha0 * v2 + beta0 * v1)
        return d1, r2, r2 + beta1 * d1

    _, _, d2_o = advance(b_o, v1_o, dv1_o + cv1_o)
    cd2_o = contact(d2_o)
    d1_ext, r2_ext, d2_ext = advance(b_ext, v1_ext, v2_ext)
    d1, r2, d2 = (d1_ext[:, 1:-1], r2_ext[:, 1:-1], d2_ext[:, 1:-1])
    dd2 = own_apply(d2_ext)
    (cd2,), (rr2, dad2) = exchange(
        [cd2_o], [jnp.sum(r2 * r2), jnp.sum(d2 * dd2) + jnp.sum(d2_o * cd2_o)]
    )
    alpha2 = rr2 / dad2
    solution = alpha0 * right_side + alpha1 * d1 + alpha2 * d2
    residual = r2 - alpha2 * (dd2 + spread(cd2))
    return (solution, residual)


def solution(mesh):
    placed = (
        P(None, ("groups", "gx"), None),
        P(("groups", "gx"), None),
        P(None, ("groups", "gx"), None),
        P(("groups", "gx"), None, None),
        P(("groups", "gx"), None),
        P(("groups", "gx"), None),
        P(("groups", "gx")),
    )
    return jax.shard_map(
        per_device,
        mesh=mesh,
        in_specs=placed,
        out_specs=(P(None, ("groups", "gx"), None), P(None, ("groups", "gx"), None)),
        check_vma=False,
    )
```

time: 298 us -> 145 us (0.49)
  blocking collectives: 151 us -> 23.3 us
  waiting for transfers between devices: 36.2 us -> 15.1 us
  starting transfers between devices: 39 us -> 19.1 us
  between operations: 8.63 us -> 15.4 us
  local copies, waits for them, and re-layouts: 21.5 us -> 26.1 us
  other arithmetic: 17.5 us -> 21.3 us
    psum x5 -> x0, blocking collectives: 151 us -> none  [the longest x3 90.6 us: squares(): return lax.psum(jnp.sum(vector * vector), 'gx')]
    all_to_all x0 -> x2, blocking collectives: none -> 23.3 us  [exchange(): lax.all_to_all(jnp.concatenate([rows, line], axis=1), 'gx', split_axis=0,...]
    all_to_all x6 -> x2, waiting for transfers between devices: 36.2 us -> 15 us  [exchange(): lax.all_to_all(jnp.concatenate([rows, line], axis=1), 'gx', split_axis=0,...]
    all_to_all x6 -> x2, starting transfers between devices: 24.5 us -> 12.8 us  [exchange(): lax.all_to_all(jnp.concatenate([rows, line], axis=1), 'gx', split_axis=0,...]
    ppermute x7 -> x4, starting transfers between devices: 14.4 us -> 6.23 us  [the longest x1 2.36 us: per_device(): lax.ppermute(jnp.concatenate([right_side[:, -1], kx[-2:], ky[-1:], masses...]
    another operation x6 -> x7, local copies, waits for them, and re-layouts: 0.26 us -> 5.41 us  [the longest x1 5.11 us: exchange(): line = jnp.zeros((width,), f32).at[:len(scalars)].set(jnp.stack(scalars))]
    slice x7 -> x22, local copies, waits for them, and re-layouts: 1.3 us -> 5.58 us  [the longest x3 1.88 us: exchange(): sums[k]]
    scatter-add x3 -> x0, other arithmetic: 4.15 us -> none  [per_device(): jnp.zeros_like(block_rows).at[send_order]]
  transfers between devices with their start and end apart: 13 -> 6, of which waited for: 6 -> 2; matrix products, arithmetic and copies ran while one was open for 4% -> 7% of each run, Pallas kernels for 0% -> 0%
where the time goes in v1:
time: 145 us; the launch traced here: 144 us
  local copies, waits for them, and re-layouts  26.1 us (18%)
  matrix products  23.8 us (16%)
  blocking collectives  23.3 us (16%)
  other arithmetic  21.3 us (15%)
  starting transfers between devices  19.1 us (13%)
  between operations  15.4 us (11%)
  waiting for transfers between devices  15.1 us (10%)
    all_to_all x2, blocking collectives, exchange(): lax.all_to_all(jnp.concatenate([rows, line], axis=1), 'gx', split_axis=0,...  23.3 us
    dot_general x3, matrix products, contact(): jnp.einsum('hij,hkj->hki', hessian, both, preferred_element_type=f32)  21.5 us
    all_to_all x2, waiting for transfers between devices, exchange(): lax.all_to_all(jnp.concatenate([rows, line], axis=1), 'gx', split_axis=0,...  15 us
    all_to_all x2, starting transfers between devices, exchange(): lax.all_to_all(jnp.concatenate([rows, line], axis=1), 'gx', split_axis=0,...  12.8 us
    another operation x1, local copies, waits for them, and re-layouts, exchange(): line = jnp.zeros((width,), f32).at[:len(scalars)].set(jnp.stack(scalars))  5.11 us
    gather x6, local copies, waits for them, and re-layouts, contact(): delta = held[pair_refs[:, 0]] - held[pair_refs[:, 1]]  3.67 us
  transfers between devices with their start and end apart: 6, of which 2 were waited for; matrix products, arithmetic and copies ran while one was open for 7% of the time, Pallas kernels for 0%

profile of v1, /device:TPU:0, one launch (start us, length us, event | category | flops | bytes accessed | tf_op | source)
XLA Modules:
  0.0 143.9 jit_solution(11629279731017349733)
XLA Ops:
  0.7 1.0 bitcast_select_fusion.1
  3.3 2.4 %collective-permute-start.1 = (f32[7,512]{1,0:T(8,128)S(1)}, f32[7,512]{1,0:T(8,128)S(1)}, u32[]{:S(2)}, u32[]{:S(2)}) collective-permute-start(f32[7,512]{1,0:T(8,128)S(1)} %pad_maximum_fusion.17), channel_id=1, source_target_pairs={{0,1},{1,2},{2,3},{3,4},{4,5},{5,6},{6,7},{7,8},{8,9},{9,10},{10,1... | collective-permute-start | bytes 43016 | tf_op jit(solution)/shard_map/ppermute | solution.py:58
  5.8 1.3 collective-permute-start
  7.1 1.0 select_bitcast_fusion.1
  8.1 1.4 fusion.80
  11.6 1.1 reshape.300
  13.9 2.4 %multiply_reduce_fusion.11 = (f32[]{:T(128)}, f32[]{:T(128)}, f32[3,64,512]{2,1,0:T(8,128)S(1)}) fusion(f32[3,64,512]{2,1,0:T(8,128)} %param.15, f32[3,64,511]{2,1,0:T(8,128)S(1)} %get-tuple-element.79, f32[64,512]{1,0:T(8,128)S(1)} %concatenate.96, f32[3,64,511]{2,1,0:T(8,128)S(1)} %get-tuple-element.78, f32[64,512]{1,0:T(8,128)S(1)} %get-tuple-element.81, ...), kind=kLoop, calls=%fused_computation.65 | loop fusion | flops 1867774 | bytes 2238984 | tf_op jit(solution)/shard_map/reduce_sum | solution.py:111
  17.7 1.4 select_maximum_fusion.1
  19.8 9.3 %all-to-all-start = ((f32[16,7,384]{2,1,0:T(8,128)}), f32[16,7,384]{2,1,0:T(8,128)S(1)}, u32[]{:S(2)}, u32[]{:S(2)}) async-start(f32[16,7,384]{2,1,0:T(8,128)} %pad_maximum_fusion.5), calls=%async_computation | async-start | bytes 393216 | tf_op jit(solution)/shard_map/all_to_all | solution.py:94
  30.6 7.4 %all-to-all-done = f32[16,7,384]{2,1,0:T(8,128)S(1)} async-done(((f32[16,7,384]{2,1,0:T(8,128)}), f32[16,7,384]{2,1,0:T(8,128)S(1)}, u32[]{:S(2)}, u32[]{:S(2)}) %all-to-all-start) | async-done | bytes 172064 | tf_op jit(solution)/shard_map/all_to_all | solution.py:94
  39.7 7.2 %fusion.45 = f32[36,2,384]{2,1,0:T(2,128)S(1)} fusion(bf16[36,384,384]{2,1,0:T(8,128)(2,1)} %param.18, bf16[36,1,384]{2,1,0:T(2,128)(2,1)S(1)} %subtract_convert_fusion.2, bf16[36,1,384]{2,1,0:T(2,128)(2,1)S(1)} %sub.258), kind=kOutput, calls=%fused_computation.111 | convolution fusion | flops 21344256 | bytes 10782720 | tf_op jit(solution)/shard_map/hij,hkj->hki/dot_general | solution.py:85
  46.9 1.0 fusion.31
  49.2 7.2 %fusion.49 = f32[36,2,384]{2,1,0:T(2,128)S(1)} fusion(bf16[36,384,384]{2,1,0:T(8,128)(2,1)} %param.18, bf16[36,1,384]{2,1,0:T(2,128)(2,1)S(1)} %subtract_convert_fusion.1, bf16[36,1,384]{2,1,0:T(2,128)(2,1)S(1)} %sub.257), kind=kOutput, calls=%fused_computation.115 | convolution fusion | flops 21344256 | bytes 10782720 | tf_op jit(solution)/shard_map/hij,hkj->hki/dot_general | solution.py:85
  59.1 3.5 %all-to-all-start.1 = ((f32[16,7,384]{2,1,0:T(8,128)}), f32[16,7,384]{2,1,0:T(8,128)S(1)}, u32[]{:S(2)}, u32[]{:S(2)}) async-start(f32[16,7,384]{2,1,0:T(8,128)} %pad_maximum_fusion.6), calls=%async_computation.1 | async-start | bytes 393216 | tf_op jit(solution)/shard_map/all_to_all | solution.py:94
  64.0 7.6 %all-to-all-done.1 = f32[16,7,384]{2,1,0:T(8,128)S(1)} async-done(((f32[16,7,384]{2,1,0:T(8,128)}), f32[16,7,384]{2,1,0:T(8,128)S(1)}, u32[]{:S(2)}, u32[]{:S(2)}) %all-to-all-start.1) | async-done | bytes 172064 | tf_op jit(solution)/shard_map/all_to_all | solution.py:94
  72.3 0.9 scatter_custom_fusion
  73.7 0.9 scatter_custom_fusion.1
  75.0 1.3 collective-permute-start.2
  76.4 1.3 collective-permute-start.3
  77.7 1.5 %slice_reduce_fusion.2 = f32[]{:T(128)} fusion(f32[16,7,384]{2,1,0:T(8,128)} %copy-done.4), kind=kLoop, calls=%fused_computation.147 | loop fusion | flops 15 | bytes 68 | tf_op jit(solution)/shard_map/reduce_sum | solution.py:98
  81.5 1.5 %fusion.7 = (f32[3,66,512]{2,1,0:T(8,128)S(1)}, f32[3,66,512]{2,1,0:T(8,128)S(1)}) fusion(f32[3,1,512]{2,1,0:T(1,128)S(1)} %slice.439, f32[3,64,512]{2,1,0:T(8,128)S(1)} %reshape.312, f32[3,1,512]{2,1,0:T(1,128)S(1)} %slice.438, f32[3,68,512]{2,1,0:T(8,128)S(1)} %pad_maximum_fusion, f32[]{:T(128)S(6)} %div.18, f32[3,66,511]{2,1,0:T(8,128)S(1)} %get-tuple-element.71, ...), kind=kLoop, calls=%fused_computation.24 | loop fusion | flops 2027520 | bytes 3525076 | tf_op jit(solution)/shard_map/sub | solution.py:133
  84.2 1.0 multiply_reduce_fusion.3
  85.2 5.1 %stack.98 = f32[8]{0:T(128)S(1)} concatenate(f32[1]{0:T(128)} %bitcast.31, f32[1]{0:T(128)} %bitcast.32, f32[1]{0:T(128)} %bitcast.33, f32[1]{0:T(128)} %bitcast.34, f32[1]{0:T(128)} %bitcast.35, f32[1]{0:T(128)} %bitcast.36, f32[1]{0:T(128)} %bitcast.37, f32[1]{0:T(128)} %bitcast.38), dimensions={0} | concatenate | bytes 64 | tf_op jit(solution)/shard_map/stack | solution.py:92
  90.4 13.3 %all_to_all.20 = f32[16,4,384]{2,1,0:T(4,128)S(1)} all-to-all(f32[16,4,384]{2,1,0:T(4,128)S(1)} %pad_maximum_fusion.12), channel_id=1, replica_groups=mesh['groups'=2,'gx'=16] {'gx'}, dimensions={0} | all-to-all | bytes 196608 | tf_op jit(solution)/shard_map/all_to_all | solution.py:94
  113.2 0.9 multiply_add_fusion.2
  115.7 7.1 %fusion.53 = f32[36,2,384]{2,1,0:T(2,128)S(1)} fusion(bf16[36,384,384]{2,1,0:T(8,128)(2,1)} %param.18, bf16[36,1,384]{2,1,0:T(2,128)(2,1)S(1)} %subtract_convert_fusion, bf16[36,1,384]{2,1,0:T(2,128)(2,1)S(1)} %sub.256), kind=kOutput, calls=%fused_computation.119 | convolution fusion | flops 21344256 | bytes 10782720 | tf_op jit(solution)/shard_map/hij,hkj->hki/dot_general | solution.py:85
  123.0 1.0 multiply_reduce_fusion.12
  124.9 1.9 %multiply_reduce_fusion = (f32[]{:T(128)}, f32[3,64,512]{2,1,0:T(8,128)S(1)}) fusion(f32[3,66,512]{2,1,0:T(8,128)S(1)} %get-tuple-element.62, f32[3,64,511]{2,1,0:T(8,128)S(1)} %get-tuple-element.69, f32[64,512]{1,0:T(8,128)S(1)} %concatenate.96, f32[3,64,511]{2,1,0:T(8,128)S(1)} %get-tuple-element.68, f32[64,512]{1,0:T(8,128)} %copy-done.3, ...), kind=kLoop, calls=%fused_computation.54 | loop fusion | flops 1474559 | bytes 3013124 | tf_op jit(solution)/shard_map/reduce_sum | solution.py:169
  128.7 10.0 %all_to_all.21 = f32[16,4,384]{2,1,0:T(4,128)S(1)} all-to-all(f32[16,4,384]{2,1,0:T(4,128)S(1)} %pad_maximum_fusion.13), channel_id=1, replica_groups=mesh['groups'=2,'gx'=16] {'gx'}, dimensions={0} | all-to-all | bytes 196608 | tf_op jit(solution)/shard_map/all_to_all | solution.py:94
  138.8 1.0 scatter_custom_fusion.2
  142.2 0.9 fusion.15
  143.0 0.9 multiply_subtract_fusion.2
  (135 shorter events, 23.0 us)
Async XLA Ops:
  3.3 10.5 %collective-permute-start.1 = (f32[7,512]{1,0:T(8,128)S(1)}, f32[7,512]{1,0:T(8,128)S(1)}, u32[]{:S(2)}, u32[]{:S(2)}) collective-permute-start(f32[7,512]{1,0:T(8,128)S(1)} %pad_maximum_fusion.17), channel_id=1, source_target_pairs={{0,1},{1,2},{2,3},{3,4},{4,5},{5,6},{6,7},{7,8},{8,9},{9,10},{10,1... | collective-permute-start | bytes 43016 | tf_op jit(solution)/shard_map/ppermute | solution.py:58
  5.8 8.1 %collective-permute-start = (f32[6,512]{1,0:T(8,128)S(1)}, f32[6,512]{1,0:T(8,128)S(1)}, u32[]{:S(2)}, u32[]{:S(2)}) collective-permute-start(f32[6,512]{1,0:T(8,128)S(1)} %pad_maximum_fusion.16), channel_id=1, source_target_pairs={{1,0},{2,1},{3,2},{4,3},{5,4},{6,5},{7,6},{8,7},{9,8},{10,9},{11,1... | collective-permute-start | bytes 36872 | tf_op jit(solution)/shard_map/ppermute | solution.py:61
  8.1 73.4 %copy-start.2 = (f32[64,512]{1,0:T(8,128)}, f32[64,512]{1,0:T(8,128)S(1)}, u32[]{:S(2)}) copy-start(f32[64,512]{1,0:T(8,128)S(1)} %get-tuple-element.80) | copy-start | bytes 393220
  8.1 73.4 %copy-start.3 = (f32[64,512]{1,0:T(8,128)}, f32[64,512]{1,0:T(8,128)S(1)}, u32[]{:S(2)}) copy-start(f32[64,512]{1,0:T(8,128)S(1)} %get-tuple-element.81) | copy-start | bytes 393220
  10.2 63.5 %copy-start.7 = (s32[48]{0:T(128)}, s32[48]{0:T(128)S(1)}, u32[]{:S(2)}) copy-start(s32[48]{0:T(128)S(1)} %fusion.66) | copy-start | bytes 580
  19.8 18.3 %all-to-all-start = ((f32[16,7,384]{2,1,0:T(8,128)}), f32[16,7,384]{2,1,0:T(8,128)S(1)}, u32[]{:S(2)}, u32[]{:S(2)}) async-start(f32[16,7,384]{2,1,0:T(8,128)} %pad_maximum_fusion.5), calls=%async_computation | async-start | bytes 393216 | tf_op jit(solution)/shard_map/all_to_all | solution.py:94
  39.6 23.0 %copy-start.1 = (f32[64,512]{1,0:T(8,128)S(1)}, f32[64,512]{1,0:T(8,128)}, u32[]{:S(2)}) copy-start(f32[64,512]{1,0:T(8,128)} %param.16) | copy-start | bytes 393220
  49.2 32.1 %copy-start = (f32[3,64,512]{2,1,0:T(8,128)S(1)}, f32[3,64,512]{2,1,0:T(8,128)}, u32[]{:S(2)}) copy-start(f32[3,64,512]{2,1,0:T(8,128)} %param.15) | copy-start | bytes 1179652
  56.9 0.6 copy-start.6
  59.1 12.5 %all-to-all-start.1 = ((f32[16,7,384]{2,1,0:T(8,128)}), f32[16,7,384]{2,1,0:T(8,128)S(1)}, u32[]{:S(2)}, u32[]{:S(2)}) async-start(f32[16,7,384]{2,1,0:T(8,128)} %pad_maximum_fusion.6), calls=%async_computation.1 | async-start | bytes 393216 | tf_op jit(solution)/shard_map/all_to_all | solution.py:94
  63.4 18.1 %copy-start.5 = (f32[66,512]{1,0:T(8,128)S(1)}, f32[66,512]{1,0:T(8,128)}, u32[]{:S(2)}) copy-start(f32[66,512]{1,0:T(8,128)} %pad_maximum_fusion.9) | copy-start | bytes 405508
  71.6 0.7 copy-start.4
  75.0 6.0 %collective-permute-start.2 = (f32[3,3,512]{2,1,0:T(4,128)S(1)}, f32[3,3,512]{2,1,0:T(4,128)S(1)}, u32[]{:S(2)}, u32[]{:S(2)}) collective-permute-start(f32[3,3,512]{2,1,0:T(4,128)S(1)} %pad_maximum_fusion.14), channel_id=1, source_target_pairs={{0,1},{1,2},{2,3},{3,4},{4,5},{5,6},{6,7},{7,8},{8,9},{9,10},{10,1... | collective-permute-start | bytes 55304 | tf_op jit(solution)/shard_map/ppermute | solution.py:121
  76.4 4.7 %collective-permute-start.3 = (f32[3,3,512]{2,1,0:T(4,128)S(1)}, f32[3,3,512]{2,1,0:T(4,128)S(1)}, u32[]{:S(2)}, u32[]{:S(2)}) collective-permute-start(f32[3,3,512]{2,1,0:T(4,128)S(1)} %pad_maximum_fusion.15), channel_id=1, source_target_pairs={{1,0},{2,1},{3,2},{4,3},{5,4},{6,5},{7,6},{8,7},{9,8},{10,9},{11,1... | collective-permute-start | bytes 55304 | tf_op jit(solution)/shard_map/ppermute | solution.py:124

commit v2 on v0

v2 whole, which is shorter than its diff:
```python
import functools

import jax
import jax.numpy as jnp
from jax import lax
from jax.experimental import pallas as pl
from jax.experimental.pallas import tpu as pltpu
from jax.sharding import PartitionSpec as P

F32 = jnp.float32
VMEM_LIMIT = 40 * 1024 * 1024
CAP = 3
SUMS_TWO, SUMS_ONE = 2 * CAP, CAP


def iota(shape, dim):
    return lax.broadcasted_iota(jnp.int32, shape, dim)


def total(value):
    return jnp.sum(jnp.sum(value, axis=0, keepdims=True), axis=1, keepdims=True)


def line_of(scalars, width):
    lanes = iota((1, width), 1)
    line = jnp.zeros((1, width), F32)
    for k, value in enumerate(scalars):
        line = jnp.where(lanes == k, value, line)
    return line


def line_sum(message, row):
    peers = message.shape[0]
    parts = [message[d, row : row + 1, 0:128] for d in range(peers)]
    while len(parts) > 1:
        parts = [a + b for a, b in zip(parts[::2], parts[1::2])] + (
            parts[-1:] if len(parts) % 2 else []
        )
    return parts[0]


def pick(line, k):
    return line[:, k : k + 1]


def place_of(send, position, col_blocks):
    block = send[0, position]
    return lax.div(block, jnp.int32(col_blocks)), lax.rem(block, jnp.int32(col_blocks))


def gather_blocks(send, panels, message):
    peers = message.shape[0]
    _, col_blocks, _, block_len = panels[0].shape

    def one(d, carry):
        for c in range(CAP):
            row, col = place_of(send, d * CAP + c, col_blocks)
            for f, field in enumerate(panels):
                for e in range(3):
                    message[d, f * CAP + c : f * CAP + c + 1, e * block_len : (e + 1) * block_len] = (
                        field[e, col, pl.ds(row, 1), :]
                    )
        return carry

    lax.fori_loop(0, peers, one, 0, unroll=4)


def scatter_blocks(send, message, panels):
    peers = message.shape[0]
    _, col_blocks, _, block_len = panels[0].shape
    for field in panels:
        field[...] = jnp.zeros_like(field)

    def one(d, carry):
        for c in range(CAP):
            row, col = place_of(send, d * CAP + c, col_blocks)
            for f, field in enumerate(panels):
                for e in range(3):
                    field[e, col, pl.ds(row, 1), :] = message[
                        d, f * CAP + c : f * CAP + c + 1, e * block_len : (e + 1) * block_len
                    ]
        return carry

    lax.fori_loop(0, peers, one, 0, unroll=4)


def to_panels(panels, e, value):
    _, col_blocks, _, block_len = panels.shape
    for q in range(col_blocks):
        panels[e, q] = value[:, q * block_len : (q + 1) * block_len]


def from_panels(panels, e):
    return jnp.concatenate([panels[e, q] for q in range(panels.shape[1])], axis=1)


def put_line(message, row, line):
    for d in range(message.shape[0]):
        message[d, row : row + 1, :] = line


def inner_apply(v, mass, kx, ky):
    rows, cols = v.shape
    row_ids = iota((rows, cols), 0)
    flux_x = jnp.where(row_ids == rows - 1, 0.0, kx * (v - pltpu.roll(v, rows - 1, 0)))
    flux_y = ky * (v - pltpu.roll(v, cols - 1, 1))
    return mass * v + (flux_x - pltpu.roll(flux_x, 1, 0)) + (flux_y - pltpu.roll(flux_y, 1, 1))


def masked_ky(stiff):
    ky = stiff[1]
    return jnp.where(iota(ky.shape, 1) == ky.shape[1] - 1, 0.0, ky)


def edge_coefs(stiff, low, high):
    rows = stiff.shape[1]
    last = jnp.where(high[3:4, :] > 0.5, stiff[0, rows - 1 : rows, :], 0.0)
    return low[3:4, :], last


def start_kernel(send, b, mass, stiff, low, high, message, db, b_panels, db_panels):
    rows = b.shape[1]
    kx_low, kx_high = edge_coefs(stiff, low, high)
    ky = masked_ky(stiff)
    sq, dot = [], []
    for e in range(3):
        v = b[e]
        db[e] = inner_apply(v, mass[...], stiff[0], ky)
        first, last = b[e, 0:1, :], b[e, rows - 1 : rows, :]
        db[e, 0:1, :] = db[e, 0:1, :] + kx_low * (first - low[e : e + 1, :])
        db[e, rows - 1 : rows, :] = db[e, rows - 1 : rows, :] + kx_high * (last - high[e : e + 1, :])
        to_panels(b_panels, e, v)
        to_panels(db_panels, e, db[e])
        sq.append(v * v)
        dot.append(v * db[e])
    line = line_of([total(sq[0] + sq[1] + sq[2]), total(dot[0] + dot[1] + dot[2])], message.shape[2])
    gather_blocks(send, [b_panels, db_panels], message)
    put_line(message, SUMS_TWO, line)
    put_line(message, SUMS_TWO + 1, jnp.zeros_like(line))


def fetch_hessian(hessian, held, sems):
    chunks = sems.shape[0]
    size = hessian.shape[0] // chunks
    copies = [
        pltpu.make_async_copy(
            hessian.at[pl.ds(k * size, size)], held.at[pl.ds(k * size, size)], sems.at[k]
        )
        for k in range(chunks)
    ]
    for copy in copies:
        copy.start()
    return copies, size


def contact_products(pairs, live_count, x8, y8, held, copies, size):
    y8[...] = jnp.zeros_like(y8)
    for h in range(held.shape[0]):
        if copies is not None and h % size == 0:
            copies[h // size].wait()
        a, b = pairs[h, 0], pairs[h, 1]
        delta = x8[a] - x8[b]
        delta = jnp.where(h < live_count, delta, 0.0)
        coarse = delta.astype(jnp.bfloat16).astype(F32)
        both = jnp.concatenate([coarse, delta - coarse], axis=0).astype(jnp.bfloat16)
        product = jnp.dot(both, held[h], preferred_element_type=F32)
        y = product[0:8] + product[8:16]
        y8[a] = y8[a] + y
        y8[b] = y8[b] - y


def wide(row):
    return jnp.broadcast_to(row, (8, row.shape[1]))


def contact_dot(x8, y8):
    value = x8[0] * y8[0]
    for p in range(1, x8.shape[0]):
        value = value + x8[p] * y8[p]
    return total(value[0:1])


def owner_kernel(pairs, live, got, hessian, message, x8, y8, z8, held, sems):
    copies, size = fetch_hessian(hessian, held, sems)
    peers, _, width = got.shape
    for d in range(peers):
        for c in range(CAP):
            x8[d * CAP + c] = wide(got[d, c : c + 1, :])
    contact_products(pairs, live[0], x8, y8, held, copies, size)
    line = line_of([contact_dot(x8, y8)], width)
    for d in range(peers):
        for c in range(CAP):
            p = d * CAP + c
            x8[p] = wide(got[d, CAP + c : CAP + c + 1, :]) + y8[p]
    contact_products(pairs, live[0], x8, z8, held, None, size)
    sub = iota((8, width), 0)
    for d in range(peers):
        tile = jnp.where(sub == SUMS_TWO, wide(line), 0.0)
        for c in range(CAP):
            tile = jnp.where(sub == c, y8[d * CAP + c], tile)
            tile = jnp.where(sub == CAP + c, z8[d * CAP + c], tile)
        message[d] = tile


def spread_kernel(send, got1, got2, db, mass, stiff, v1, dv1, v2, up, down, known, cb, cv1):
    rows = db.shape[1]
    scatter_blocks(send, got2, [cb, cv1])
    ky = masked_ky(stiff)
    for e in range(3):
        v = db[e] + from_panels(cb, e)
        v1[e] = v
        image = inner_apply(v, mass[...], stiff[0], ky)
        dv1[e] = image
        v2[e] = image + from_panels(cv1, e)
        up[e : e + 1, :] = v1[e, rows - 1 : rows, :]
        up[3 + e : 4 + e, :] = v2[e, rows - 1 : rows, :]
        down[e : e + 1, :] = v1[e, 0:1, :]
        down[3 + e : 4 + e, :] = v2[e, 0:1, :]
    sums1, sums2 = line_sum(got1, SUMS_TWO), line_sum(got2, SUMS_TWO)
    rr0 = pick(sums1, 0)
    alpha0 = rr0 / (pick(sums1, 1) + pick(sums2, 0))
    known[...] = line_of([rr0, alpha0], 128)


def edge_kernel(send, b, v1, dv1, v2, stiff, low, high, low1, high1, known, message, v2_out, full, panels):
    rows = b.shape[1]
    alpha0 = pick(known[...], 1)
    kx_low, kx_high = edge_coefs(stiff, low, high)
    sums = None
    for e in range(3):
        first = kx_low * (v1[e, 0:1, :] - low1[e : e + 1, :])
        last = kx_high * (v1[e, rows - 1 : rows, :] - high1[e : e + 1, :])
        full[e] = dv1[e]
        full[e, 0:1, :] = full[e, 0:1, :] + first
        full[e, rows - 1 : rows, :] = full[e, rows - 1 : rows, :] + last
        to_panels(panels, e, full[e])
        v2_out[e] = v2[e]
        v2_out[e, 0:1, :] = v2_out[e, 0:1, :] + first
        v2_out[e, rows - 1 : rows, :] = v2_out[e, rows - 1 : rows, :] + last
        right, image = b[e], v1[e]
        r1 = right - alpha0 * image
        w = image - alpha0 * v2_out[e]
        terms = [r1 * r1, r1 * w, r1 * image, right * w, right * image, w * w, w * image, image * image]
        sums = terms if sums is None else [s + t for s, t in zip(sums, terms)]
    line = line_of([total(s) for s in sums], message.shape[2])
    gather_blocks(send, [panels], message)
    put_line(message, SUMS_ONE, line)


def coefficients(known, sums):
    rr0, alpha0 = pick(known, 0), pick(known, 1)
    rr1, r1w, r1v1, bw, bv1, ww, wv1, v1v1 = [pick(sums, k) for k in range(8)]
    beta0 = rr1 / rr0
    alpha1 = rr1 / (r1w + beta0 * (r1v1 + bw) + beta0 * beta0 * bv1)
    image_sq = ww + 2.0 * beta0 * wv1 + beta0 * beta0 * v1v1
    rr2 = rr1 - 2.0 * alpha1 * (r1w + beta0 * r1v1) + alpha1 * alpha1 * image_sq
    return alpha0, beta0, alpha1, rr2 / rr1


def advance(b, v1, v2, coefs):
    alpha0, beta0, alpha1, beta1 = coefs
    r1 = b - alpha0 * v1
    d1 = r1 + beta0 * b
    r2 = r1 - alpha1 * (v1 - alpha0 * v2 + beta0 * v1)
    return d1, r2, r2 + beta1 * d1


def last_kernel(
    pairs, live, got1, sent2, got3, known, b, v1, v2, mass, stiff, low, high, low1, high1, hessian,
    message, part, r2_out, d2_out, dd2, x8, y8, held, sems,
):
    copies, size = fetch_hessian(hessian, held, sems)
    peers, _, width = got1.shape
    rows = b.shape[1]
    coefs = coefficients(known[...], line_sum(got3, SUMS_ONE))
    for d in range(peers):
        b_o = got1[d, 0:CAP, :]
        v1_o = got1[d, CAP : 2 * CAP, :] + sent2[d, 0:CAP, :]
        v2_o = got3[d, 0:CAP, :] + sent2[d, CAP : 2 * CAP, :]
        d2_o = advance(b_o, v1_o, v2_o, coefs)[2]
        for c in range(CAP):
            x8[d * CAP + c] = wide(d2_o[c : c + 1, :])

    kx_low, kx_high = edge_coefs(stiff, low, high)
    ky = masked_ky(stiff)
    sq = dot = None
    for e in range(3):
        d1, r2, d2 = advance(b[e], v1[e], v2[e], coefs)
        part[e] = coefs[0] * b[e] + coefs[2] * d1
        r2_out[e] = r2
        d2_out[e] = d2
        v1_low, v1_high = low1[e : e + 1, :], high1[e : e + 1, :]
        v2_low = low1[3 + e : 4 + e, :] + kx_low * (v1_low - v1[e, 0:1, :])
        v2_high = high1[3 + e : 4 + e, :] + kx_high * (v1_high - v1[e, rows - 1 : rows, :])
        d2_low = advance(low[e : e + 1, :], v1_low, v2_low, coefs)[2]
        d2_high = advance(high[e : e + 1, :], v1_high, v2_high, coefs)[2]
        dd2[e] = inner_apply(d2, mass[...], stiff[0], ky)
        dd2[e, 0:1, :] = dd2[e, 0:1, :] + kx_low * (d2_out[e, 0:1, :] - d2_low)
        dd2[e, rows - 1 : rows, :] = dd2[e, rows - 1 : rows, :] + kx_high * (
            d2_out[e, rows - 1 : rows, :] - d2_high
        )
        sq = r2 * r2 if sq is None else sq + r2 * r2
        dot = d2 * dd2[e] if dot is None else dot + d2 * dd2[e]
    rr2, dad2 = total(sq), total(dot)

    contact_products(pairs, live[0], x8, y8, held, copies, size)
    line = line_of([rr2, dad2 + contact_dot(x8, y8)], width)
    for d in range(peers):
        for c in range(CAP):
            message[d, c : c + 1, :] = y8[d * CAP + c, 0:1, :]
    put_line(message, SUMS_ONE, line)


def finish_kernel(send, got4, part, r2, d2, dd2, solution, residual, cd2):
    scatter_blocks(send, got4, [cd2])
    sums = line_sum(got4, SUMS_ONE)
    alpha2 = pick(sums, 0) / pick(sums, 1)
    for e in range(3):
        solution[e] = part[e] + alpha2 * d2[e]
        residual[e] = r2[e] - alpha2 * (dd2[e] + from_panels(cd2, e))


def call(kernel, spaces, outs, scratch=(), name=None):
    kinds = {"s": pltpu.SMEM, "v": pltpu.VMEM, "a": pl.ANY}
    return pl.pallas_call(
        kernel,
        out_shape=tuple(jax.ShapeDtypeStruct(shape, F32) for shape in outs),
        in_specs=[pl.BlockSpec(memory_space=kinds[k]) for k in spaces],
        out_specs=tuple(pl.BlockSpec(memory_space=pltpu.VMEM) for _ in outs),
        scratch_shapes=list(scratch),
        compiler_params=pltpu.CompilerParams(vmem_limit_bytes=VMEM_LIMIT),
        name=name,
    )


def per_device(right_side, masses, stiffness, hessian, send_list, pair_refs, counts):
    _, row_count, col_count = right_side.shape
    slot_count, width, _ = hessian.shape
    peers = lax.axis_size("gx")
    assert send_list.shape[1] == peers * CAP
    positions = peers * CAP
    field = right_side.shape
    two, one, edge = (peers, 8, width), (peers, 4, width), (6, col_count)
    chunks = next(k for k in (9, 6, 4, 3, 2, 1) if slot_count % k == 0)
    panels = pltpu.VMEM((3, col_count * 3 // width, row_count, width // 3), F32)
    tiles = pltpu.VMEM((positions, 8, width), F32)
    stored = [pltpu.VMEM(hessian.shape, hessian.dtype), pltpu.SemaphoreType.DMA((chunks,))]

    up = [(i, i + 1) for i in range(peers - 1)]
    down = [(i + 1, i) for i in range(peers - 1)]

    def swap(message):
        return lax.all_to_all(message, "gx", split_axis=0, concat_axis=0, tiled=True)

    low = lax.ppermute(jnp.concatenate([right_side[:, -1], stiffness[0, -1:]], axis=0), "gx", up)
    high = lax.ppermute(
        jnp.concatenate([right_side[:, 0], jnp.ones((1, col_count), F32)], axis=0), "gx", down
    )
    sent1, db = call(start_kernel, "svvvvv", [two, field], [panels, panels], name="start")(
        send_list, right_side, masses, stiffness, low, high
    )
    got1 = swap(sent1)
    (sent2,) = call(owner_kernel, "ssva", [two], [tiles, tiles, tiles, *stored], name="owner")(
        pair_refs, counts, got1, hessian
    )
    got2 = swap(sent2)
    v1, dv1, v2, up1, down1, known = call(
        spread_kernel,
        "svvvvv",
        [field, field, field, edge, edge, (1, 128)],
        [panels, panels],
        name="spread",
    )(send_list, got1, got2, db, masses, stiffness)
    low1 = lax.ppermute(up1, "gx", up)
    high1 = lax.ppermute(down1, "gx", down)
    sent3, v2 = call(
        edge_kernel, "svvvvvvvvvv", [one, field], [pltpu.VMEM(field, F32), panels], name="edge"
    )(send_list, right_side, v1, dv1, v2, stiffness, low, high, low1, high1, known)
    got3 = swap(sent3)
    sent4, part, r2, d2, dd2 = call(
        last_kernel, "ssvvvvvvvvvvvvva", [one] + [field] * 4, [tiles, tiles, *stored], name="last"
    )(
        pair_refs, counts, got1, sent2, got3, known, right_side, v1, v2, masses, stiffness,
        low, high, low1, high1, hessian,
    )
    got4 = swap(sent4)
    return call(
        finish_kernel, "svvvvv", [field, field], [panels], name="finish"
    )(send_list, got4, part, r2, d2, dd2)


def solution(mesh):
    placed = (
        P(None, ("groups", "gx"), None),
        P(("groups", "gx"), None),
        P(None, ("groups", "gx"), None),
        P(("groups", "gx"), None, None),
        P(("groups", "gx"), None),
        P(("groups", "gx"), None),
        P(("groups", "gx")),
    )
    return jax.shard_map(
        per_device,
        mesh=mesh,
        in_specs=placed,
        out_specs=(P(None, ("groups", "gx"), None), P(None, ("groups", "gx"), None)),
        check_vma=False,
    )
```

time: 298 us -> 102 us (0.34)
  blocking collectives: 151 us -> 35.7 us
  starting transfers between devices: 39 us -> 14.1 us
  waiting for transfers between devices: 36.2 us -> 13.2 us
  matrix products: 22.2 us -> 0 us
  Pallas kernels: 0 us -> 21 us
  other arithmetic: 17.5 us -> 0.01 us
  between operations: 8.63 us -> 1.44 us
  local copies, waits for them, and re-layouts: 21.5 us -> 16.1 us
    psum x5 -> x0, blocking collectives: 151 us -> none  [the longest x3 90.6 us: squares(): return lax.psum(jnp.sum(vector * vector), 'gx')]
    all_to_all x0 -> x3, blocking collectives: none -> 35.7 us  [swap(): lax.all_to_all(message, 'gx', split_axis=0, concat_axis=0, tiled=True)]
    all_to_all x6 -> x1, waiting for transfers between devices: 36.2 us -> 7.57 us  [swap(): lax.all_to_all(message, 'gx', split_axis=0, concat_axis=0, tiled=True)]
    dot_general x6 -> x0, matrix products: 22.2 us -> none  [the longest x3 21.4 us: owner_products(): jnp.einsum('hij,hkj->hki', hessian, stacked, preferred_element_type=jnp.f...]
    pallas_call x0 -> x6, Pallas kernels: none -> 21 us  [the longest x1 7.68 us: per_device(): call(owner_kernel, 'ssva', [two], [tiles, tiles, tiles, *stored], name='o...]
    all_to_all x6 -> x1, starting transfers between devices: 24.5 us -> 7.83 us  [swap(): lax.all_to_all(message, 'gx', split_axis=0, concat_axis=0, tiled=True)]
    unnamed x7 -> x37, local copies, waits for them, and re-layouts: 0.11 us -> 14.5 us
    reshape x18 -> x0, local copies, waits for them, and re-layouts: 8.25 us -> none  [the longest x3 3.95 us: from_blocks(): return shaped.transpose(2, 0, 1, 3).reshape(3, row_count, col_count)]
  transfers between devices with their start and end apart: 13 -> 5, of which waited for: 6 -> 3; matrix products, arithmetic and copies ran while one was open for 4% -> 1% of each run, Pallas kernels for 0% -> 0%
where the time goes in v2:
time: 102 us
  blocking collectives  35.7 us (35%)
  Pallas kernels  21 us (21%)
  local copies, waits for them, and re-layouts  16.1 us (16%)
  starting transfers between devices  14.1 us (14%)
  waiting for transfers between devices  13.2 us (13%)
  between operations  1.44 us (1%)
    all_to_all x3, blocking collectives, swap(): lax.all_to_all(message, 'gx', split_axis=0, concat_axis=0, tiled=True)  35.7 us
    unnamed x37, local copies, waits for them, and re-layouts  14.5 us
    all_to_all x1, starting transfers between devices, swap(): lax.all_to_all(message, 'gx', split_axis=0, concat_axis=0, tiled=True)  7.83 us
    pallas_call x1, Pallas kernels, per_device(): call(owner_kernel, 'ssva', [two], [tiles, tiles, tiles, *stored], name='o...  7.68 us
    all_to_all x1, waiting for transfers between devices, swap(): lax.all_to_all(message, 'gx', split_axis=0, concat_axis=0, tiled=True)  7.57 us
    pallas_call x1, Pallas kernels, per_device(): call(last_kernel, 'ssvvvvvvvvvvvvva', [one] + [field] * 4, [tiles, tiles,...  6.96 us
    ppermute x1, waiting for transfers between devices, per_device(): lax.ppermute(jnp.concatenate([right_side[:, 0], jnp.ones((1, col_count),...  3.89 us
    ppermute x1, starting transfers between devices, per_device(): lax.ppermute(jnp.concatenate([right_side[:, -1], stiffness[0, -1:]], axis...  2.36 us
  transfers between devices with their start and end apart: 5, of which 3 were waited for; matrix products, arithmetic and copies ran while one was open for 1% of the time, Pallas kernels for 0%

profile of v2, /device:TPU:0, one launch (start us, length us, event | category | flops | bytes accessed | tf_op | source)
XLA Modules:
  0.0 101.5 jit_solution(3106522226745276813)
XLA Ops:
  0.6 0.7 slice_bitcast_fusion
  1.4 0.8 fusion
  2.2 2.4 %collective-permute-start = (f32[4,512]{1,0:T(4,128)S(1)}, f32[4,512]{1,0:T(4,128)S(1)}, u32[]{:S(2)}, u32[]{:S(2)}) collective-permute-start(f32[4,512]{1,0:T(4,128)S(1)} %pad_maximum_fusion), channel_id=1, source_target_pairs={{0,1},{1,2},{2,3},{3,4},{4,5},{5,6},{6,7},{7,8},{8,9},{9,10},{10,1... | collective-permute-start | bytes 24584 | tf_op jit(solution)/shard_map/ppermute | solution.py:355
  4.6 1.3 %collective-permute-start.1 = (f32[4,512]{1,0:T(4,128)S(1)}, f32[4,512]{1,0:T(4,128)S(1)}, u32[]{:S(2)}, u32[]{:S(2)}) collective-permute-start(f32[4,512]{1,0:T(4,128)S(1)} %concatenate.7), channel_id=1, source_target_pairs={{1,0},{2,1},{3,2},{4,3},{5,4},{6,5},{7,6},{8,7},{9,8},{10,9},{11,1... | collective-permute-start | bytes 24584 | tf_op jit(solution)/shard_map/ppermute | solution.py:356
  5.9 3.9 %collective-permute-done.1.high = f32[4,512]{1,0:T(4,128)S(1)} collective-permute-done((f32[4,512]{1,0:T(4,128)S(1)}, f32[4,512]{1,0:T(4,128)S(1)}, u32[]{:S(2)}, u32[]{:S(2)}) %collective-permute-start.1) | collective-permute-done | bytes 8224 | tf_op jit(solution)/shard_map/ppermute | solution.py:356
  9.8 0.9 copy-done.2
  10.8 1.0 copy-done.4
  11.8 0.9 copy-done.11
  12.7 0.7 copy-done.15
  13.3 2.0 %start.1 = (f32[16,8,384]{2,1,0:T(8,128)}, f32[3,64,512]{2,1,0:T(8,128)S(1)}) custom-call(s32[1,48]{1,0:T(1,128)S(1)} %copy-done.15, f32[3,64,512]{2,1,0:T(8,128)S(1)} %copy-done.4, f32[64,512]{1,0:T(8,128)S(1)} %copy-done.11, f32[2,64,512]{2,1,0:T(8,128)S(1)} %copy-done.2, f32[4,512]{1,0:T(4,128)S(1)} %collective-permute-done.low, ...), custom_call_target="tpu_custom_call" | custom-call | tf_op jit(solution)/shard_map/start/pallas_call | solution.py:359
  15.3 0.7 copy-done.13
  16.1 7.8 %all-to-all-start = ((f32[16,8,384]{2,1,0:T(8,128)}), f32[16,8,384]{2,1,0:T(8,128)S(1)}, u32[]{:S(2)}, u32[]{:S(2)}) async-start(f32[16,8,384]{2,1,0:T(8,128)} %get-tuple-element.17), calls=%async_computation | async-start | bytes 393216 | tf_op jit(solution)/shard_map/all_to_all | solution.py:353
  24.6 0.8 copy.12.pairs
  25.3 7.6 %all-to-all-done.got.got1 = f32[16,8,384]{2,1,0:T(8,128)S(1)} async-done(((f32[16,8,384]{2,1,0:T(8,128)}), f32[16,8,384]{2,1,0:T(8,128)S(1)}, u32[]{:S(2)}, u32[]{:S(2)}) %all-to-all-start) | async-done | bytes 196640 | tf_op jit(solution)/shard_map/all_to_all | solution.py:353
  32.9 0.7 copy-done.7
  33.6 4.0 %copy-done = bf16[36,384,384]{2,1,0:T(8,128)(2,1)S(1)} copy-done((bf16[36,384,384]{2,1,0:T(8,128)(2,1)S(1)}, bf16[36,384,384]{2,1,0:T(8,128)(2,1)}, u32[]{:S(2)}) %copy-start) | copy-done | bytes 10616856
  37.6 0.9 copy-done.8
  38.5 7.7 %owner.1.sent2 = f32[16,8,384]{2,1,0:T(8,128)S(1)} custom-call(s32[36,2]{1,0:T(8,128)S(1)} %copy.12.pairs, s32[1]{0:T(128)S(6)} %copy.19.live, f32[16,8,384]{2,1,0:T(8,128)S(1)} %copy-done.8, bf16[36,384,384]{2,1,0:T(8,128)(2,1)S(1)} %copy-done), custom_call_target="tpu_custom_call" | custom-call | tf_op jit(solution)/shard_map/owner/pallas_call | solution.py:363
  46.2 11.6 %all_to_all.20.got2 = f32[16,8,384]{2,1,0:T(8,128)S(1)} all-to-all(f32[16,8,384]{2,1,0:T(8,128)S(1)} %owner.1.sent2), channel_id=1, replica_groups=mesh['groups'=2,'gx'=16] {'gx'}, dimensions={0} | all-to-all | bytes 393216 | tf_op jit(solution)/shard_map/all_to_all | solution.py:353
  57.8 0.9 copy-done.9
  58.8 1.0 copy-done.14
  59.8 1.3 %spread.1 = (f32[3,64,512]{2,1,0:T(8,128)S(1)}, f32[3,64,512]{2,1,0:T(8,128)S(1)}, f32[3,64,512]{2,1,0:T(8,128)S(1)}, f32[6,512]{1,0:T(8,128)S(1)}, f32[6,512]{1,0:T(8,128)S(1)}, /*index=5*/f32[1,128]{1,0:T(1,128)S(1)}) custom-call(s32[1,48]{1,0:T(1,128)S(1)} %copy-done.16, f32[16,8,384]{2,1,0:T(8,128)S(1)} %copy-done.9, f32[16,8,384]{2,1,0:T(8,128)S(1)} %all_to_all.20.got2, ...), custom_call_target="tpu_custom_call" | custom-call | tf_op jit(solution)/shard_map/spread/pallas_call | solution.py:367
  61.0 1.3 %collective-permute-start.2 = (f32[6,512]{1,0:T(8,128)S(1)}, f32[6,512]{1,0:T(8,128)S(1)}, u32[]{:S(2)}, u32[]{:S(2)}) collective-permute-start(f32[6,512]{1,0:T(8,128)S(1)} %get-tuple-element.22), channel_id=1, source_target_pairs={{0,1},{1,2},{2,3},{3,4},{4,5},{5,6},{6,7},{7,8},{8,9},{9,10},{10,1... | collective-permute-start | bytes 36872 | tf_op jit(solution)/shard_map/ppermute | solution.py:374
  62.3 1.3 %collective-permute-start.3 = (f32[6,512]{1,0:T(8,128)S(1)}, f32[6,512]{1,0:T(8,128)S(1)}, u32[]{:S(2)}, u32[]{:S(2)}) collective-permute-start(f32[6,512]{1,0:T(8,128)S(1)} %get-tuple-element.23), channel_id=1, source_target_pairs={{1,0},{2,1},{3,2},{4,3},{5,4},{6,5},{7,6},{8,7},{9,8},{10,9},{11,1... | collective-permute-start | bytes 36872 | tf_op jit(solution)/shard_map/ppermute | solution.py:375
  63.6 1.8 %collective-permute-done.3.high1 = f32[6,512]{1,0:T(8,128)S(1)} collective-permute-done((f32[6,512]{1,0:T(8,128)S(1)}, f32[6,512]{1,0:T(8,128)S(1)}, u32[]{:S(2)}, u32[]{:S(2)}) %collective-permute-start.3) | collective-permute-done | bytes 12320 | tf_op jit(solution)/shard_map/ppermute | solution.py:375
  65.4 1.3 %edge.1 = (f32[16,4,384]{2,1,0:T(4,128)S(1)}, f32[3,64,512]{2,1,0:T(8,128)S(1)}) custom-call(s32[1,48]{1,0:T(1,128)S(1)} %copy-done.16, f32[3,64,512]{2,1,0:T(8,128)S(1)} %copy-done.5, f32[3,64,512]{2,1,0:T(8,128)S(1)} %get-tuple-element.19.v1, f32[3,64,512]{2,1,0:T(8,128)S(1)} %get-tuple-element.20.dv1, f32[3,64,512]{2,1,0:T(8,128)S(1)} %get-tuple-element.21.v2, ...), custom_call_target="tpu_custom_call" | custom-call | tf_op jit(solution)/shard_map/edge/pallas_call | solution.py:376
  66.7 14.1 %all_to_all.21.got3 = f32[16,4,384]{2,1,0:T(4,128)S(1)} all-to-all(f32[16,4,384]{2,1,0:T(4,128)S(1)} %get-tuple-element.25), channel_id=1, replica_groups=mesh['groups'=2,'gx'=16] {'gx'}, dimensions={0} | all-to-all | bytes 196608 | tf_op jit(solution)/shard_map/all_to_all | solution.py:353
  80.8 1.0 copy-done.6
  81.8 0.9 copy-done.10
  82.7 7.0 %last.1 = (f32[16,4,384]{2,1,0:T(4,128)S(1)}, f32[3,64,512]{2,1,0:T(8,128)S(1)}, f32[3,64,512]{2,1,0:T(8,128)S(1)}, f32[3,64,512]{2,1,0:T(8,128)S(1)}, f32[3,64,512]{2,1,0:T(8,128)S(1)}) custom-call(s32[36,2]{1,0:T(8,128)S(1)} %copy.12.pairs, s32[1]{0:T(128)S(6)} %copy.19.live, f32[16,8,384]{2,1,0:T(8,128)S(1)} %copy-done.10, f32[16,8,384]{2,1,0:T(8,128)S(1)} %owner.1.sent2, ...), custom_call_target="tpu_custom_call" | custom-call | tf_op jit(solution)/shard_map/last/pallas_call | solution.py:380
  89.7 10.0 %all_to_all.22.got4 = f32[16,4,384]{2,1,0:T(4,128)S(1)} all-to-all(f32[16,4,384]{2,1,0:T(4,128)S(1)} %get-tuple-element.27), channel_id=1, replica_groups=mesh['groups'=2,'gx'=16] {'gx'}, dimensions={0} | all-to-all | bytes 196608 | tf_op jit(solution)/shard_map/all_to_all | solution.py:353
  99.7 1.8 %finish.1 = (f32[3,64,512]{2,1,0:T(8,128)}, f32[3,64,512]{2,1,0:T(8,128)}) custom-call(s32[1,48]{1,0:T(1,128)S(1)} %copy-done.16, f32[16,4,384]{2,1,0:T(4,128)S(1)} %all_to_all.22.got4, f32[3,64,512]{2,1,0:T(8,128)S(1)} %get-tuple-element.28.part, f32[3,64,512]{2,1,0:T(8,128)S(1)} %get-tuple-element.29.r2, f32[3,64,512]{2,1,0:T(8,128)S(1)} %get-tuple-element.30.d2, ...), custom_call_target="tpu_custom_call" | custom-call | tf_op jit(solution)/shard_map/finish/pallas_call | solution.py:387
  (28 shorter events, 0.1 us)
Async XLA Ops:
  0.6 57.2 %copy-start.16 = (s32[1,48]{1,0:T(1,128)S(1)}, s32[1,48]{1,0:T(1,128)}, u32[]{:S(2)}) copy-start(s32[1,48]{1,0:T(1,128)} %send.7) | copy-start | bytes 580
  2.2 3.7 %collective-permute-start = (f32[4,512]{1,0:T(4,128)S(1)}, f32[4,512]{1,0:T(4,128)S(1)}, u32[]{:S(2)}, u32[]{:S(2)}) collective-permute-start(f32[4,512]{1,0:T(4,128)S(1)} %pad_maximum_fusion), channel_id=1, source_target_pairs={{0,1},{1,2},{2,3},{3,4},{4,5},{5,6},{6,7},{7,8},{8,9},{9,10},{10,1... | collective-permute-start | bytes 24584 | tf_op jit(solution)/shard_map/ppermute | solution.py:355
  4.6 5.2 %collective-permute-start.1 = (f32[4,512]{1,0:T(4,128)S(1)}, f32[4,512]{1,0:T(4,128)S(1)}, u32[]{:S(2)}, u32[]{:S(2)}) collective-permute-start(f32[4,512]{1,0:T(4,128)S(1)} %concatenate.7), channel_id=1, source_target_pairs={{1,0},{2,1},{3,2},{4,3},{5,4},{6,5},{7,6},{8,7},{9,8},{10,9},{11,1... | collective-permute-start | bytes 24584 | tf_op jit(solution)/shard_map/ppermute | solution.py:356
  9.8 1.0 copy-start.2
  10.8 1.0 copy-start.4
  11.8 0.9 copy-start.11
  12.7 0.7 copy-start.15
  15.3 0.7 copy-start.13
  16.1 16.8 %all-to-all-start = ((f32[16,8,384]{2,1,0:T(8,128)}), f32[16,8,384]{2,1,0:T(8,128)S(1)}, u32[]{:S(2)}, u32[]{:S(2)}) async-start(f32[16,8,384]{2,1,0:T(8,128)} %get-tuple-element.17), calls=%async_computation | async-start | bytes 393216 | tf_op jit(solution)/shard_map/all_to_all | solution.py:353
  32.9 0.7 copy-start.7
  33.6 4.0 %copy-start = (bf16[36,384,384]{2,1,0:T(8,128)(2,1)S(1)}, bf16[36,384,384]{2,1,0:T(8,128)(2,1)}, u32[]{:S(2)}) copy-start(bf16[36,384,384]{2,1,0:T(8,128)(2,1)} %hessian.3) | copy-start | bytes 31850500
  37.6 0.9 copy-start.8
  38.5 19.3 %copy-start.3 = (f32[2,64,512]{2,1,0:T(8,128)S(1)}, f32[2,64,512]{2,1,0:T(8,128)}, u32[]{:S(2)}) copy-start(f32[2,64,512]{2,1,0:T(8,128)} %stiff.7) | copy-start | bytes 786436
  38.5 19.3 %copy-start.12 = (f32[64,512]{1,0:T(8,128)S(1)}, f32[64,512]{1,0:T(8,128)}, u32[]{:S(2)}) copy-start(f32[64,512]{1,0:T(8,128)} %mass.5) | copy-start | bytes 393220
  38.5 26.9 %copy-start.5 = (f32[3,64,512]{2,1,0:T(8,128)S(1)}, f32[3,64,512]{2,1,0:T(8,128)}, u32[]{:S(2)}) copy-start(f32[3,64,512]{2,1,0:T(8,128)} %b.5) | copy-start | bytes 1179652
  38.5 42.3 %copy-start.1 = (bf16[36,384,384]{2,1,0:T(8,128)(2,1)S(1)}, bf16[36,384,384]{2,1,0:T(8,128)(2,1)}, u32[]{:S(2)}) copy-start(bf16[36,384,384]{2,1,0:T(8,128)(2,1)} %hessian.3) | copy-start | bytes 31850500
  57.8 0.9 copy-start.9
  58.8 1.0 copy-start.14
  61.0 2.6 %collective-permute-start.2 = (f32[6,512]{1,0:T(8,128)S(1)}, f32[6,512]{1,0:T(8,128)S(1)}, u32[]{:S(2)}, u32[]{:S(2)}) collective-permute-start(f32[6,512]{1,0:T(8,128)S(1)} %get-tuple-element.22), channel_id=1, source_target_pairs={{0,1},{1,2},{2,3},{3,4},{4,5},{5,6},{6,7},{7,8},{8,9},{9,10},{10,1... | collective-permute-start | bytes 36872 | tf_op jit(solution)/shard_map/ppermute | solution.py:374
  62.3 3.1 %collective-permute-start.3 = (f32[6,512]{1,0:T(8,128)S(1)}, f32[6,512]{1,0:T(8,128)S(1)}, u32[]{:S(2)}, u32[]{:S(2)}) collective-permute-start(f32[6,512]{1,0:T(8,128)S(1)} %get-tuple-element.23), channel_id=1, source_target_pairs={{1,0},{2,1},{3,2},{4,3},{5,4},{6,5},{7,6},{8,7},{9,8},{10,9},{11,1... | collective-permute-start | bytes 36872 | tf_op jit(solution)/shard_map/ppermute | solution.py:375
  80.8 1.0 copy-start.6
  81.8 0.9 copy-start.10

commit v3 on v2

--- a/solution.py
+++ b/solution.py
@@ -8,7 +8,6 @@
 from jax.sharding import PartitionSpec as P
 
 F32 = jnp.float32
-VMEM_LIMIT = 40 * 1024 * 1024
 CAP = 3
 SUMS_TWO, SUMS_ONE = 2 * CAP, CAP
 
@@ -139,25 +138,9 @@
     put_line(message, SUMS_TWO + 1, jnp.zeros_like(line))
 
 
-def fetch_hessian(hessian, held, sems):
-    chunks = sems.shape[0]
-    size = hessian.shape[0] // chunks
-    copies = [
-        pltpu.make_async_copy(
-            hessian.at[pl.ds(k * size, size)], held.at[pl.ds(k * size, size)], sems.at[k]
-        )
-        for k in range(chunks)
-    ]
-    for copy in copies:
-        copy.start()
-    return copies, size
-
-
-def contact_products(pairs, live_count, x8, y8, held, copies, size):
+def contact_products(pairs, live_count, x8, y8, held):
     y8[...] = jnp.zeros_like(y8)
     for h in range(held.shape[0]):
-        if copies is not None and h % size == 0:
-            copies[h // size].wait()
         a, b = pairs[h, 0], pairs[h, 1]
         delta = x8[a] - x8[b]
         delta = jnp.where(h < live_count, delta, 0.0)
@@ -180,19 +163,18 @@
     return total(value[0:1])
 
 
-def owner_kernel(pairs, live, got, hessian, message, x8, y8, z8, held, sems):
-    copies, size = fetch_hessian(hessian, held, sems)
+def owner_kernel(pairs, live, got, hessian, message, x8, y8, z8):
     peers, _, width = got.shape
     for d in range(peers):
         for c in range(CAP):
             x8[d * CAP + c] = wide(got[d, c : c + 1, :])
-    contact_products(pairs, live[0], x8, y8, held, copies, size)
+    contact_products(pairs, live[0], x8, y8, hessian)
     line = line_of([contact_dot(x8, y8)], width)
     for d in range(peers):
         for c in range(CAP):
             p = d * CAP + c
             x8[p] = wide(got[d, CAP + c : CAP + c + 1, :]) + y8[p]
-    contact_products(pairs, live[0], x8, z8, held, None, size)
+    contact_products(pairs, live[0], x8, z8, hessian)
     sub = iota((8, width), 0)
     for d in range(peers):
         tile = jnp.where(sub == SUMS_TWO, wide(line), 0.0)
@@ -267,9 +249,8 @@
 
 def last_kernel(
     pairs, live, got1, sent2, got3, known, b, v1, v2, mass, stiff, low, high, low1, high1, hessian,
-    message, part, r2_out, d2_out, dd2, x8, y8, held, sems,
+    message, part, r2_out, d2_out, dd2, x8, y8,
 ):
-    copies, size = fetch_hessian(hessian, held, sems)
     peers, _, width = got1.shape
     rows = b.shape[1]
     coefs = coefficients(known[...], line_sum(got3, SUMS_ONE))
@@ -303,7 +284,7 @@
         dot = d2 * dd2[e] if dot is None else dot + d2 * dd2[e]
     rr2, dad2 = total(sq), total(dot)
 
-    contact_products(pairs, live[0], x8, y8, held, copies, size)
+    contact_products(pairs, live[0], x8, y8, hessian)
     line = line_of([rr2, dad2 + contact_dot(x8, y8)], width)
     for d in range(peers):
         for c in range(CAP):
@@ -320,31 +301,29 @@
         residual[e] = r2[e] - alpha2 * (dd2[e] + from_panels(cd2, e))
 
 
-def call(kernel, spaces, outs, scratch=(), name=None):
-    kinds = {"s": pltpu.SMEM, "v": pltpu.VMEM, "a": pl.ANY}
+def call(kernel, spaces, outs, scratch=(), mebibytes=12, name=None):
+    kinds = {"s": pltpu.SMEM, "v": pltpu.VMEM}
     return pl.pallas_call(
         kernel,
         out_shape=tuple(jax.ShapeDtypeStruct(shape, F32) for shape in outs),
         in_specs=[pl.BlockSpec(memory_space=kinds[k]) for k in spaces],
         out_specs=tuple(pl.BlockSpec(memory_space=pltpu.VMEM) for _ in outs),
         scratch_shapes=list(scratch),
-        compiler_params=pltpu.CompilerParams(vmem_limit_bytes=VMEM_LIMIT),
+        compiler_params=pltpu.CompilerParams(vmem_limit_bytes=mebibytes * 1024 * 1024),
         name=name,
     )
 
 
 def per_device(right_side, masses, stiffness, hessian, send_list, pair_refs, counts):
     _, row_count, col_count = right_side.shape
-    slot_count, width, _ = hessian.shape
+    width = hessian.shape[1]
     peers = lax.axis_size("gx")
     assert send_list.shape[1] == peers * CAP
     positions = peers * CAP
     field = right_side.shape
     two, one, edge = (peers, 8, width), (peers, 4, width), (6, col_count)
-    chunks = next(k for k in (9, 6, 4, 3, 2, 1) if slot_count % k == 0)
     panels = pltpu.VMEM((3, col_count * 3 // width, row_count, width // 3), F32)
     tiles = pltpu.VMEM((positions, 8, width), F32)
-    stored = [pltpu.VMEM(hessian.shape, hessian.dtype), pltpu.SemaphoreType.DMA((chunks,))]
 
     up = [(i, i + 1) for i in range(peers - 1)]
     down = [(i + 1, i) for i in range(peers - 1)]
@@ -360,7 +339,7 @@
         send_list, right_side, masses, stiffness, low, high
     )
     got1 = swap(sent1)
-    (sent2,) = call(owner_kernel, "ssva", [two], [tiles, tiles, tiles, *stored], name="owner")(
+    (sent2,) = call(owner_kernel, "ssvv", [two], [tiles] * 3, 24, name="owner")(
         pair_refs, counts, got1, hessian
     )
     got2 = swap(sent2)
@@ -378,7 +357,7 @@
     )(send_list, right_side, v1, dv1, v2, stiffness, low, high, low1, high1, known)
     got3 = swap(sent3)
     sent4, part, r2, d2, dd2 = call(
-        last_kernel, "ssvvvvvvvvvvvvva", [one] + [field] * 4, [tiles, tiles, *stored], name="last"
+        last_kernel, "ssvvvvvvvvvvvvvv", [one] + [field] * 4, [tiles] * 2, 24, name="last"
     )(
         pair_refs, counts, got1, sent2, got3, known, right_side, v1, v2, masses, stiffness,
         low, high, low1, high1, hessian,

time: 102 us -> 89.4 us (0.88)
  Pallas kernels: 21 us -> 14.4 us
  local copies, waits for them, and re-layouts: 16.1 us -> 9.89 us
    pallas_call x2, Pallas kernels: 14.6 us -> 8.09 us  [the longest x1 4.49 us: per_device(): call(owner_kernel, 'ssvv', [two], [tiles] * 3, 24, name='owner')]
    unnamed x37 -> x23, local copies, waits for them, and re-layouts: 14.5 us -> 8.32 us
where the time goes in v3:
time: 89.4 us; the launch traced here: 88.7 us
  blocking collectives  35.7 us (40%)
  Pallas kernels  14.4 us (16%)
  starting transfers between devices  14.1 us (16%)
  waiting for transfers between devices  13.2 us (15%)
  local copies, waits for them, and re-layouts  9.89 us (11%)
  between operations  1.41 us (2%)
    all_to_all x3, blocking collectives, swap(): lax.all_to_all(message, 'gx', split_axis=0, concat_axis=0, tiled=True)  35.7 us
    unnamed x23, local copies, waits for them, and re-layouts  8.32 us
    all_to_all x1, starting transfers between devices, swap(): lax.all_to_all(message, 'gx', split_axis=0, concat_axis=0, tiled=True)  7.83 us
    all_to_all x1, waiting for transfers between devices, swap(): lax.all_to_all(message, 'gx', split_axis=0, concat_axis=0, tiled=True)  7.57 us
    pallas_call x1, Pallas kernels, per_device(): call(owner_kernel, 'ssvv', [two], [tiles] * 3, 24, name='owner')  4.49 us
    ppermute x1, waiting for transfers between devices, per_device(): lax.ppermute(jnp.concatenate([right_side[:, 0], jnp.ones((1, col_count),...  3.89 us
    pallas_call x1, Pallas kernels, per_device(): call(last_kernel, 'ssvvvvvvvvvvvvvv', [one] + [field] * 4, [tiles] * 2, 2...  3.6 us
    ppermute x1, starting transfers between devices, per_device(): lax.ppermute(jnp.concatenate([right_side[:, -1], stiffness[0, -1:]], axis...  2.36 us
  transfers between devices with their start and end apart: 5, of which 3 were waited for; matrix products, arithmetic and copies ran while one was open for 1% of the time, Pallas kernels for 0%

profile of v3, /device:TPU:0, one launch (start us, length us, event | category | flops | bytes accessed | tf_op | source)
XLA Modules:
  0.0 88.7 jit_solution(9351885864963165382)
XLA Ops:
  0.6 0.0 copy-start.9
  0.6 0.7 slice_bitcast_fusion
  1.4 0.8 fusion
  2.2 2.4 %collective-permute-start = (f32[4,512]{1,0:T(4,128)S(1)}, f32[4,512]{1,0:T(4,128)S(1)}, u32[]{:S(2)}, u32[]{:S(2)}) collective-permute-start(f32[4,512]{1,0:T(4,128)S(1)} %pad_maximum_fusion), channel_id=1, source_target_pairs={{0,1},{1,2},{2,3},{3,4},{4,5},{5,6},{6,7},{7,8},{8,9},{9,10},{10,1... | collective-permute-start | bytes 24584 | tf_op jit(solution)/shard_map/ppermute | solution.py:334
  4.6 1.3 %collective-permute-start.1 = (f32[4,512]{1,0:T(4,128)S(1)}, f32[4,512]{1,0:T(4,128)S(1)}, u32[]{:S(2)}, u32[]{:S(2)}) collective-permute-start(f32[4,512]{1,0:T(4,128)S(1)} %concatenate.7), channel_id=1, source_target_pairs={{1,0},{2,1},{3,2},{4,3},{5,4},{6,5},{7,6},{8,7},{9,8},{10,9},{11,1... | collective-permute-start | bytes 24584 | tf_op jit(solution)/shard_map/ppermute | solution.py:335
  5.9 0.0 collective-permute-done.low
  5.9 3.9 %collective-permute-done.1.high = f32[4,512]{1,0:T(4,128)S(1)} collective-permute-done((f32[4,512]{1,0:T(4,128)S(1)}, f32[4,512]{1,0:T(4,128)S(1)}, u32[]{:S(2)}, u32[]{:S(2)}) %collective-permute-start.1) | collective-permute-done | bytes 8224 | tf_op jit(solution)/shard_map/ppermute | solution.py:335
  9.8 0.9 %copy-done.2 = f32[2,64,512]{2,1,0:T(8,128)S(1)} copy-done((f32[2,64,512]{2,1,0:T(8,128)S(1)}, f32[2,64,512]{2,1,0:T(8,128)}, u32[]{:S(2)}) %copy-start.2) | copy-done | bytes 262168
  10.8 1.0 %copy-done.4 = f32[3,64,512]{2,1,0:T(8,128)S(1)} copy-done((f32[3,64,512]{2,1,0:T(8,128)S(1)}, f32[3,64,512]{2,1,0:T(8,128)}, u32[]{:S(2)}) %copy-start.4) | copy-done | bytes 393240
  11.8 0.9 %copy-done.6 = f32[64,512]{1,0:T(8,128)S(1)} copy-done((f32[64,512]{1,0:T(8,128)S(1)}, f32[64,512]{1,0:T(8,128)}, u32[]{:S(2)}) %copy-start.6) | copy-done | bytes 131096
  12.7 0.7 copy-done.8
  13.3 2.0 %start.1 = (f32[16,8,384]{2,1,0:T(8,128)}, f32[3,64,512]{2,1,0:T(8,128)S(1)}) custom-call(s32[1,48]{1,0:T(1,128)S(1)} %copy-done.8, f32[3,64,512]{2,1,0:T(8,128)S(1)} %copy-done.4, f32[64,512]{1,0:T(8,128)S(1)} %copy-done.6, f32[2,64,512]{2,1,0:T(8,128)S(1)} %copy-done.2, f32[4,512]{1,0:T(4,128)S(1)} %collective-permute-done.low, ...), custom_call_target="tpu_custom_call" | custom-call | tf_op jit(solution)/shard_map/start/pallas_call | solution.py:338
  15.3 7.8 %all-to-all-start = ((f32[16,8,384]{2,1,0:T(8,128)}), f32[16,8,384]{2,1,0:T(8,128)S(1)}, u32[]{:S(2)}, u32[]{:S(2)}) async-start(f32[16,8,384]{2,1,0:T(8,128)} %get-tuple-element.17), calls=%async_computation | async-start | bytes 393216 | tf_op jit(solution)/shard_map/all_to_all | solution.py:332
  23.8 0.8 copy.12.pairs
  24.6 7.6 %all-to-all-done.got.got1 = f32[16,8,384]{2,1,0:T(8,128)S(1)} async-done(((f32[16,8,384]{2,1,0:T(8,128)}), f32[16,8,384]{2,1,0:T(8,128)S(1)}, u32[]{:S(2)}, u32[]{:S(2)}) %all-to-all-start) | async-done | bytes 196640 | tf_op jit(solution)/shard_map/all_to_all | solution.py:332
  32.1 4.0 %copy-done = bf16[36,384,384]{2,1,0:T(8,128)(2,1)S(1)} copy-done((bf16[36,384,384]{2,1,0:T(8,128)(2,1)S(1)}, bf16[36,384,384]{2,1,0:T(8,128)(2,1)}, u32[]{:S(2)}) %copy-start) | copy-done | bytes 10616856
  36.2 4.5 %owner.1.sent2 = f32[16,8,384]{2,1,0:T(8,128)S(1)} custom-call(s32[36,2]{1,0:T(8,128)S(1)} %copy.12.pairs, s32[1]{0:T(128)S(6)} %copy.19.live, f32[16,8,384]{2,1,0:T(8,128)S(1)} %all-to-all-done.got.got1, bf16[36,384,384]{2,1,0:T(8,128)(2,1)S(1)} %copy-done), custom_call_target="tpu_custom_call" | custom-call | tf_op jit(solution)/shard_map/owner/pallas_call | solution.py:342
  40.7 11.6 %all_to_all.20.got2 = f32[16,8,384]{2,1,0:T(8,128)S(1)} all-to-all(f32[16,8,384]{2,1,0:T(8,128)S(1)} %owner.1.sent2), channel_id=1, replica_groups=mesh['groups'=2,'gx'=16] {'gx'}, dimensions={0} | all-to-all | bytes 393216 | tf_op jit(solution)/shard_map/all_to_all | solution.py:332
  52.3 0.0 copy-done.9
  52.3 0.0 copy-done.3
  52.3 0.0 copy-done.7
  52.3 1.3 %spread.1 = (f32[3,64,512]{2,1,0:T(8,128)S(1)}, f32[3,64,512]{2,1,0:T(8,128)S(1)}, f32[3,64,512]{2,1,0:T(8,128)S(1)}, f32[6,512]{1,0:T(8,128)S(1)}, f32[6,512]{1,0:T(8,128)S(1)}, /*index=5*/f32[1,128]{1,0:T(1,128)S(1)}) custom-call(s32[1,48]{1,0:T(1,128)S(1)} %copy-done.9, f32[16,8,384]{2,1,0:T(8,128)S(1)} %all-to-all-done.got.got1, ...), custom_call_target="tpu_custom_call" | custom-call | tf_op jit(solution)/shard_map/spread/pallas_call | solution.py:346
  53.5 1.3 %collective-permute-start.2 = (f32[6,512]{1,0:T(8,128)S(1)}, f32[6,512]{1,0:T(8,128)S(1)}, u32[]{:S(2)}, u32[]{:S(2)}) collective-permute-start(f32[6,512]{1,0:T(8,128)S(1)} %get-tuple-element.22), channel_id=1, source_target_pairs={{0,1},{1,2},{2,3},{3,4},{4,5},{5,6},{6,7},{7,8},{8,9},{9,10},{10,1... | collective-permute-start | bytes 36872 | tf_op jit(solution)/shard_map/ppermute | solution.py:353
  54.8 1.3 %collective-permute-start.3 = (f32[6,512]{1,0:T(8,128)S(1)}, f32[6,512]{1,0:T(8,128)S(1)}, u32[]{:S(2)}, u32[]{:S(2)}) collective-permute-start(f32[6,512]{1,0:T(8,128)S(1)} %get-tuple-element.23), channel_id=1, source_target_pairs={{1,0},{2,1},{3,2},{4,3},{5,4},{6,5},{7,6},{8,7},{9,8},{10,9},{11,1... | collective-permute-start | bytes 36872 | tf_op jit(solution)/shard_map/ppermute | solution.py:354
  56.1 0.0 collective-permute-done.2.low1
  56.2 1.8 %collective-permute-done.3.high1 = f32[6,512]{1,0:T(8,128)S(1)} collective-permute-done((f32[6,512]{1,0:T(8,128)S(1)}, f32[6,512]{1,0:T(8,128)S(1)}, u32[]{:S(2)}, u32[]{:S(2)}) %collective-permute-start.3) | collective-permute-done | bytes 12320 | tf_op jit(solution)/shard_map/ppermute | solution.py:354
  57.9 1.3 %edge.1 = (f32[16,4,384]{2,1,0:T(4,128)S(1)}, f32[3,64,512]{2,1,0:T(8,128)S(1)}) custom-call(s32[1,48]{1,0:T(1,128)S(1)} %copy-done.9, f32[3,64,512]{2,1,0:T(8,128)S(1)} %copy-done.5, f32[3,64,512]{2,1,0:T(8,128)S(1)} %get-tuple-element.19.v1, f32[3,64,512]{2,1,0:T(8,128)S(1)} %get-tuple-element.20.dv1, f32[3,64,512]{2,1,0:T(8,128)S(1)} %get-tuple-element.21.v2, ...), custom_call_target="tpu_custom_call" | custom-call | tf_op jit(solution)/shard_map/edge/pallas_call | solution.py:355
  59.2 14.1 %all_to_all.21.got3 = f32[16,4,384]{2,1,0:T(4,128)S(1)} all-to-all(f32[16,4,384]{2,1,0:T(4,128)S(1)} %get-tuple-element.25), channel_id=1, replica_groups=mesh['groups'=2,'gx'=16] {'gx'}, dimensions={0} | all-to-all | bytes 196608 | tf_op jit(solution)/shard_map/all_to_all | solution.py:332
  73.3 0.0 copy-done.1
  73.3 3.6 %last.1 = (f32[16,4,384]{2,1,0:T(4,128)S(1)}, f32[3,64,512]{2,1,0:T(8,128)S(1)}, f32[3,64,512]{2,1,0:T(8,128)S(1)}, f32[3,64,512]{2,1,0:T(8,128)S(1)}, f32[3,64,512]{2,1,0:T(8,128)S(1)}) custom-call(s32[36,2]{1,0:T(8,128)S(1)} %copy.12.pairs, s32[1]{0:T(128)S(6)} %copy.19.live, f32[16,8,384]{2,1,0:T(8,128)S(1)} %all-to-all-done.got.got1, ...), custom_call_target="tpu_custom_call" | custom-call | tf_op jit(solution)/shard_map/last/pallas_call | solution.py:359
  76.9 10.0 %all_to_all.22.got4 = f32[16,4,384]{2,1,0:T(4,128)S(1)} all-to-all(f32[16,4,384]{2,1,0:T(4,128)S(1)} %get-tuple-element.27), channel_id=1, replica_groups=mesh['groups'=2,'gx'=16] {'gx'}, dimensions={0} | all-to-all | bytes 196608 | tf_op jit(solution)/shard_map/all_to_all | solution.py:332
  86.9 1.8 %finish.1 = (f32[3,64,512]{2,1,0:T(8,128)}, f32[3,64,512]{2,1,0:T(8,128)}) custom-call(s32[1,48]{1,0:T(1,128)S(1)} %copy-done.9, f32[16,4,384]{2,1,0:T(4,128)S(1)} %all_to_all.22.got4, f32[3,64,512]{2,1,0:T(8,128)S(1)} %get-tuple-element.28.part, f32[3,64,512]{2,1,0:T(8,128)S(1)} %get-tuple-element.29.r2, f32[3,64,512]{2,1,0:T(8,128)S(1)} %get-tuple-element.30.d2, ...), custom_call_target="tpu_custom_call" | custom-call | tf_op jit(solution)/shard_map/finish/pallas_call | solution.py:366
  (14 shorter events, 0.0 us)
Async XLA Ops:
  0.6 51.6 %copy-start.9 = (s32[1,48]{1,0:T(1,128)S(1)}, s32[1,48]{1,0:T(1,128)}, u32[]{:S(2)}) copy-start(s32[1,48]{1,0:T(1,128)} %send.7) | copy-start | bytes 580
  2.2 3.7 %collective-permute-start = (f32[4,512]{1,0:T(4,128)S(1)}, f32[4,512]{1,0:T(4,128)S(1)}, u32[]{:S(2)}, u32[]{:S(2)}) collective-permute-start(f32[4,512]{1,0:T(4,128)S(1)} %pad_maximum_fusion), channel_id=1, source_target_pairs={{0,1},{1,2},{2,3},{3,4},{4,5},{5,6},{6,7},{7,8},{8,9},{9,10},{10,1... | collective-permute-start | bytes 24584 | tf_op jit(solution)/shard_map/ppermute | solution.py:334
  4.6 5.2 %collective-permute-start.1 = (f32[4,512]{1,0:T(4,128)S(1)}, f32[4,512]{1,0:T(4,128)S(1)}, u32[]{:S(2)}, u32[]{:S(2)}) collective-permute-start(f32[4,512]{1,0:T(4,128)S(1)} %concatenate.7), channel_id=1, source_target_pairs={{1,0},{2,1},{3,2},{4,3},{5,4},{6,5},{7,6},{8,7},{9,8},{10,9},{11,1... | collective-permute-start | bytes 24584 | tf_op jit(solution)/shard_map/ppermute | solution.py:335
  9.8 1.0 %copy-start.2 = (f32[2,64,512]{2,1,0:T(8,128)S(1)}, f32[2,64,512]{2,1,0:T(8,128)}, u32[]{:S(2)}) copy-start(f32[2,64,512]{2,1,0:T(8,128)} %stiff.7) | copy-start | bytes 786436
  10.8 1.0 %copy-start.4 = (f32[3,64,512]{2,1,0:T(8,128)S(1)}, f32[3,64,512]{2,1,0:T(8,128)}, u32[]{:S(2)}) copy-start(f32[3,64,512]{2,1,0:T(8,128)} %b.5) | copy-start | bytes 1179652
  11.8 0.9 %copy-start.6 = (f32[64,512]{1,0:T(8,128)S(1)}, f32[64,512]{1,0:T(8,128)}, u32[]{:S(2)}) copy-start(f32[64,512]{1,0:T(8,128)} %mass.5) | copy-start | bytes 393220
  12.7 0.7 copy-start.8
  13.3 38.9 %copy-start.3 = (f32[2,64,512]{2,1,0:T(8,128)S(1)}, f32[2,64,512]{2,1,0:T(8,128)}, u32[]{:S(2)}) copy-start(f32[2,64,512]{2,1,0:T(8,128)} %stiff.7) | copy-start | bytes 786436
  13.3 38.9 %copy-start.7 = (f32[64,512]{1,0:T(8,128)S(1)}, f32[64,512]{1,0:T(8,128)}, u32[]{:S(2)}) copy-start(f32[64,512]{1,0:T(8,128)} %mass.5) | copy-start | bytes 393220
  13.3 44.6 %copy-start.5 = (f32[3,64,512]{2,1,0:T(8,128)S(1)}, f32[3,64,512]{2,1,0:T(8,128)}, u32[]{:S(2)}) copy-start(f32[3,64,512]{2,1,0:T(8,128)} %b.5) | copy-start | bytes 1179652
  15.3 16.8 %all-to-all-start = ((f32[16,8,384]{2,1,0:T(8,128)}), f32[16,8,384]{2,1,0:T(8,128)S(1)}, u32[]{:S(2)}, u32[]{:S(2)}) async-start(f32[16,8,384]{2,1,0:T(8,128)} %get-tuple-element.17), calls=%async_computation | async-start | bytes 393216 | tf_op jit(solution)/shard_map/all_to_all | solution.py:332
  32.1 4.0 %copy-start = (bf16[36,384,384]{2,1,0:T(8,128)(2,1)S(1)}, bf16[36,384,384]{2,1,0:T(8,128)(2,1)}, u32[]{:S(2)}) copy-start(bf16[36,384,384]{2,1,0:T(8,128)(2,1)} %hessian.3) | copy-start | bytes 31850500
  36.2 37.1 %copy-start.1 = (bf16[36,384,384]{2,1,0:T(8,128)(2,1)S(1)}, bf16[36,384,384]{2,1,0:T(8,128)(2,1)}, u32[]{:S(2)}) copy-start(bf16[36,384,384]{2,1,0:T(8,128)(2,1)} %hessian.3) | copy-start | bytes 31850500
  53.5 2.6 %collective-permute-start.2 = (f32[6,512]{1,0:T(8,128)S(1)}, f32[6,512]{1,0:T(8,128)S(1)}, u32[]{:S(2)}, u32[]{:S(2)}) collective-permute-start(f32[6,512]{1,0:T(8,128)S(1)} %get-tuple-element.22), channel_id=1, source_target_pairs={{0,1},{1,2},{2,3},{3,4},{4,5},{5,6},{6,7},{7,8},{8,9},{9,10},{10,1... | collective-permute-start | bytes 36872 | tf_op jit(solution)/shard_map/ppermute | solution.py:353
  54.8 3.1 %collective-permute-start.3 = (f32[6,512]{1,0:T(8,128)S(1)}, f32[6,512]{1,0:T(8,128)S(1)}, u32[]{:S(2)}, u32[]{:S(2)}) collective-permute-start(f32[6,512]{1,0:T(8,128)S(1)} %get-tuple-element.23), channel_id=1, source_target_pairs={{1,0},{2,1},{3,2},{4,3},{5,4},{6,5},{7,6},{8,7},{9,8},{10,9},{11,1... | collective-permute-start | bytes 36872 | tf_op jit(solution)/shard_map/ppermute | solution.py:354

commit v4 on v3

v4 whole, which is shorter than its diff:
```python
import jax
import jax.numpy as jnp
from jax import lax
from jax.experimental import pallas as pl
from jax.experimental.pallas import tpu as pltpu
from jax.sharding import PartitionSpec as P

F32 = jnp.float32
BF16 = jnp.bfloat16
CAP = 3
SUMS_TWO, SUMS_ONE = 2 * CAP, CAP
CODE_LANE = 64


def iota(shape, dim):
    return lax.broadcasted_iota(jnp.int32, shape, dim)


def total(value):
    return jnp.sum(jnp.sum(value, axis=0, keepdims=True), axis=1, keepdims=True)


def line_of(scalars, width):
    lanes = iota((1, width), 1)
    line = jnp.zeros((1, width), F32)
    for k, value in enumerate(scalars):
        line = jnp.where(lanes == k, value, line)
    return line


def line_sum(message, row):
    peers = message.shape[0]
    parts = [message[d, row : row + 1, 0:128] for d in range(peers)]
    while len(parts) > 1:
        parts = [a + b for a, b in zip(parts[::2], parts[1::2])] + (
            parts[-1:] if len(parts) % 2 else []
        )
    return parts[0]


def pick(line, k):
    return line[:, k : k + 1]


def place_of(send, position, col_blocks):
    block = send[0, position]
    return lax.div(block, jnp.int32(col_blocks)), lax.rem(block, jnp.int32(col_blocks))


def scatter_blocks(send, message, panels):
    peers = message.shape[0]
    _, col_blocks, _, block_len = panels[0].shape
    for field in panels:
        field[...] = jnp.zeros_like(field)

    def one(d, carry):
        for c in range(CAP):
            row, col = place_of(send, d * CAP + c, col_blocks)
            for f, field in enumerate(panels):
                for e in range(3):
                    field[e, col, pl.ds(row, 1), :] = message[
                        d, f * CAP + c : f * CAP + c + 1, e * block_len : (e + 1) * block_len
                    ]
        return carry

    lax.fori_loop(0, peers, one, 0, unroll=4)


def to_panels(panels, e, value):
    _, col_blocks, _, block_len = panels.shape
    for q in range(col_blocks):
        panels[e, q] = value[:, q * block_len : (q + 1) * block_len]


def from_panels(panels, e):
    return jnp.concatenate([panels[e, q] for q in range(panels.shape[1])], axis=1)


def put_line(message, row, line):
    for d in range(message.shape[0]):
        message[d, row : row + 1, :] = line


def inner_apply(v, mass, kx, ky):
    rows, cols = v.shape
    row_ids = iota((rows, cols), 0)
    flux_x = jnp.where(row_ids == rows - 1, 0.0, kx * (v - pltpu.roll(v, rows - 1, 0)))
    flux_y = ky * (v - pltpu.roll(v, cols - 1, 1))
    return mass * v + (flux_x - pltpu.roll(flux_x, 1, 0)) + (flux_y - pltpu.roll(flux_y, 1, 1))


def masked_ky(stiff):
    ky = stiff[1]
    return jnp.where(iota(ky.shape, 1) == ky.shape[1] - 1, 0.0, ky)


def rounded(value):
    return value.astype(BF16).astype(F32)


def packed_line(scalars):
    parts = []
    for value in scalars:
        high = rounded(value)
        middle = rounded(value - high)
        parts += [high, middle, value - high - middle]
    return line_of(parts, 128)


def pick_packed(line, k):
    return pick(line, 3 * k) + pick(line, 3 * k + 1) + pick(line, 3 * k + 2)


def thrice(tile):
    return jnp.concatenate([tile] * 3, axis=1)


def write_rim(target, field):
    rows, block_len = field.shape[1], 128
    col_blocks = field.shape[2] // block_len
    for side, row in enumerate((0, rows - 1)):
        for q in range(col_blocks):
            for e in range(3):
                line = side * col_blocks + q
                target[line : line + 1, e * block_len : (e + 1) * block_len] = field[
                    e, row : row + 1, q * block_len : (q + 1) * block_len
                ]


def rim_row(tile, side, e):
    block_len = tile.shape[1] // 3
    half = tile.shape[0] // 2
    return jnp.concatenate(
        [
            tile[side * half + q : side * half + q + 1, e * block_len : (e + 1) * block_len]
            for q in range(half)
        ],
        axis=1,
    )


def across(before, after):
    half = before.shape[0] // 2
    return pltpu.roll(jnp.where(iota(before.shape, 0) >= half, before, after), half, 0)


def around(d, peers):
    return jnp.maximum(d - 1, 0), jnp.minimum(d + 1, peers - 1)


def rim_coefs(tiles, d):
    before, _ = around(d, tiles.shape[0])
    here, other = tiles[d, 0:8, 384:512], tiles[before, 0:8, 384:512]
    other = jnp.where(d > 0, other, 0.0)
    return thrice(jnp.where(iota(here.shape, 0) < 4, other, here))


def chosen(code, tile):
    return jnp.sum(
        jnp.where(iota(tile.shape, 0).astype(F32) == code, tile, 0.0), axis=0, keepdims=True
    )


def start_kernel(send, b, mass, stiff, message, loc, b_panels, loc_panels, rim, stage):
    rows, peers = b.shape[1], message.shape[0]
    col_blocks, block_len = b_panels.shape[1], b_panels.shape[3]
    ky = masked_ky(stiff)
    sq = dot = None
    for e in range(3):
        v = b[e]
        image = inner_apply(v, mass[...], stiff[0], ky)
        loc[e] = image
        to_panels(b_panels, e, v)
        to_panels(loc_panels, e, image)
        sq = v * v if sq is None else sq + v * v
        dot = v * image if dot is None else dot + v * image
    write_rim(rim, b)
    ends = lax.axis_index("gx") == peers - 1
    for q in range(col_blocks):
        kx = stiff[0, rows - 1 : rows, q * block_len : (q + 1) * block_len]
        kx = jnp.where(ends, 0.0, kx)
        rim[q : q + 1, 3 * block_len :] = kx
        rim[col_blocks + q : col_blocks + q + 1, 3 * block_len :] = kx
    line = packed_line([total(sq), total(dot)])
    lanes, sub = iota((1, 128), 1), iota((8, 3 * block_len), 0)
    sub_one = iota((8, block_len), 0)

    def one(d, carry):
        own_line = line
        for c in range(CAP):
            row, col = place_of(send, d * CAP + c, col_blocks)
            code = jnp.where(row == 0, col, jnp.where(row == rows - 1, col_blocks + col, 99))
            own_line = jnp.where(lanes == CODE_LANE + c, code.astype(F32), own_line)
            for e in range(3):
                span = slice(e * block_len, (e + 1) * block_len)
                stage[d, c : c + 1, span] = b_panels[e, col, pl.ds(row, 1), :]
                stage[d, CAP + c : CAP + c + 1, span] = loc_panels[e, col, pl.ds(row, 1), :]
        body = stage[d]
        rest = pltpu.roll(body - rounded(body), 3, 0)
        body = jnp.where(sub >= 2 * CAP, rest, body)
        extra = jnp.where(sub_one == 4, wide(own_line), 0.0)
        for j in range(3):
            piece = rest[0:1, j * block_len : (j + 1) * block_len]
            extra = jnp.where(sub_one == j, wide(piece), extra)
        lower = jnp.concatenate([body, extra], axis=1)
        message[d] = jnp.concatenate([rim[...], lower], axis=0).astype(BF16)
        return carry

    lax.fori_loop(0, peers, one, 0, unroll=4)


def contact_products(pairs, live_count, x8, y8, held):
    y8[...] = jnp.zeros_like(y8)
    for h in range(held.shape[0]):
        a, b = pairs[h, 0], pairs[h, 1]
        delta = x8[a] - x8[b]
        delta = jnp.where(h < live_count, delta, 0.0)
        coarse = delta.astype(jnp.bfloat16).astype(F32)
        both = jnp.concatenate([coarse, delta - coarse], axis=0).astype(jnp.bfloat16)
        product = jnp.dot(both, held[h], preferred_element_type=F32)
        y = product[0:8] + product[8:16]
        y8[a] = y8[a] + y
        y8[b] = y8[b] - y


def wide(row):
    return jnp.broadcast_to(row, (8, row.shape[1]))


def contact_dot(x8, y8):
    value = x8[0] * y8[0]
    for p in range(1, x8.shape[0]):
        value = value + x8[p] * y8[p]
    return total(value[0:1])


def owner_kernel(
    pairs, live, got, hessian, message, held, own, known, x8, y8, z8, f8, tiles, corr
):
    peers, _, _ = got.shape
    width = x8.shape[2]
    block_len = width // 3
    for d in range(peers):
        tiles[d] = got[d].astype(F32)

    def one(d, carry):
        energy, sums = carry
        before, after = around(d, peers)
        diff = tiles[d, 0:8, 0:width] - across(
            tiles[before, 0:8, 0:width], tiles[after, 0:8, 0:width]
        )
        fix = rim_coefs(tiles, d) * diff
        corr[d] = fix
        body, extra = tiles[d, 8:16, 0:width], tiles[d, 8:16, width:]
        line = extra[4:5, :]
        rest = [body[6:7], body[7:8], jnp.concatenate([extra[j : j + 1] for j in range(3)], axis=1)]
        for c in range(CAP):
            p = d * CAP + c
            x8[p] = wide(body[c : c + 1])
            value = body[CAP + c : CAP + c + 1] + rest[c]
            f8[p] = wide(value + chosen(pick(line, CODE_LANE + c), fix))
        return energy + fix * diff, sums + line

    zero = jnp.zeros((8, width), F32)
    energy, sums = lax.fori_loop(0, peers, one, (zero, jnp.zeros((1, block_len), F32)), unroll=4)
    known[...] = line_of(
        [pick_packed(sums, 0), pick_packed(sums, 1) + 0.5 * total(energy)], known.shape[1]
    )
    own[...] = corr[lax.axis_index("gx")]

    contact_products(pairs, live[0], x8, y8, hessian)
    line = line_of([contact_dot(x8, y8)], width)
    for p in range(x8.shape[0]):
        x8[p] = f8[p] + y8[p]
    contact_products(pairs, live[0], x8, z8, hessian)
    sub = iota((8, width), 0)
    for d in range(peers):
        tile = jnp.where(sub == SUMS_TWO, wide(line), 0.0)
        kept = tiles[d, 8:16, 0:width]
        for c in range(CAP):
            tile = jnp.where(sub == c, y8[d * CAP + c], tile)
            tile = jnp.where(sub == CAP + c, z8[d * CAP + c], tile)
            kept = jnp.where(sub == CAP + c, x8[d * CAP + c], kept)
        message[d] = tile
        held[d] = kept


def middle_kernel(
    send, got2, own, known1, b, loc, mass, stiff, message, v1, v2, known, cb, cv1, panels, common, stage
):
    rows, peers = b.shape[1], message.shape[0]
    col_blocks, block_len = panels.shape[1], panels.shape[3]
    scatter_blocks(send, got2, [cb, cv1])
    ky = masked_ky(stiff)
    rr0 = pick(known1[...], 0)
    alpha0 = rr0 / (pick(known1[...], 1) + pick(line_sum(got2, SUMS_TWO), 0))
    known[...] = line_of([rr0, alpha0], known.shape[1])
    sums = None
    for e in range(3):
        v1[e] = loc[e] + from_panels(cb, e)
        for side, row in enumerate((0, rows - 1)):
            v1[e, row : row + 1, :] = v1[e, row : row + 1, :] + rim_row(own[...], side, e)
        image = v1[e]
        inner = inner_apply(image, mass[...], stiff[0], ky)
        to_panels(panels, e, inner)
        second = inner + from_panels(cv1, e)
        v2[e] = second
        right = b[e]
        r1 = right - alpha0 * image
        w = image - alpha0 * second
        terms = [r1 * r1, r1 * w, r1 * image, right * w, right * image, w * w, w * image, image * image]
        sums = terms if sums is None else [s + t for s, t in zip(sums, terms)]
    write_rim(common.at[0], v1)
    write_rim(common.at[1], v2)
    line = packed_line([total(s) for s in sums])
    line = jnp.broadcast_to(line, (16, block_len))
    sub = iota((16, block_len), 0)

    def one(d, carry):
        for c in range(CAP):
            row, col = place_of(send, d * CAP + c, col_blocks)
            for e in range(3):
                stage[d, c * 3 + e : c * 3 + e + 1, :] = panels[e, col, pl.ds(row, 1), :]
        extra = jnp.where(sub < 9, stage[d], jnp.where(sub == 9, line, 0.0))
        rims = jnp.concatenate([common[0], common[1]], axis=0)
        message[d] = jnp.concatenate([rims, extra], axis=1).astype(BF16)
        return carry

    lax.fori_loop(0, peers, one, 0, unroll=4)


def coefficients(known, sums, b_x, v1_x, v2_x, x_x):
    rr0, alpha0 = pick(known, 0), pick(known, 1)
    rr1, r1w, r1v1, bw, bv1, ww, wv1, v1v1 = [pick_packed(sums, k) for k in range(8)]
    r1w = r1w - alpha0 * (b_x - alpha0 * v1_x)
    bw = bw - alpha0 * b_x
    ww = ww - 2.0 * alpha0 * (v1_x - alpha0 * v2_x) + alpha0 * alpha0 * x_x
    wv1 = wv1 - alpha0 * v1_x
    beta0 = rr1 / rr0
    alpha1 = rr1 / (r1w + beta0 * (r1v1 + bw) + beta0 * beta0 * bv1)
    image_sq = ww + 2.0 * beta0 * wv1 + beta0 * beta0 * v1v1
    rr2 = rr1 - 2.0 * alpha1 * (r1w + beta0 * r1v1) + alpha1 * alpha1 * image_sq
    return alpha0, beta0, alpha1, rr2 / rr1


def advance(b, v1, v2, coefs):
    alpha0, beta0, alpha1, beta1 = coefs
    r1 = b - alpha0 * v1
    d1 = r1 + beta0 * b
    r2 = r1 - alpha1 * (v1 - alpha0 * v2 + beta0 * v1)
    return d1, r2, r2 + beta1 * d1


def last_kernel(
    pairs, live, got1, got3, held, sent2, known, b, v1, v2, mass, stiff, hessian,
    message, part, r2_out, d2_out, dd2, x8, y8, tiles1, tiles3, corr, rim,
):
    peers = got1.shape[0]
    width = x8.shape[2]
    rows = b.shape[1]
    for d in range(peers):
        tiles1[d] = got1[d].astype(F32)
        tiles3[d] = got3[d].astype(F32)

    def one(d, carry):
        before, after = around(d, peers)
        first = tiles3[d, 0:8, 0:width]
        fix = rim_coefs(tiles1, d) * (
            first - across(tiles3[before, 0:8, 0:width], tiles3[after, 0:8, 0:width])
        )
        corr[d] = fix
        others = [tiles1[d, 0:8, 0:width], first, tiles3[d, 8:16, 0:width], fix]
        return (
            *[kept + other * fix for kept, other in zip(carry, others)],
            carry[4] + tiles3[d, 9:10, width:],
        )

    zero = jnp.zeros((8, width), F32)
    *crossing, sums = lax.fori_loop(
        0, peers, one, (zero, zero, zero, zero, jnp.zeros((1, 128), F32)), unroll=4
    )
    coefs = coefficients(known[...], sums, *[total(value) for value in crossing])

    def two(d, carry):
        extra, line = tiles3[d, 0:16, width:], tiles1[d, 12:13, width:]
        fix = corr[d]
        kept, sent = held[d], sent2[d]
        for c in range(CAP):
            value = jnp.concatenate([extra[c * 3 + e : c * 3 + e + 1] for e in range(3)], axis=1)
            value = value + chosen(pick(line, CODE_LANE + c), fix) + sent[CAP + c : CAP + c + 1]
            x8[d * CAP + c] = wide(
                advance(kept[c : c + 1], kept[CAP + c : CAP + c + 1], value, coefs)[2]
            )
        return carry

    lax.fori_loop(0, peers, two, 0, unroll=4)

    me = lax.axis_index("gx")
    before, after = around(me, peers)
    ky = masked_ky(stiff)
    mine = corr[me] * (coefs[0] * coefs[2])
    for e in range(3):
        d1, r2, d2 = advance(b[e], v1[e], v2[e], coefs)
        part[e] = coefs[0] * b[e] + coefs[2] * d1
        r2_out[e] = r2
        d2_out[e] = d2
        for side, row in enumerate((0, rows - 1)):
            r2_out[e, row : row + 1, :] = r2_out[e, row : row + 1, :] + rim_row(mine, side, e)
            d2_out[e, row : row + 1, :] = d2_out[e, row : row + 1, :] + rim_row(mine, side, e)
    write_rim(rim, d2_out)

    def rim_direction(d):
        return advance(
            tiles1[d, 0:8, 0:width],
            tiles3[d, 0:8, 0:width],
            tiles3[d, 8:16, 0:width] + corr[d],
            coefs,
        )[2]

    fix = rim_coefs(tiles1, me) * (rim[...] - across(rim_direction(before), rim_direction(after)))
    sq = dot = None
    for e in range(3):
        r2, d2 = r2_out[e], d2_out[e]
        dd2[e] = inner_apply(d2, mass[...], stiff[0], ky)
        for side, row in enumerate((0, rows - 1)):
            dd2[e, row : row + 1, :] = dd2[e, row : row + 1, :] + rim_row(fix, side, e)
        sq = r2 * r2 if sq is None else sq + r2 * r2
        dot = d2 * dd2[e] if dot is None else dot + d2 * dd2[e]
    rr2, dad2 = total(sq), total(dot)

    contact_products(pairs, live[0], x8, y8, hessian)
    line = line_of([rr2, dad2 + contact_dot(x8, y8)], width)
    for d in range(peers):
        for c in range(CAP):
            message[d, c : c + 1, :] = y8[d * CAP + c, 0:1, :]
    put_line(message, SUMS_ONE, line)


def finish_kernel(send, got4, part, r2, d2, dd2, solution, residual, cd2):
    scatter_blocks(send, got4, [cd2])
    sums = line_sum(got4, SUMS_ONE)
    alpha2 = pick(sums, 0) / pick(sums, 1)
    for e in range(3):
        solution[e] = part[e] + alpha2 * d2[e]
        residual[e] = r2[e] - alpha2 * (dd2[e] + from_panels(cd2, e))


def call(kernel, spaces, outs, scratch=(), mebibytes=16, name=None):
    kinds = {"s": pltpu.SMEM, "v": pltpu.VMEM}
    return pl.pallas_call(
        kernel,
        out_shape=tuple(jax.ShapeDtypeStruct(shape, kind) for shape, kind in outs),
        in_specs=[pl.BlockSpec(memory_space=kinds[k]) for k in spaces],
        out_specs=tuple(pl.BlockSpec(memory_space=pltpu.VMEM) for _ in outs),
        scratch_shapes=[pltpu.VMEM(shape, F32) for shape in scratch],
        compiler_params=pltpu.CompilerParams(vmem_limit_bytes=mebibytes * 2**20),
        name=name,
    )


def per_device(right_side, masses, stiffness, hessian, send_list, pair_refs, counts):
    _, row_count, col_count = right_side.shape
    width = hessian.shape[1]
    block_len = width // 3
    peers = lax.axis_size("gx")
    assert send_list.shape[1] == peers * CAP and col_count == 4 * block_len and block_len == 128
    field = (right_side.shape, F32)
    two, one = ((peers, 8, width), F32), ((peers, 4, width), F32)
    full = ((peers, 16, 4 * block_len), BF16)
    panels = (3, 4, row_count, block_len)
    tiles, wide_tiles, rims = (peers * CAP, 8, width), (peers, 16, 4 * block_len), (peers, 8, width)
    line = ((1, 128), F32)

    def swap(message):
        return lax.all_to_all(message, "gx", split_axis=0, concat_axis=0, tiled=True)

    sent1, loc = call(
        start_kernel,
        "svvv",
        [full, field],
        [panels, panels, (8, 4 * block_len), rims],
        name="start",
    )(send_list, right_side, masses, stiffness)
    got1 = swap(sent1)
    sent2, held, own, known1 = call(
        owner_kernel,
        "ssvv",
        [two, two, ((8, width), F32), line],
        [tiles, tiles, tiles, tiles, wide_tiles, rims],
        32,
        name="owner",
    )(pair_refs, counts, got1, hessian)
    got2 = swap(sent2)
    sent3, v1, v2, known = call(
        middle_kernel,
        "svvvvvvv",
        [full, field, field, line],
        [panels, panels, panels, (2, 8, width), (peers, 16, block_len)],
        name="middle",
    )(send_list, got2, own, known1, right_side, loc, masses, stiffness)
    got3 = swap(sent3)
    sent4, part, r2, d2, dd2 = call(
        last_kernel,
        "ssvvvvvvvvvvv",
        [one, field, field, field, field],
        [tiles, tiles, wide_tiles, wide_tiles, rims, (8, width)],
        32,
        name="last",
    )(
        pair_refs, counts, got1, got3, held, sent2, known, right_side, v1, v2, masses, stiffness,
        hessian,
    )
    got4 = swap(sent4)
    return call(finish_kernel, "svvvvv", [field, field], [panels], name="finish")(
        send_list, got4, part, r2, d2, dd2
    )


def solution(mesh):
    placed = (
        P(None, ("groups", "gx"), None),
        P(("groups", "gx"), None),
        P(None, ("groups", "gx"), None),
        P(("groups", "gx"), None, None),
        P(("groups", "gx"), None),
        P(("groups", "gx"), None),
        P(("groups", "gx")),
    )
    return jax.shard_map(
        per_device,
        mesh=mesh,
        in_specs=placed,
        out_specs=(P(None, ("groups", "gx"), None), P(None, ("groups", "gx"), None)),
        check_vma=False,
    )
```

time: 89.4 us -> 76.2 us (0.85)
  starting transfers between devices: 14.1 us -> 7.39 us
  waiting for transfers between devices: 13.2 us -> 8.62 us
  local copies, waits for them, and re-layouts: 9.89 us -> 8.31 us
  blocking collectives: 35.7 us -> 34.6 us
  Pallas kernels: 14.4 us -> 15.5 us
    ppermute x4 -> x0, starting transfers between devices: 6.23 us -> none  [the longest x1 2.36 us: per_device(): lax.ppermute(jnp.concatenate([right_side[:, -1], stiffness[0, -1:]], axis...]
    ppermute x4 -> x0, waiting for transfers between devices: 5.66 us -> none  [the longest x1 3.89 us: per_device(): lax.ppermute(jnp.concatenate([right_side[:, 0], jnp.ones((1, col_count),...]
    all_to_all x3, blocking collectives: 35.7 us -> 34.6 us  [swap(): lax.all_to_all(message, 'gx', split_axis=0, concat_axis=0, tiled=True)]
    pallas_call x5 -> x4, Pallas kernels: 12.6 us -> 13.7 us  [the longest x1 5.12 us: per_device(): call(owner_kernel, 'ssvv', [two, two, ((8, width), F32), line], [tiles, t...]
    all_to_all x1, waiting for transfers between devices: 7.57 us -> 8.62 us  [swap(): lax.all_to_all(message, 'gx', split_axis=0, concat_axis=0, tiled=True)]
    unnamed x23 -> x21, local copies, waits for them, and re-layouts: 8.32 us -> 8.31 us
  transfers between devices with their start and end apart: 5 -> 1, of which waited for: 3 -> 1; matrix products, arithmetic and copies ran while one was open for 1% -> 1% of each run, Pallas kernels for 0% -> 0%
where the time goes in v4:
time: 76.2 us; the launch traced here: 75.7 us
  blocking collectives  34.6 us (45%)
  Pallas kernels  15.5 us (20%)
  waiting for transfers between devices  8.62 us (11%)
  local copies, waits for them, and re-layouts  8.31 us (11%)
  starting transfers between devices  7.39 us (10%)
  between operations  1.33 us (2%)
    all_to_all x3, blocking collectives, swap(): lax.all_to_all(message, 'gx', split_axis=0, concat_axis=0, tiled=True)  34.6 us
    all_to_all x1, waiting for transfers between devices, swap(): lax.all_to_all(message, 'gx', split_axis=0, concat_axis=0, tiled=True)  8.62 us
    unnamed x21, local copies, waits for them, and re-layouts  8.31 us
    all_to_all x1, starting transfers between devices, swap(): lax.all_to_all(message, 'gx', split_axis=0, concat_axis=0, tiled=True)  7.39 us
    pallas_call x1, Pallas kernels, per_device(): call(owner_kernel, 'ssvv', [two, two, ((8, width), F32), line], [tiles, t...  5.12 us
    pallas_call x1, Pallas kernels, per_device(): call(last_kernel, 'ssvvvvvvvvvvv', [one, field, field, field, field], [ti...  4.58 us
    pallas_call x1, Pallas kernels, per_device(): call(start_kernel, 'svvv', [full, field], [panels, panels, (8, 4 * block_...  2.07 us
    pallas_call x1, Pallas kernels, per_device(): call(middle_kernel, 'svvvvvvv', [full, field, field, line], [panels, pane...  1.9 us
  transfers between devices with their start and end apart: 1, of which 1 were waited for; matrix products, arithmetic and copies ran while one was open for 1% of the time, Pallas kernels for 0%

profile of v4, /device:TPU:0, one launch (start us, length us, event | category | flops | bytes accessed | tf_op | source)
XLA Modules:
  0.0 75.7 jit_solution(4060443319745523724)
XLA Ops:
  0.6 0.0 copy-start.2
  0.6 1.0 %copy-done.2 = f32[3,64,512]{2,1,0:T(8,128)S(1)} copy-done((f32[3,64,512]{2,1,0:T(8,128)S(1)}, f32[3,64,512]{2,1,0:T(8,128)}, u32[]{:S(2)}) %copy-start.2) | copy-done | bytes 393240
  1.6 0.0 copy-start.4
  1.6 0.9 %copy-done.4 = f32[2,64,512]{2,1,0:T(8,128)S(1)} copy-done((f32[2,64,512]{2,1,0:T(8,128)S(1)}, f32[2,64,512]{2,1,0:T(8,128)}, u32[]{:S(2)}) %copy-start.4) | copy-done | bytes 262168
  2.6 0.0 copy-start.6
  2.6 0.9 %copy-done.6 = f32[64,512]{1,0:T(8,128)S(1)} copy-done((f32[64,512]{1,0:T(8,128)S(1)}, f32[64,512]{1,0:T(8,128)}, u32[]{:S(2)}) %copy-start.6) | copy-done | bytes 131096
  3.5 0.0 copy-start.8
  3.5 0.7 copy-done.8
  4.1 0.0 copy-start.3
  4.1 0.0 copy-start.5
  4.1 0.0 copy-start.7
  4.1 0.0 copy-start.9
  4.1 2.1 %start.1 = (bf16[16,16,512]{2,1,0:T(8,128)(2,1)}, f32[3,64,512]{2,1,0:T(8,128)S(1)}) custom-call(s32[1,48]{1,0:T(1,128)S(1)} %copy-done.8, f32[3,64,512]{2,1,0:T(8,128)S(1)} %copy-done.2, f32[64,512]{1,0:T(8,128)S(1)} %copy-done.6, f32[2,64,512]{2,1,0:T(8,128)S(1)} %copy-done.4), custom_call_target="tpu_custom_call" | custom-call | tf_op jit(solution)/shard_map/start/pallas_call | solution.py:477
  6.2 7.4 %all-to-all-start = ((bf16[16,16,512]{2,1,0:T(8,128)(2,1)}), bf16[16,16,512]{2,1,0:T(8,128)(2,1)S(1)}, u32[]{:S(2)}, u32[]{:S(2)}) async-start(bf16[16,16,512]{2,1,0:T(8,128)(2,1)} %get-tuple-element.17), calls=%async_computation | async-start | bytes 524288 | tf_op jit(solution)/shard_map/all_to_all | solution.py:475
  14.3 0.8 %copy.10.pairs = s32[36,2]{1,0:T(8,128)S(1)} copy(s32[36,2]{0,1:T(2,128)} %param.12) | data formatting | bytes 576 | tf_op args[5]
  15.0 8.6 %all-to-all-done.got.got1 = bf16[16,16,512]{2,1,0:T(8,128)(2,1)S(1)} async-done(((bf16[16,16,512]{2,1,0:T(8,128)(2,1)}), bf16[16,16,512]{2,1,0:T(8,128)(2,1)S(1)}, u32[]{:S(2)}, u32[]{:S(2)}) %all-to-all-start) | async-done | bytes 262176 | tf_op jit(solution)/shard_map/all_to_all | solution.py:475
  23.7 0.0 copy-start
  23.7 4.0 %copy-done = bf16[36,384,384]{2,1,0:T(8,128)(2,1)S(1)} copy-done((bf16[36,384,384]{2,1,0:T(8,128)(2,1)S(1)}, bf16[36,384,384]{2,1,0:T(8,128)(2,1)}, u32[]{:S(2)}) %copy-start) | copy-done | bytes 10616856
  27.7 0.0 copy-start.1
  27.7 5.1 %owner.1 = (f32[16,8,384]{2,1,0:T(8,128)S(1)}, f32[16,8,384]{2,1,0:T(8,128)S(1)}, f32[8,384]{1,0:T(8,128)S(1)}, f32[1,128]{1,0:T(1,128)S(1)}) custom-call(s32[36,2]{1,0:T(8,128)S(1)} %copy.10.pairs, s32[1]{0:T(128)S(6)} %copy.11.live, bf16[16,16,512]{2,1,0:T(8,128)(2,1)S(1)} %all-to-all-done.got.got1, bf16[36,384,384]{2,1,0:T(8,128)(2,1)S(1)} %copy-done), custom_call_target="tpu_custom_call" | custom-call | tf_op jit(solution)/shard_map/owner/pallas_call | solution.py:485
  32.8 11.8 %all_to_all.20.got2 = f32[16,8,384]{2,1,0:T(8,128)S(1)} all-to-all(f32[16,8,384]{2,1,0:T(8,128)S(1)} %get-tuple-element.18.sent2), channel_id=1, replica_groups=mesh['groups'=2,'gx'=16] {'gx'}, dimensions={0} | all-to-all | bytes 393216 | tf_op jit(solution)/shard_map/all_to_all | solution.py:475
  44.6 0.0 copy-done.3
  44.6 0.0 copy-done.5
  44.6 0.0 copy-done.7
  44.6 0.0 copy-done.9
  44.6 1.9 %middle.1 = (bf16[16,16,512]{2,1,0:T(8,128)(2,1)S(1)}, f32[3,64,512]{2,1,0:T(8,128)S(1)}, f32[3,64,512]{2,1,0:T(8,128)S(1)}, f32[1,128]{1,0:T(1,128)S(1)}) custom-call(s32[1,48]{1,0:T(1,128)S(1)} %copy-done.9, f32[16,8,384]{2,1,0:T(8,128)S(1)} %all_to_all.20.got2, f32[8,384]{1,0:T(8,128)S(1)} %get-tuple-element.19.own, ...), custom_call_target="tpu_custom_call" | custom-call | tf_op jit(solution)/shard_map/middle/pallas_call | solution.py:494
  46.5 12.6 %all_to_all.21.got3 = bf16[16,16,512]{2,1,0:T(8,128)(2,1)S(1)} all-to-all(bf16[16,16,512]{2,1,0:T(8,128)(2,1)S(1)} %get-tuple-element.22), channel_id=1, replica_groups=mesh['groups'=2,'gx'=16] {'gx'}, dimensions={0} | all-to-all | bytes 524288 | tf_op jit(solution)/shard_map/all_to_all | solution.py:475
  59.1 0.0 copy-done.1
  59.1 4.6 %last.1 = (f32[16,4,384]{2,1,0:T(4,128)S(1)}, f32[3,64,512]{2,1,0:T(8,128)S(1)}, f32[3,64,512]{2,1,0:T(8,128)S(1)}, f32[3,64,512]{2,1,0:T(8,128)S(1)}, f32[3,64,512]{2,1,0:T(8,128)S(1)}) custom-call(s32[36,2]{1,0:T(8,128)S(1)} %copy.10.pairs, s32[1]{0:T(128)S(6)} %copy.11.live, bf16[16,16,512]{2,1,0:T(8,128)(2,1)S(1)} %all-to-all-done.got.got1, ...), custom_call_target="tpu_custom_call" | custom-call | tf_op jit(solution)/shard_map/last/pallas_call | solution.py:502
  63.7 10.2 %all_to_all.22.got4 = f32[16,4,384]{2,1,0:T(4,128)S(1)} all-to-all(f32[16,4,384]{2,1,0:T(4,128)S(1)} %get-tuple-element.27), channel_id=1, replica_groups=mesh['groups'=2,'gx'=16] {'gx'}, dimensions={0} | all-to-all | bytes 196608 | tf_op jit(solution)/shard_map/all_to_all | solution.py:475
  73.9 1.8 %finish.1 = (f32[3,64,512]{2,1,0:T(8,128)}, f32[3,64,512]{2,1,0:T(8,128)}) custom-call(s32[1,48]{1,0:T(1,128)S(1)} %copy-done.9, f32[16,4,384]{2,1,0:T(4,128)S(1)} %all_to_all.22.got4, f32[3,64,512]{2,1,0:T(8,128)S(1)} %get-tuple-element.28.part, f32[3,64,512]{2,1,0:T(8,128)S(1)} %get-tuple-element.29.r2, f32[3,64,512]{2,1,0:T(8,128)S(1)} %get-tuple-element.30.d2, ...), custom_call_target="tpu_custom_call" | custom-call | tf_op jit(solution)/shard_map/finish/pallas_call | solution.py:514
Async XLA Ops:
  0.6 1.0 %copy-start.2 = (f32[3,64,512]{2,1,0:T(8,128)S(1)}, f32[3,64,512]{2,1,0:T(8,128)}, u32[]{:S(2)}) copy-start(f32[3,64,512]{2,1,0:T(8,128)} %b.5) | copy-start | bytes 1179652
  1.6 0.9 %copy-start.4 = (f32[2,64,512]{2,1,0:T(8,128)S(1)}, f32[2,64,512]{2,1,0:T(8,128)}, u32[]{:S(2)}) copy-start(f32[2,64,512]{2,1,0:T(8,128)} %stiff.5) | copy-start | bytes 786436
  2.6 0.9 %copy-start.6 = (f32[64,512]{1,0:T(8,128)S(1)}, f32[64,512]{1,0:T(8,128)}, u32[]{:S(2)}) copy-start(f32[64,512]{1,0:T(8,128)} %mass.5) | copy-start | bytes 393220
  3.5 0.7 copy-start.8
  4.1 40.4 %copy-start.3 = (f32[3,64,512]{2,1,0:T(8,128)S(1)}, f32[3,64,512]{2,1,0:T(8,128)}, u32[]{:S(2)}) copy-start(f32[3,64,512]{2,1,0:T(8,128)} %b.5) | copy-start | bytes 1179652
  4.1 40.4 %copy-start.5 = (f32[2,64,512]{2,1,0:T(8,128)S(1)}, f32[2,64,512]{2,1,0:T(8,128)}, u32[]{:S(2)}) copy-start(f32[2,64,512]{2,1,0:T(8,128)} %stiff.5) | copy-start | bytes 786436
  4.1 40.4 %copy-start.7 = (f32[64,512]{1,0:T(8,128)S(1)}, f32[64,512]{1,0:T(8,128)}, u32[]{:S(2)}) copy-start(f32[64,512]{1,0:T(8,128)} %mass.5) | copy-start | bytes 393220
  4.1 40.4 %copy-start.9 = (s32[1,48]{1,0:T(1,128)S(1)}, s32[1,48]{1,0:T(1,128)}, u32[]{:S(2)}) copy-start(s32[1,48]{1,0:T(1,128)} %send.5) | copy-start | bytes 580
  6.2 17.4 %all-to-all-start = ((bf16[16,16,512]{2,1,0:T(8,128)(2,1)}), bf16[16,16,512]{2,1,0:T(8,128)(2,1)S(1)}, u32[]{:S(2)}, u32[]{:S(2)}) async-start(bf16[16,16,512]{2,1,0:T(8,128)(2,1)} %get-tuple-element.17), calls=%async_computation | async-start | bytes 524288 | tf_op jit(solution)/shard_map/all_to_all | solution.py:475
  23.7 4.0 %copy-start = (bf16[36,384,384]{2,1,0:T(8,128)(2,1)S(1)}, bf16[36,384,384]{2,1,0:T(8,128)(2,1)}, u32[]{:S(2)}) copy-start(bf16[36,384,384]{2,1,0:T(8,128)(2,1)} %hessian.3) | copy-start | bytes 31850500
  27.7 31.5 %copy-start.1 = (bf16[36,384,384]{2,1,0:T(8,128)(2,1)S(1)}, bf16[36,384,384]{2,1,0:T(8,128)(2,1)}, u32[]{:S(2)}) copy-start(bf16[36,384,384]{2,1,0:T(8,128)(2,1)} %hessian.3) | copy-start | bytes 31850500

commit v5 on v4

--- a/solution.py
+++ b/solution.py
@@ -161,7 +161,11 @@
     )
 
 
-def start_kernel(send, b, mass, stiff, message, loc, b_panels, loc_panels, rim, stage):
+def announce_kernel(hessian, token):
+    token[...] = jnp.zeros_like(token)
+
+
+def start_kernel(_, send, b, mass, stiff, message, loc, b_panels, loc_panels, rim, stage):
     rows, peers = b.shape[1], message.shape[0]
     col_blocks, block_len = b_panels.shape[1], b_panels.shape[3]
     ky = masked_ky(stiff)
@@ -212,7 +216,7 @@
 def contact_products(pairs, live_count, x8, y8, held):
     y8[...] = jnp.zeros_like(y8)
     for h in range(held.shape[0]):
-        a, b = pairs[h, 0], pairs[h, 1]
+        a, b = pairs[0, h], pairs[1, h]
         delta = x8[a] - x8[b]
         delta = jnp.where(h < live_count, delta, 0.0)
         coarse = delta.astype(jnp.bfloat16).astype(F32)
@@ -268,11 +272,11 @@
     )
     own[...] = corr[lax.axis_index("gx")]
 
-    contact_products(pairs, live[0], x8, y8, hessian)
+    contact_products(pairs, live[0, live.shape[1] - 1], x8, y8, hessian)
     line = line_of([contact_dot(x8, y8)], width)
     for p in range(x8.shape[0]):
         x8[p] = f8[p] + y8[p]
-    contact_products(pairs, live[0], x8, z8, hessian)
+    contact_products(pairs, live[0, live.shape[1] - 1], x8, z8, hessian)
     sub = iota((8, width), 0)
     for d in range(peers):
         tile = jnp.where(sub == SUMS_TWO, wide(line), 0.0)
@@ -428,7 +432,7 @@
         dot = d2 * dd2[e] if dot is None else dot + d2 * dd2[e]
     rr2, dad2 = total(sq), total(dot)
 
-    contact_products(pairs, live[0], x8, y8, hessian)
+    contact_products(pairs, live[0, live.shape[1] - 1], x8, y8, hessian)
     line = line_of([rr2, dad2 + contact_dot(x8, y8)], width)
     for d in range(peers):
         for c in range(CAP):
@@ -446,7 +450,7 @@
 
 
 def call(kernel, spaces, outs, scratch=(), mebibytes=16, name=None):
-    kinds = {"s": pltpu.SMEM, "v": pltpu.VMEM}
+    kinds = {"s": pltpu.SMEM, "v": pltpu.VMEM, "a": pl.ANY}
     return pl.pallas_call(
         kernel,
         out_shape=tuple(jax.ShapeDtypeStruct(shape, kind) for shape, kind in outs),
@@ -471,16 +475,20 @@
     tiles, wide_tiles, rims = (peers * CAP, 8, width), (peers, 16, 4 * block_len), (peers, 8, width)
     line = ((1, 128), F32)
 
+    routes = jnp.concatenate([send_list, counts.reshape(1, 1)], axis=1)
+    pair_refs = pair_refs.T
+
     def swap(message):
         return lax.all_to_all(message, "gx", split_axis=0, concat_axis=0, tiled=True)
 
+    (token,) = call(announce_kernel, "a", [line], [], 56, name="announce")(hessian)
     sent1, loc = call(
         start_kernel,
-        "svvv",
+        "asvvv",
         [full, field],
         [panels, panels, (8, 4 * block_len), rims],
         name="start",
-    )(send_list, right_side, masses, stiffness)
+    )(token, routes, right_side, masses, stiffness)
     got1 = swap(sent1)
     sent2, held, own, known1 = call(
         owner_kernel,
@@ -489,7 +497,7 @@
         [tiles, tiles, tiles, tiles, wide_tiles, rims],
         32,
         name="owner",
-    )(pair_refs, counts, got1, hessian)
+    )(pair_refs, routes, got1, hessian)
     got2 = swap(sent2)
     sent3, v1, v2, known = call(
         middle_kernel,
@@ -497,7 +505,7 @@
         [full, field, field, line],
         [panels, panels, panels, (2, 8, width), (peers, 16, block_len)],
         name="middle",
-    )(send_list, got2, own, known1, right_side, loc, masses, stiffness)
+    )(routes, got2, own, known1, right_side, loc, masses, stiffness)
     got3 = swap(sent3)
     sent4, part, r2, d2, dd2 = call(
         last_kernel,
@@ -507,12 +515,12 @@
         32,
         name="last",
     )(
-        pair_refs, counts, got1, got3, held, sent2, known, right_side, v1, v2, masses, stiffness,
+        pair_refs, routes, got1, got3, held, sent2, known, right_side, v1, v2, masses, stiffness,
         hessian,
     )
     got4 = swap(sent4)
     return call(finish_kernel, "svvvvv", [field, field], [panels], name="finish")(
-        send_list, got4, part, r2, d2, dd2
+        routes, got4, part, r2, d2, dd2
     )
 
 

time: 76.2 us -> 72.9 us (0.957)
  blocking collectives: 34.6 us -> 51.8 us
  waiting for transfers between devices: 8.62 us -> 0 us
  starting transfers between devices: 7.39 us -> 0 us
  local copies, waits for them, and re-layouts: 8.31 us -> 4.69 us
  Pallas kernels: 15.5 us -> 14.6 us
    all_to_all x3 -> x4, blocking collectives: 34.6 us -> 51.8 us  [swap(): lax.all_to_all(message, 'gx', split_axis=0, concat_axis=0, tiled=True)]
    all_to_all x1 -> x0, waiting for transfers between devices: 8.62 us -> none  [swap(): lax.all_to_all(message, 'gx', split_axis=0, concat_axis=0, tiled=True)]
    all_to_all x1 -> x0, starting transfers between devices: 7.39 us -> none  [swap(): lax.all_to_all(message, 'gx', split_axis=0, concat_axis=0, tiled=True)]
    unnamed x21 -> x14, local copies, waits for them, and re-layouts: 8.31 us -> 4.69 us
    pallas_call x1 -> x2, Pallas kernels: 2.07 us -> 1.87 us  [the longest x1 1.35 us: per_device(): call(start_kernel, 'asvvv', [full, field], [panels, panels, (8, 4 * block...]
  transfers between devices with their start and end apart: 1 -> 0, of which waited for: 1 -> 0; matrix products, arithmetic and copies ran while one was open for 1% -> 0% of each run, Pallas kernels for 0% -> 0%
where the time goes in v5:
time: 72.9 us; the launch traced here: 72.6 us
  blocking collectives  51.8 us (71%)
  Pallas kernels  14.6 us (20%)
  local copies, waits for them, and re-layouts  4.69 us (6%)
  between operations  1.41 us (2%)
    all_to_all x4, blocking collectives, swap(): lax.all_to_all(message, 'gx', split_axis=0, concat_axis=0, tiled=True)  51.8 us
    pallas_call x1, Pallas kernels, per_device(): call(owner_kernel, 'ssvv', [two, two, ((8, width), F32), line], [tiles, t...  4.76 us
    unnamed x14, local copies, waits for them, and re-layouts  4.69 us
    pallas_call x1, Pallas kernels, per_device(): call(last_kernel, 'ssvvvvvvvvvvv', [one, field, field, field, field], [ti...  4.26 us
    pallas_call x1, Pallas kernels, per_device(): call(middle_kernel, 'svvvvvvv', [full, field, field, line], [panels, pane...  1.89 us
    pallas_call x1, Pallas kernels, per_device(): call(finish_kernel, 'svvvvv', [field, field], [panels], name='finish')  1.83 us

profile of v5, /device:TPU:0, one launch (start us, length us, event | category | flops | bytes accessed | tf_op | source)
XLA Modules:
  0.0 72.6 jit_solution(12784770358698632089)
XLA Ops:
  0.6 0.0 copy-start.6
  0.6 0.0 copy-start.2
  0.7 0.0 copy-start.3
  0.7 0.0 copy-start.1
  0.7 0.0 copy-start.4
  1.4 0.5 announce.1._
  1.9 0.0 copy-done.6
  1.9 0.1 pad_add_fusion.send.live
  2.0 0.0 copy-done.2
  2.0 0.0 copy-done.3
  2.0 0.0 copy-done.1
  2.0 0.0 copy-start.5
  2.0 0.7 copy-done.5
  2.7 1.4 %start.1 = (bf16[16,16,512]{2,1,0:T(8,128)(2,1)S(1)}, f32[3,64,512]{2,1,0:T(8,128)S(1)}) custom-call(f32[1,128]{1,0:T(1,128)S(1)} %copy-done.5, s32[1,49]{1,0:T(1,128)S(1)} %pad_add_fusion.send.live, f32[3,64,512]{2,1,0:T(8,128)S(1)} %copy-done.1, f32[64,512]{1,0:T(8,128)S(1)} %copy-done.3, f32[2,64,512]{2,1,0:T(8,128)S(1)} %copy-done.2), custom_call_target="tpu_custom_call" | custom-call | tf_op jit(solution)/shard_map/start/pallas_call | solution.py:485
  4.0 17.2 %all_to_all.20.got.got1 = bf16[16,16,512]{2,1,0:T(8,128)(2,1)S(1)} all-to-all(bf16[16,16,512]{2,1,0:T(8,128)(2,1)S(1)} %get-tuple-element.17), channel_id=1, replica_groups=mesh['groups'=2,'gx'=16] {'gx'}, dimensions={0} | all-to-all | bytes 524288 | tf_op jit(solution)/shard_map/all_to_all | solution.py:482
  21.2 0.0 copy-done.4
  21.2 0.0 copy-start
  21.2 4.0 %copy-done = bf16[36,384,384]{2,1,0:T(8,128)(2,1)S(1)} copy-done((bf16[36,384,384]{2,1,0:T(8,128)(2,1)S(1)}, bf16[36,384,384]{2,1,0:T(8,128)(2,1)}, u32[]{:S(2)}) %copy-start) | copy-done | bytes 10616856
  25.3 4.8 %owner.1 = (f32[16,8,384]{2,1,0:T(8,128)S(1)}, f32[16,8,384]{2,1,0:T(8,128)S(1)}, f32[8,384]{1,0:T(8,128)S(1)}, f32[1,128]{1,0:T(1,128)S(1)}) custom-call(s32[2,36]{1,0:T(2,128)S(1)} %bitcast.3, s32[1,49]{1,0:T(1,128)S(1)} %pad_add_fusion.send.live, bf16[16,16,512]{2,1,0:T(8,128)(2,1)S(1)} %all_to_all.20.got.got1, bf16[36,384,384]{2,1,0:T(8,128)(2,1)S(1)} %copy-done), custom_call_target="tpu_custom_call" | custom-call | tf_op jit(solution)/shard_map/owner/pallas_call | solution.py:493
  30.0 11.8 %all_to_all.21.got2 = f32[16,8,384]{2,1,0:T(8,128)S(1)} all-to-all(f32[16,8,384]{2,1,0:T(8,128)S(1)} %get-tuple-element.18.sent2), channel_id=1, replica_groups=mesh['groups'=2,'gx'=16] {'gx'}, dimensions={0} | all-to-all | bytes 393216 | tf_op jit(solution)/shard_map/all_to_all | solution.py:482
  41.8 1.9 %middle.1 = (bf16[16,16,512]{2,1,0:T(8,128)(2,1)S(1)}, f32[3,64,512]{2,1,0:T(8,128)S(1)}, f32[3,64,512]{2,1,0:T(8,128)S(1)}, f32[1,128]{1,0:T(1,128)S(1)}) custom-call(s32[1,49]{1,0:T(1,128)S(1)} %pad_add_fusion.send.live, f32[16,8,384]{2,1,0:T(8,128)S(1)} %all_to_all.21.got2, f32[8,384]{1,0:T(8,128)S(1)} %get-tuple-element.19.own, ...), custom_call_target="tpu_custom_call" | custom-call | tf_op jit(solution)/shard_map/middle/pallas_call | solution.py:502
  43.7 12.6 %all_to_all.22.got3 = bf16[16,16,512]{2,1,0:T(8,128)(2,1)S(1)} all-to-all(bf16[16,16,512]{2,1,0:T(8,128)(2,1)S(1)} %get-tuple-element.22), channel_id=1, replica_groups=mesh['groups'=2,'gx'=16] {'gx'}, dimensions={0} | all-to-all | bytes 524288 | tf_op jit(solution)/shard_map/all_to_all | solution.py:482
  56.3 4.3 %last.1 = (f32[16,4,384]{2,1,0:T(4,128)S(1)}, f32[3,64,512]{2,1,0:T(8,128)S(1)}, f32[3,64,512]{2,1,0:T(8,128)S(1)}, f32[3,64,512]{2,1,0:T(8,128)S(1)}, f32[3,64,512]{2,1,0:T(8,128)S(1)}) custom-call(s32[2,36]{1,0:T(2,128)S(1)} %bitcast.4, s32[1,49]{1,0:T(1,128)S(1)} %pad_add_fusion.send.live, bf16[16,16,512]{2,1,0:T(8,128)(2,1)S(1)} %all_to_all.20.got.got1, ...), custom_call_target="tpu_custom_call" | custom-call | tf_op jit(solution)/shard_map/last/pallas_call | solution.py:510
  60.6 10.2 %all_to_all.23.got4 = f32[16,4,384]{2,1,0:T(4,128)S(1)} all-to-all(f32[16,4,384]{2,1,0:T(4,128)S(1)} %get-tuple-element.27), channel_id=1, replica_groups=mesh['groups'=2,'gx'=16] {'gx'}, dimensions={0} | all-to-all | bytes 196608 | tf_op jit(solution)/shard_map/all_to_all | solution.py:482
  70.8 1.8 %finish.1 = (f32[3,64,512]{2,1,0:T(8,128)}, f32[3,64,512]{2,1,0:T(8,128)}) custom-call(s32[1,49]{1,0:T(1,128)S(1)} %pad_add_fusion.send.live, f32[16,4,384]{2,1,0:T(4,128)S(1)} %all_to_all.23.got4, f32[3,64,512]{2,1,0:T(8,128)S(1)} %get-tuple-element.28.part, f32[3,64,512]{2,1,0:T(8,128)S(1)} %get-tuple-element.29.r2, ...), custom_call_target="tpu_custom_call" | custom-call | tf_op jit(solution)/shard_map/finish/pallas_call | solution.py:522
Async XLA Ops:
  0.6 1.3 %copy-start.6 = (s32[1,48]{1,0:T(1,128)S(1)}, s32[1,48]{1,0:T(1,128)}, u32[]{:S(2)}) copy-start(s32[1,48]{1,0:T(1,128)} %param.11) | copy-start | bytes 580
  0.6 1.3 %copy-start.2 = (f32[2,64,512]{2,1,0:T(8,128)S(1)}, f32[2,64,512]{2,1,0:T(8,128)}, u32[]{:S(2)}) copy-start(f32[2,64,512]{2,1,0:T(8,128)} %stiff.5) | copy-start | bytes 786436
  0.7 1.3 %copy-start.3 = (f32[64,512]{1,0:T(8,128)S(1)}, f32[64,512]{1,0:T(8,128)}, u32[]{:S(2)}) copy-start(f32[64,512]{1,0:T(8,128)} %mass.5) | copy-start | bytes 393220
  0.7 1.3 %copy-start.1 = (f32[3,64,512]{2,1,0:T(8,128)S(1)}, f32[3,64,512]{2,1,0:T(8,128)}, u32[]{:S(2)}) copy-start(f32[3,64,512]{2,1,0:T(8,128)} %b.5) | copy-start | bytes 1179652
  0.7 20.6 %copy-start.4 = (s32[36,2]{0,1:T(2,128)S(1)}, s32[36,2]{0,1:T(2,128)}, u32[]{:S(2)}) copy-start(s32[36,2]{0,1:T(2,128)} %param.12) | copy-start | bytes 868
  2.0 0.7 copy-start.5
  21.2 4.0 %copy-start = (bf16[36,384,384]{2,1,0:T(8,128)(2,1)S(1)}, bf16[36,384,384]{2,1,0:T(8,128)(2,1)}, u32[]{:S(2)}) copy-start(bf16[36,384,384]{2,1,0:T(8,128)(2,1)} %hessian.5) | copy-start | bytes 31850500

commit v6 on v5

--- a/solution.py
+++ b/solution.py
@@ -148,9 +148,20 @@
     return jnp.maximum(d - 1, 0), jnp.minimum(d + 1, peers - 1)
 
 
-def rim_coefs(tiles, d):
-    before, _ = around(d, tiles.shape[0])
-    here, other = tiles[d, 0:8, 384:512], tiles[before, 0:8, 384:512]
+def unpack_first(got, tiles, edges):
+    sub = iota(edges.shape[1:], 0)
+    for d in range(got.shape[0]):
+        tile = got[d].astype(F32)
+        tiles[d] = tile
+        kx = jnp.where(sub % 4 == 3, wide(tile[15:16, 0:128]), 0.0)
+        for q in range(3):
+            kx = jnp.where(sub % 4 == q, wide(tile[14:15, q * 128 : (q + 1) * 128]), kx)
+        edges[d] = kx
+
+
+def rim_coefs(edges, d):
+    before, _ = around(d, edges.shape[0])
+    here, other = edges[d], edges[before]
     other = jnp.where(d > 0, other, 0.0)
     return thrice(jnp.where(iota(here.shape, 0) < 4, other, here))
 
@@ -180,14 +191,9 @@
         dot = v * image if dot is None else dot + v * image
     write_rim(rim, b)
     ends = lax.axis_index("gx") == peers - 1
-    for q in range(col_blocks):
-        kx = stiff[0, rows - 1 : rows, q * block_len : (q + 1) * block_len]
-        kx = jnp.where(ends, 0.0, kx)
-        rim[q : q + 1, 3 * block_len :] = kx
-        rim[col_blocks + q : col_blocks + q + 1, 3 * block_len :] = kx
+    kx = jnp.where(ends, 0.0, stiff[0, rows - 1 : rows, :])
     line = packed_line([total(sq), total(dot)])
     lanes, sub = iota((1, 128), 1), iota((8, 3 * block_len), 0)
-    sub_one = iota((8, block_len), 0)
 
     def one(d, carry):
         own_line = line
@@ -199,14 +205,9 @@
                 span = slice(e * block_len, (e + 1) * block_len)
                 stage[d, c : c + 1, span] = b_panels[e, col, pl.ds(row, 1), :]
                 stage[d, CAP + c : CAP + c + 1, span] = loc_panels[e, col, pl.ds(row, 1), :]
-        body = stage[d]
-        rest = pltpu.roll(body - rounded(body), 3, 0)
-        body = jnp.where(sub >= 2 * CAP, rest, body)
-        extra = jnp.where(sub_one == 4, wide(own_line), 0.0)
-        for j in range(3):
-            piece = rest[0:1, j * block_len : (j + 1) * block_len]
-            extra = jnp.where(sub_one == j, wide(piece), extra)
-        lower = jnp.concatenate([body, extra], axis=1)
+        tail = jnp.concatenate([kx[:, 3 * block_len :], own_line, jnp.zeros_like(own_line)], axis=1)
+        lower = jnp.where(sub == 2 * CAP, wide(kx[:, : 3 * block_len]), stage[d])
+        lower = jnp.where(sub == 2 * CAP + 1, wide(tail), lower)
         message[d] = jnp.concatenate([rim[...], lower], axis=0).astype(BF16)
         return carry
 
@@ -239,13 +240,12 @@
 
 
 def owner_kernel(
-    pairs, live, got, hessian, message, held, own, known, x8, y8, z8, f8, tiles, corr
+    pairs, live, got, hessian, message, held, own, known, x8, y8, z8, f8, tiles, corr, edges
 ):
     peers, _, _ = got.shape
     width = x8.shape[2]
     block_len = width // 3
-    for d in range(peers):
-        tiles[d] = got[d].astype(F32)
+    unpack_first(got, tiles, edges)
 
     def one(d, carry):
         energy, sums = carry
@@ -253,16 +253,13 @@
         diff = tiles[d, 0:8, 0:width] - across(
             tiles[before, 0:8, 0:width], tiles[after, 0:8, 0:width]
         )
-        fix = rim_coefs(tiles, d) * diff
+        fix = rim_coefs(edges, d) * diff
         corr[d] = fix
-        body, extra = tiles[d, 8:16, 0:width], tiles[d, 8:16, width:]
-        line = extra[4:5, :]
-        rest = [body[6:7], body[7:8], jnp.concatenate([extra[j : j + 1] for j in range(3)], axis=1)]
+        body, line = tiles[d, 8:16, 0:width], tiles[d, 15:16, block_len : 2 * block_len]
         for c in range(CAP):
             p = d * CAP + c
             x8[p] = wide(body[c : c + 1])
-            value = body[CAP + c : CAP + c + 1] + rest[c]
-            f8[p] = wide(value + chosen(pick(line, CODE_LANE + c), fix))
+            f8[p] = wide(body[CAP + c : CAP + c + 1] + chosen(pick(line, CODE_LANE + c), fix))
         return energy + fix * diff, sums + line
 
     zero = jnp.zeros((8, width), F32)
@@ -273,9 +270,10 @@
     own[...] = corr[lax.axis_index("gx")]
 
     contact_products(pairs, live[0, live.shape[1] - 1], x8, y8, hessian)
-    line = line_of([contact_dot(x8, y8)], width)
+    line = packed_line([contact_dot(x8, y8)])
+    line = jnp.concatenate([line, jnp.zeros((1, width - block_len), F32)], axis=1)
     for p in range(x8.shape[0]):
-        x8[p] = f8[p] + y8[p]
+        x8[p] = f8[p] + rounded(y8[p])
     contact_products(pairs, live[0, live.shape[1] - 1], x8, z8, hessian)
     sub = iota((8, width), 0)
     for d in range(peers):
@@ -285,19 +283,21 @@
             tile = jnp.where(sub == c, y8[d * CAP + c], tile)
             tile = jnp.where(sub == CAP + c, z8[d * CAP + c], tile)
             kept = jnp.where(sub == CAP + c, x8[d * CAP + c], kept)
-        message[d] = tile
+        message[d] = tile.astype(BF16)
         held[d] = kept
 
 
 def middle_kernel(
-    send, got2, own, known1, b, loc, mass, stiff, message, v1, v2, known, cb, cv1, panels, common, stage
+    send, got2, own, known1, b, loc, mass, stiff, message, v1, v2, known, cb, cv1, panels, common, stage, back
 ):
     rows, peers = b.shape[1], message.shape[0]
     col_blocks, block_len = panels.shape[1], panels.shape[3]
-    scatter_blocks(send, got2, [cb, cv1])
+    for d in range(peers):
+        back[d] = got2[d].astype(F32)
+    scatter_blocks(send, back, [cb, cv1])
     ky = masked_ky(stiff)
     rr0 = pick(known1[...], 0)
-    alpha0 = rr0 / (pick(known1[...], 1) + pick(line_sum(got2, SUMS_TWO), 0))
+    alpha0 = rr0 / (pick(known1[...], 1) + pick_packed(line_sum(back, SUMS_TWO), 0))
     known[...] = line_of([rr0, alpha0], known.shape[1])
     sums = None
     for e in range(3):
@@ -357,19 +357,19 @@
 
 def last_kernel(
     pairs, live, got1, got3, held, sent2, known, b, v1, v2, mass, stiff, hessian,
-    message, part, r2_out, d2_out, dd2, x8, y8, tiles1, tiles3, corr, rim,
+    message, part, r2_out, d2_out, dd2, x8, y8, tiles1, tiles3, corr, rim, edges,
 ):
     peers = got1.shape[0]
     width = x8.shape[2]
     rows = b.shape[1]
+    unpack_first(got1, tiles1, edges)
     for d in range(peers):
-        tiles1[d] = got1[d].astype(F32)
         tiles3[d] = got3[d].astype(F32)
 
     def one(d, carry):
         before, after = around(d, peers)
         first = tiles3[d, 0:8, 0:width]
-        fix = rim_coefs(tiles1, d) * (
+        fix = rim_coefs(edges, d) * (
             first - across(tiles3[before, 0:8, 0:width], tiles3[after, 0:8, 0:width])
         )
         corr[d] = fix
@@ -386,9 +386,9 @@
     coefs = coefficients(known[...], sums, *[total(value) for value in crossing])
 
     def two(d, carry):
-        extra, line = tiles3[d, 0:16, width:], tiles1[d, 12:13, width:]
+        extra, line = tiles3[d, 0:16, width:], tiles1[d, 15:16, 128:256]
         fix = corr[d]
-        kept, sent = held[d], sent2[d]
+        kept, sent = held[d], sent2[d].astype(F32)
         for c in range(CAP):
             value = jnp.concatenate([extra[c * 3 + e : c * 3 + e + 1] for e in range(3)], axis=1)
             value = value + chosen(pick(line, CODE_LANE + c), fix) + sent[CAP + c : CAP + c + 1]
@@ -421,7 +421,7 @@
             coefs,
         )[2]
 
-    fix = rim_coefs(tiles1, me) * (rim[...] - across(rim_direction(before), rim_direction(after)))
+    fix = rim_coefs(edges, me) * (rim[...] - across(rim_direction(before), rim_direction(after)))
     sq = dot = None
     for e in range(3):
         r2, d2 = r2_out[e], d2_out[e]
@@ -433,17 +433,19 @@
     rr2, dad2 = total(sq), total(dot)
 
     contact_products(pairs, live[0, live.shape[1] - 1], x8, y8, hessian)
-    line = line_of([rr2, dad2 + contact_dot(x8, y8)], width)
+    line = packed_line([rr2, dad2 + contact_dot(x8, y8)])
+    line = jnp.concatenate([line, jnp.zeros((1, width - 128), F32)], axis=1)
     for d in range(peers):
-        for c in range(CAP):
-            message[d, c : c + 1, :] = y8[d * CAP + c, 0:1, :]
-    put_line(message, SUMS_ONE, line)
-
-
-def finish_kernel(send, got4, part, r2, d2, dd2, solution, residual, cd2):
-    scatter_blocks(send, got4, [cd2])
-    sums = line_sum(got4, SUMS_ONE)
-    alpha2 = pick(sums, 0) / pick(sums, 1)
+        rows = [y8[d * CAP + c, 0:1, :] for c in range(CAP)]
+        message[d] = jnp.concatenate([*rows, line], axis=0).astype(BF16)
+
+
+def finish_kernel(send, got4, part, r2, d2, dd2, solution, residual, cd2, back):
+    for d in range(got4.shape[0]):
+        back[d] = got4[d].astype(F32)
+    scatter_blocks(send, back, [cd2])
+    sums = line_sum(back, SUMS_ONE)
+    alpha2 = pick_packed(sums, 0) / pick_packed(sums, 1)
     for e in range(3):
         solution[e] = part[e] + alpha2 * d2[e]
         residual[e] = r2[e] - alpha2 * (dd2[e] + from_panels(cd2, e))
@@ -469,8 +471,9 @@
     peers = lax.axis_size("gx")
     assert send_list.shape[1] == peers * CAP and col_count == 4 * block_len and block_len == 128
     field = (right_side.shape, F32)
-    two, one = ((peers, 8, width), F32), ((peers, 4, width), F32)
-    full = ((peers, 16, 4 * block_len), BF16)
+    first, second = ((peers, 16, width), BF16), ((peers, 8, width), BF16)
+    third, fourth = ((peers, 16, 4 * block_len), BF16), ((peers, 4, width), BF16)
+    held_shape, edges = ((peers, 8, width), F32), (peers, 8, block_len)
     panels = (3, 4, row_count, block_len)
     tiles, wide_tiles, rims = (peers * CAP, 8, width), (peers, 16, 4 * block_len), (peers, 8, width)
     line = ((1, 128), F32)
@@ -485,16 +488,16 @@
     sent1, loc = call(
         start_kernel,
         "asvvv",
-        [full, field],
-        [panels, panels, (8, 4 * block_len), rims],
+        [first, field],
+        [panels, panels, (8, width), rims],
         name="start",
     )(token, routes, right_side, masses, stiffness)
     got1 = swap(sent1)
     sent2, held, own, known1 = call(
         owner_kernel,
         "ssvv",
-        [two, two, ((8, width), F32), line],
-        [tiles, tiles, tiles, tiles, wide_tiles, rims],
+        [second, held_shape, ((8, width), F32), line],
+        [tiles, tiles, tiles, tiles, (peers, 16, width), rims, edges],
         32,
         name="owner",
     )(pair_refs, routes, got1, hessian)
@@ -502,16 +505,16 @@
     sent3, v1, v2, known = call(
         middle_kernel,
         "svvvvvvv",
-        [full, field, field, line],
-        [panels, panels, panels, (2, 8, width), (peers, 16, block_len)],
+        [third, field, field, line],
+        [panels, panels, panels, (2, 8, width), (peers, 16, block_len), rims],
         name="middle",
     )(routes, got2, own, known1, right_side, loc, masses, stiffness)
     got3 = swap(sent3)
     sent4, part, r2, d2, dd2 = call(
         last_kernel,
         "ssvvvvvvvvvvv",
-        [one, field, field, field, field],
-        [tiles, tiles, wide_tiles, wide_tiles, rims, (8, width)],
+        [fourth, field, field, field, field],
+        [tiles, tiles, (peers, 16, width), wide_tiles, rims, (8, width), edges],
         32,
         name="last",
     )(
@@ -519,7 +522,7 @@
         hessian,
     )
     got4 = swap(sent4)
-    return call(finish_kernel, "svvvvv", [field, field], [panels], name="finish")(
+    return call(finish_kernel, "svvvvv", [field, field], [panels, (peers, 4, width)], name="finish")(
         routes, got4, part, r2, d2, dd2
     )
 

time: 72.9 us -> 69.5 us (0.953)
  blocking collectives: 51.8 us -> 48.4 us
    all_to_all x4, blocking collectives: 51.8 us -> 48.4 us  [swap(): lax.all_to_all(message, 'gx', split_axis=0, concat_axis=0, tiled=True)]
where the time goes in v6:
time: 69.5 us; the launch traced here: 69.2 us
  blocking collectives  48.4 us (70%)
  Pallas kernels  14.6 us (21%)
  local copies, waits for them, and re-layouts  4.69 us (7%)
  between operations  1.42 us (2%)
    all_to_all x4, blocking collectives, swap(): lax.all_to_all(message, 'gx', split_axis=0, concat_axis=0, tiled=True)  48.4 us
    unnamed x14, local copies, waits for them, and re-layouts  4.69 us
    pallas_call x1, Pallas kernels, per_device(): call(owner_kernel, 'ssvv', [second, held_shape, ((8, width), F32), line],...  4.63 us
    pallas_call x1, Pallas kernels, per_device(): call(last_kernel, 'ssvvvvvvvvvvv', [fourth, field, field, field, field],...  4.24 us
    pallas_call x1, Pallas kernels, per_device(): call(middle_kernel, 'svvvvvvv', [third, field, field, line], [panels, pan...  1.98 us
    pallas_call x1, Pallas kernels, per_device(): call(finish_kernel, 'svvvvv', [field, field], [panels, (peers, 4, width)]...  1.93 us

profile of v6, /device:TPU:0, one launch (start us, length us, event | category | flops | bytes accessed | tf_op | source)
XLA Modules:
  0.0 69.2 jit_solution(12376936898210477169)
XLA Ops:
  0.6 0.0 copy-start.6
  0.6 0.0 copy-start.2
  0.7 0.0 copy-start.3
  0.7 0.0 copy-start.1
  0.7 0.0 copy-start.4
  1.4 0.5 announce.1._
  1.9 0.0 copy-done.6
  1.9 0.1 pad_add_fusion.send.live
  2.0 0.0 copy-done.2
  2.0 0.0 copy-done.3
  2.0 0.0 copy-done.1
  2.0 0.0 copy-start.5
  2.0 0.7 copy-done.5
  2.7 1.3 %start.1 = (bf16[16,16,384]{2,1,0:T(8,128)(2,1)S(1)}, f32[3,64,512]{2,1,0:T(8,128)S(1)}) custom-call(f32[1,128]{1,0:T(1,128)S(1)} %copy-done.5, s32[1,49]{1,0:T(1,128)S(1)} %pad_add_fusion.send.live, f32[3,64,512]{2,1,0:T(8,128)S(1)} %copy-done.1, f32[64,512]{1,0:T(8,128)S(1)} %copy-done.3, f32[2,64,512]{2,1,0:T(8,128)S(1)} %copy-done.2), custom_call_target="tpu_custom_call" | custom-call | tf_op jit(solution)/shard_map/start/pallas_call | solution.py:488
  4.0 16.2 %all_to_all.20.got.got1 = bf16[16,16,384]{2,1,0:T(8,128)(2,1)S(1)} all-to-all(bf16[16,16,384]{2,1,0:T(8,128)(2,1)S(1)} %get-tuple-element.17), channel_id=1, replica_groups=mesh['groups'=2,'gx'=16] {'gx'}, dimensions={0} | all-to-all | bytes 393216 | tf_op jit(solution)/shard_map/all_to_all | solution.py:485
  20.2 0.0 copy-done.4
  20.2 0.0 copy-start
  20.2 4.0 %copy-done = bf16[36,384,384]{2,1,0:T(8,128)(2,1)S(1)} copy-done((bf16[36,384,384]{2,1,0:T(8,128)(2,1)S(1)}, bf16[36,384,384]{2,1,0:T(8,128)(2,1)}, u32[]{:S(2)}) %copy-start) | copy-done | bytes 10616856
  24.2 4.6 %owner.1 = (bf16[16,8,384]{2,1,0:T(8,128)(2,1)S(1)}, f32[16,8,384]{2,1,0:T(8,128)S(1)}, f32[8,384]{1,0:T(8,128)S(1)}, f32[1,128]{1,0:T(1,128)S(1)}) custom-call(s32[2,36]{1,0:T(2,128)S(1)} %bitcast.3, s32[1,49]{1,0:T(1,128)S(1)} %pad_add_fusion.send.live, bf16[16,16,384]{2,1,0:T(8,128)(2,1)S(1)} %all_to_all.20.got.got1, bf16[36,384,384]{2,1,0:T(8,128)(2,1)S(1)} %copy-done), custom_call_target="tpu_custom_call" | custom-call | tf_op jit(solution)/shard_map/owner/pallas_call | solution.py:496
  28.8 10.0 %all_to_all.21.got2 = bf16[16,8,384]{2,1,0:T(8,128)(2,1)S(1)} all-to-all(bf16[16,8,384]{2,1,0:T(8,128)(2,1)S(1)} %get-tuple-element.18.sent2), channel_id=1, replica_groups=mesh['groups'=2,'gx'=16] {'gx'}, dimensions={0} | all-to-all | bytes 196608 | tf_op jit(solution)/shard_map/all_to_all | solution.py:485
  38.8 2.0 %middle.1 = (bf16[16,16,512]{2,1,0:T(8,128)(2,1)S(1)}, f32[3,64,512]{2,1,0:T(8,128)S(1)}, f32[3,64,512]{2,1,0:T(8,128)S(1)}, f32[1,128]{1,0:T(1,128)S(1)}) custom-call(s32[1,49]{1,0:T(1,128)S(1)} %pad_add_fusion.send.live, bf16[16,8,384]{2,1,0:T(8,128)(2,1)S(1)} %all_to_all.21.got2, f32[8,384]{1,0:T(8,128)S(1)} %get-tuple-element.19.own, ...), custom_call_target="tpu_custom_call" | custom-call | tf_op jit(solution)/shard_map/middle/pallas_call | solution.py:505
  40.8 12.6 %all_to_all.22.got3 = bf16[16,16,512]{2,1,0:T(8,128)(2,1)S(1)} all-to-all(bf16[16,16,512]{2,1,0:T(8,128)(2,1)S(1)} %get-tuple-element.22), channel_id=1, replica_groups=mesh['groups'=2,'gx'=16] {'gx'}, dimensions={0} | all-to-all | bytes 524288 | tf_op jit(solution)/shard_map/all_to_all | solution.py:485
  53.5 4.2 %last.1 = (bf16[16,4,384]{2,1,0:T(4,128)(2,1)S(1)}, f32[3,64,512]{2,1,0:T(8,128)S(1)}, f32[3,64,512]{2,1,0:T(8,128)S(1)}, f32[3,64,512]{2,1,0:T(8,128)S(1)}, f32[3,64,512]{2,1,0:T(8,128)S(1)}) custom-call(s32[2,36]{1,0:T(2,128)S(1)} %bitcast.4, s32[1,49]{1,0:T(1,128)S(1)} %pad_add_fusion.send.live, bf16[16,16,384]{2,1,0:T(8,128)(2,1)S(1)} %all_to_all.20.got.got1, ...), custom_call_target="tpu_custom_call" | custom-call | tf_op jit(solution)/shard_map/last/pallas_call | solution.py:513
  57.7 9.5 %all_to_all.23.got4 = bf16[16,4,384]{2,1,0:T(4,128)(2,1)S(1)} all-to-all(bf16[16,4,384]{2,1,0:T(4,128)(2,1)S(1)} %get-tuple-element.27), channel_id=1, replica_groups=mesh['groups'=2,'gx'=16] {'gx'}, dimensions={0} | all-to-all | bytes 98304 | tf_op jit(solution)/shard_map/all_to_all | solution.py:485
  67.2 1.9 %finish.1 = (f32[3,64,512]{2,1,0:T(8,128)}, f32[3,64,512]{2,1,0:T(8,128)}) custom-call(s32[1,49]{1,0:T(1,128)S(1)} %pad_add_fusion.send.live, bf16[16,4,384]{2,1,0:T(4,128)(2,1)S(1)} %all_to_all.23.got4, f32[3,64,512]{2,1,0:T(8,128)S(1)} %get-tuple-element.28.part, f32[3,64,512]{2,1,0:T(8,128)S(1)} %get-tuple-element.29.r2, ...), custom_call_target="tpu_custom_call" | custom-call | tf_op jit(solution)/shard_map/finish/pallas_call | solution.py:525
Async XLA Ops:
  0.6 1.3 %copy-start.6 = (s32[1,48]{1,0:T(1,128)S(1)}, s32[1,48]{1,0:T(1,128)}, u32[]{:S(2)}) copy-start(s32[1,48]{1,0:T(1,128)} %param.11) | copy-start | bytes 580
  0.6 1.3 %copy-start.2 = (f32[2,64,512]{2,1,0:T(8,128)S(1)}, f32[2,64,512]{2,1,0:T(8,128)}, u32[]{:S(2)}) copy-start(f32[2,64,512]{2,1,0:T(8,128)} %stiff.5) | copy-start | bytes 786436
  0.7 1.3 %copy-start.3 = (f32[64,512]{1,0:T(8,128)S(1)}, f32[64,512]{1,0:T(8,128)}, u32[]{:S(2)}) copy-start(f32[64,512]{1,0:T(8,128)} %mass.5) | copy-start | bytes 393220
  0.7 1.3 %copy-start.1 = (f32[3,64,512]{2,1,0:T(8,128)S(1)}, f32[3,64,512]{2,1,0:T(8,128)}, u32[]{:S(2)}) copy-start(f32[3,64,512]{2,1,0:T(8,128)} %b.5) | copy-start | bytes 1179652
  0.7 19.5 %copy-start.4 = (s32[36,2]{0,1:T(2,128)S(1)}, s32[36,2]{0,1:T(2,128)}, u32[]{:S(2)}) copy-start(s32[36,2]{0,1:T(2,128)} %param.12) | copy-start | bytes 868
  2.0 0.7 copy-start.5
  20.2 4.0 %copy-start = (bf16[36,384,384]{2,1,0:T(8,128)(2,1)S(1)}, bf16[36,384,384]{2,1,0:T(8,128)(2,1)}, u32[]{:S(2)}) copy-start(bf16[36,384,384]{2,1,0:T(8,128)(2,1)} %hessian.5) | copy-start | bytes 31850500

commit v7 on v6

--- a/solution.py
+++ b/solution.py
@@ -172,7 +172,7 @@
     )
 
 
-def announce_kernel(hessian, token):
+def announce_kernel(hessian, _, token):
     token[...] = jnp.zeros_like(token)
 
 
@@ -484,7 +484,9 @@
     def swap(message):
         return lax.all_to_all(message, "gx", split_axis=0, concat_axis=0, tiled=True)
 
-    (token,) = call(announce_kernel, "a", [line], [], 56, name="announce")(hessian)
+    token = jnp.zeros(line[0], F32)
+    for _ in range(2):
+        (token,) = call(announce_kernel, "aa", [line], [], 51, name="announce")(hessian, token)
     sent1, loc = call(
         start_kernel,
         "asvvv",

time: 69.5 us -> 65.5 us (0.942)
  local copies, waits for them, and re-layouts: 4.69 us -> 0.97 us
    unnamed x14 -> x16, local copies, waits for them, and re-layouts: 4.69 us -> 0.97 us
where the time goes in v7:
time: 65.5 us; the launch traced here: 65.3 us
  blocking collectives  48.6 us (74%)
  Pallas kernels  14.2 us (22%)
  between operations  1.41 us (2%)
  local copies, waits for them, and re-layouts  0.97 us (1%)
    all_to_all x4, blocking collectives, swap(): lax.all_to_all(message, 'gx', split_axis=0, concat_axis=0, tiled=True)  48.6 us
    pallas_call x1, Pallas kernels, per_device(): call(owner_kernel, 'ssvv', [second, held_shape, ((8, width), F32), line],...  4.67 us
    pallas_call x1, Pallas kernels, per_device(): call(last_kernel, 'ssvvvvvvvvvvv', [fourth, field, field, field, field],...  4.26 us
    pallas_call x1, Pallas kernels, per_device(): call(middle_kernel, 'svvvvvvv', [third, field, field, line], [panels, pan...  1.99 us
    pallas_call x1, Pallas kernels, per_device(): call(finish_kernel, 'svvvvv', [field, field], [panels, (peers, 4, width)]...  1.93 us
    pallas_call x1, Pallas kernels, per_device(): call(start_kernel, 'asvvv', [first, field], [panels, panels, (8, width),...  1.36 us

profile of v7, /device:TPU:0, one launch (start us, length us, event | category | flops | bytes accessed | tf_op | source)
XLA Modules:
  0.0 65.3 jit_solution(2699325828882245932)
XLA Ops:
  1.3 0.0 copy-start.4
  1.3 0.0 copy-start
  1.3 0.0 copy-start.1
  1.3 0.0 copy-start.2
  1.3 0.0 slice-start
  1.3 0.0 slice-start.1
  1.4 0.0 copy-start.3
  1.4 0.0 slice-start.2
  1.4 0.5 copy-done.4
  1.9 0.1 pad_add_fusion.send.live
  2.0 0.3 copy-done
  2.3 0.1 copy-done.1
  2.4 0.0 copy-done.2
  2.4 1.4 %start.1 = (bf16[16,16,384]{2,1,0:T(8,128)(2,1)S(1)}, f32[3,64,512]{2,1,0:T(8,128)S(1)}) custom-call(f32[1,128]{1,0:T(1,128)S(1)} %announce.3._, s32[1,49]{1,0:T(1,128)S(1)} %pad_add_fusion.send.live, f32[3,64,512]{2,1,0:T(8,128)S(1)} %copy-done, f32[64,512]{1,0:T(8,128)S(1)} %copy-done.2, f32[2,64,512]{2,1,0:T(8,128)S(1)} %copy-done.1), custom_call_target="tpu_custom_call" | custom-call | tf_op jit(solution)/shard_map/start/pallas_call | solution.py:490
  3.8 16.4 %all_to_all.20.got.got1 = bf16[16,16,384]{2,1,0:T(8,128)(2,1)S(1)} all-to-all(bf16[16,16,384]{2,1,0:T(8,128)(2,1)S(1)} %get-tuple-element.17), channel_id=1, replica_groups=mesh['groups'=2,'gx'=16] {'gx'}, dimensions={0} | all-to-all | bytes 393216 | tf_op jit(solution)/shard_map/all_to_all | solution.py:485
  20.2 0.0 slice-done
  20.2 0.0 slice-done.1
  20.2 0.0 copy-done.3
  20.2 0.0 slice-done.2
  20.2 4.7 %owner.1 = (bf16[16,8,384]{2,1,0:T(8,128)(2,1)S(1)}, f32[16,8,384]{2,1,0:T(8,128)S(1)}, f32[8,384]{1,0:T(8,128)S(1)}, f32[1,128]{1,0:T(1,128)S(1)}) custom-call(s32[2,36]{1,0:T(2,128)S(1)} %bitcast.5, s32[1,49]{1,0:T(1,128)S(1)} %pad_add_fusion.send.live, bf16[16,16,384]{2,1,0:T(8,128)(2,1)S(1)} %all_to_all.20.got.got1, bf16[36,384,384]{2,1,0:T(8,128)(2,1)S(1)} %bitcast.4), custom_call_target="tpu_custom_call" | custom-call | tf_op jit(solution)/shard_map/owner/pallas_call | solution.py:498
  24.9 10.0 %all_to_all.21.got2 = bf16[16,8,384]{2,1,0:T(8,128)(2,1)S(1)} all-to-all(bf16[16,8,384]{2,1,0:T(8,128)(2,1)S(1)} %get-tuple-element.18.sent2), channel_id=1, replica_groups=mesh['groups'=2,'gx'=16] {'gx'}, dimensions={0} | all-to-all | bytes 196608 | tf_op jit(solution)/shard_map/all_to_all | solution.py:485
  34.9 2.0 %middle.1 = (bf16[16,16,512]{2,1,0:T(8,128)(2,1)S(1)}, f32[3,64,512]{2,1,0:T(8,128)S(1)}, f32[3,64,512]{2,1,0:T(8,128)S(1)}, f32[1,128]{1,0:T(1,128)S(1)}) custom-call(s32[1,49]{1,0:T(1,128)S(1)} %pad_add_fusion.send.live, bf16[16,8,384]{2,1,0:T(8,128)(2,1)S(1)} %all_to_all.21.got2, f32[8,384]{1,0:T(8,128)S(1)} %get-tuple-element.19.own, ...), custom_call_target="tpu_custom_call" | custom-call | tf_op jit(solution)/shard_map/middle/pallas_call | solution.py:507
  36.9 12.6 %all_to_all.22.got3 = bf16[16,16,512]{2,1,0:T(8,128)(2,1)S(1)} all-to-all(bf16[16,16,512]{2,1,0:T(8,128)(2,1)S(1)} %get-tuple-element.22), channel_id=1, replica_groups=mesh['groups'=2,'gx'=16] {'gx'}, dimensions={0} | all-to-all | bytes 524288 | tf_op jit(solution)/shard_map/all_to_all | solution.py:485
  49.5 4.3 %last.1 = (bf16[16,4,384]{2,1,0:T(4,128)(2,1)S(1)}, f32[3,64,512]{2,1,0:T(8,128)S(1)}, f32[3,64,512]{2,1,0:T(8,128)S(1)}, f32[3,64,512]{2,1,0:T(8,128)S(1)}, f32[3,64,512]{2,1,0:T(8,128)S(1)}) custom-call(s32[2,36]{1,0:T(2,128)S(1)} %bitcast.6, s32[1,49]{1,0:T(1,128)S(1)} %pad_add_fusion.send.live, bf16[16,16,384]{2,1,0:T(8,128)(2,1)S(1)} %all_to_all.20.got.got1, ...), custom_call_target="tpu_custom_call" | custom-call | tf_op jit(solution)/shard_map/last/pallas_call | solution.py:515
  53.8 9.5 %all_to_all.23.got4 = bf16[16,4,384]{2,1,0:T(4,128)(2,1)S(1)} all-to-all(bf16[16,4,384]{2,1,0:T(4,128)(2,1)S(1)} %get-tuple-element.27), channel_id=1, replica_groups=mesh['groups'=2,'gx'=16] {'gx'}, dimensions={0} | all-to-all | bytes 98304 | tf_op jit(solution)/shard_map/all_to_all | solution.py:485
  63.4 1.9 %finish.1 = (f32[3,64,512]{2,1,0:T(8,128)}, f32[3,64,512]{2,1,0:T(8,128)}) custom-call(s32[1,49]{1,0:T(1,128)S(1)} %pad_add_fusion.send.live, bf16[16,4,384]{2,1,0:T(4,128)(2,1)S(1)} %all_to_all.23.got4, f32[3,64,512]{2,1,0:T(8,128)S(1)} %get-tuple-element.28.part, f32[3,64,512]{2,1,0:T(8,128)S(1)} %get-tuple-element.29.r2, ...), custom_call_target="tpu_custom_call" | custom-call | tf_op jit(solution)/shard_map/finish/pallas_call | solution.py:527
  (4 shorter events, 0.0 us)
Async XLA Ops:
  1.3 0.7 %copy-start.4 = (s32[1,48]{1,0:T(1,128)S(1)}, s32[1,48]{1,0:T(1,128)}, u32[]{:S(2)}) copy-start(s32[1,48]{1,0:T(1,128)} %param.11) | copy-start | bytes 580
  1.3 1.0 %copy-start = (f32[3,64,512]{2,1,0:T(8,128)S(1)}, f32[3,64,512]{2,1,0:T(8,128)}, u32[]{:S(2)}) copy-start(f32[3,64,512]{2,1,0:T(8,128)} %b.5) | copy-start | bytes 1179652
  1.3 1.1 %copy-start.1 = (f32[2,64,512]{2,1,0:T(8,128)S(1)}, f32[2,64,512]{2,1,0:T(8,128)}, u32[]{:S(2)}) copy-start(f32[2,64,512]{2,1,0:T(8,128)} %stiff.5) | copy-start | bytes 786436
  1.3 1.1 %copy-start.2 = (f32[64,512]{1,0:T(8,128)S(1)}, f32[64,512]{1,0:T(8,128)}, u32[]{:S(2)}) copy-start(f32[64,512]{1,0:T(8,128)} %mass.5) | copy-start | bytes 393220
  1.3 18.9 %slice-start = ((s8[10616832]{0:T(1024)(128)(4,1)}), s8[4194304]{0:T(1024)(128)(4,1)S(1)}, s32[]{:S(2)}) async-start(s8[10616832]{0:T(1024)(128)(4,1)} %bitcast.3), calls=%async_computation.4 | async-start | bytes 8388608
  1.3 18.9 %slice-start.1 = ((s8[10616832]{0:T(1024)(128)(4,1)}), s8[4194304]{0:T(1024)(128)(4,1)S(1)}, s32[]{:S(2)}) async-start(s8[10616832]{0:T(1024)(128)(4,1)} %bitcast.3), calls=%async_computation.5 | async-start | bytes 8388608
  1.4 18.9 %copy-start.3 = (s32[36,2]{0,1:T(2,128)S(1)}, s32[36,2]{0,1:T(2,128)}, u32[]{:S(2)}) copy-start(s32[36,2]{0,1:T(2,128)} %param.12) | copy-start | bytes 868
  1.4 18.8 %slice-start.2 = ((s8[10616832]{0:T(1024)(128)(4,1)}), s8[2228224]{0:T(1024)(128)(4,1)S(1)}, s32[]{:S(2)}) async-start(s8[10616832]{0:T(1024)(128)(4,1)} %bitcast.3), calls=%async_computation.6 | async-start | bytes 4456448

commit v8 on v7

--- a/solution.py
+++ b/solution.py
@@ -312,52 +312,52 @@
         right = b[e]
         r1 = right - alpha0 * image
         w = image - alpha0 * second
-        terms = [r1 * r1, r1 * w, r1 * image, right * w, right * image, w * w, w * image, image * image]
+        terms = [r1 * r1, r1 * w, r1 * image, right * w, right * image]
         sums = terms if sums is None else [s + t for s, t in zip(sums, terms)]
     write_rim(common.at[0], v1)
     write_rim(common.at[1], v2)
     line = packed_line([total(s) for s in sums])
-    line = jnp.broadcast_to(line, (16, block_len))
-    sub = iota((16, block_len), 0)
+    width = stage.shape[2]
+    line = wide(jnp.concatenate([line, jnp.zeros((1, width - block_len), F32)], axis=1))
+    sub = iota((8, width), 0)
+    me = lax.axis_index("gx")
 
     def one(d, carry):
         for c in range(CAP):
             row, col = place_of(send, d * CAP + c, col_blocks)
             for e in range(3):
-                stage[d, c * 3 + e : c * 3 + e + 1, :] = panels[e, col, pl.ds(row, 1), :]
-        extra = jnp.where(sub < 9, stage[d], jnp.where(sub == 9, line, 0.0))
-        rims = jnp.concatenate([common[0], common[1]], axis=0)
-        message[d] = jnp.concatenate([rims, extra], axis=1).astype(BF16)
+                stage[d, 4 + c : 5 + c, e * block_len : (e + 1) * block_len] = panels[
+                    e, col, pl.ds(row, 1), :
+                ]
+        facing = jnp.where(d < me, common[1], pltpu.roll(common[1], 4, 0))
+        lower = jnp.where(sub < 4, facing, jnp.where(sub == 7, line, stage[d]))
+        message[d] = jnp.concatenate([common[0], lower], axis=0).astype(BF16)
         return carry
 
     lax.fori_loop(0, peers, one, 0, unroll=4)
 
 
-def coefficients(known, sums, b_x, v1_x, v2_x, x_x):
+def coefficients(known, sums, b_x, v1_x):
     rr0, alpha0 = pick(known, 0), pick(known, 1)
-    rr1, r1w, r1v1, bw, bv1, ww, wv1, v1v1 = [pick_packed(sums, k) for k in range(8)]
+    rr1, r1w, r1v1, bw, bv1 = [pick_packed(sums, k) for k in range(5)]
     r1w = r1w - alpha0 * (b_x - alpha0 * v1_x)
     bw = bw - alpha0 * b_x
-    ww = ww - 2.0 * alpha0 * (v1_x - alpha0 * v2_x) + alpha0 * alpha0 * x_x
-    wv1 = wv1 - alpha0 * v1_x
     beta0 = rr1 / rr0
-    alpha1 = rr1 / (r1w + beta0 * (r1v1 + bw) + beta0 * beta0 * bv1)
-    image_sq = ww + 2.0 * beta0 * wv1 + beta0 * beta0 * v1v1
-    rr2 = rr1 - 2.0 * alpha1 * (r1w + beta0 * r1v1) + alpha1 * alpha1 * image_sq
-    return alpha0, beta0, alpha1, rr2 / rr1
+    dad1 = r1w + beta0 * (r1v1 + bw) + beta0 * beta0 * bv1
+    return (alpha0, beta0, rr1 / dad1), line_of([rr1, dad1], known.shape[1])
 
 
 def advance(b, v1, v2, coefs):
-    alpha0, beta0, alpha1, beta1 = coefs
+    alpha0, beta0, alpha1 = coefs
     r1 = b - alpha0 * v1
-    d1 = r1 + beta0 * b
-    r2 = r1 - alpha1 * (v1 - alpha0 * v2 + beta0 * v1)
-    return d1, r2, r2 + beta1 * d1
+    image = v1 - alpha0 * v2 + beta0 * v1
+    return r1 + beta0 * b, image, r1 - alpha1 * image
 
 
 def last_kernel(
     pairs, live, got1, got3, held, sent2, known, b, v1, v2, mass, stiff, hessian,
-    message, part, r2_out, d2_out, dd2, x8, y8, tiles1, tiles3, corr, rim, edges,
+    message, part, d1_out, ad1_out, r2_out, ar2, known_out,
+    x8, y8, tiles1, tiles3, corr, rim, edges,
 ):
     peers = got1.shape[0]
     width = x8.shape[2]
@@ -368,30 +368,29 @@
 
     def one(d, carry):
         before, after = around(d, peers)
-        first = tiles3[d, 0:8, 0:width]
-        fix = rim_coefs(edges, d) * (
-            first - across(tiles3[before, 0:8, 0:width], tiles3[after, 0:8, 0:width])
+        first = tiles3[d, 0:8, :]
+        fix = rim_coefs(edges, d) * (first - across(tiles3[before, 0:8, :], tiles3[after, 0:8, :]))
+        corr[d] = fix
+        return (
+            carry[0] + tiles1[d, 0:8, :] * fix,
+            carry[1] + first * fix,
+            carry[2] + tiles3[d, 15:16, 0:128],
         )
-        corr[d] = fix
-        others = [tiles1[d, 0:8, 0:width], first, tiles3[d, 8:16, 0:width], fix]
-        return (
-            *[kept + other * fix for kept, other in zip(carry, others)],
-            carry[4] + tiles3[d, 9:10, width:],
-        )
 
     zero = jnp.zeros((8, width), F32)
-    *crossing, sums = lax.fori_loop(
-        0, peers, one, (zero, zero, zero, zero, jnp.zeros((1, 128), F32)), unroll=4
-    )
-    coefs = coefficients(known[...], sums, *[total(value) for value in crossing])
+    b_x, v1_x, sums = lax.fori_loop(
+        0, peers, one, (zero, zero, jnp.zeros((1, 128), F32)), unroll=4
+    )
+    coefs, known_line = coefficients(known[...], sums, total(b_x), total(v1_x))
+    known_out[...] = known_line
 
     def two(d, carry):
-        extra, line = tiles3[d, 0:16, width:], tiles1[d, 15:16, 128:256]
-        fix = corr[d]
+        line = tiles1[d, 15:16, 128:256]
+        fix, values = corr[d], tiles3[d, 8:16, :]
         kept, sent = held[d], sent2[d].astype(F32)
         for c in range(CAP):
-            value = jnp.concatenate([extra[c * 3 + e : c * 3 + e + 1] for e in range(3)], axis=1)
-            value = value + chosen(pick(line, CODE_LANE + c), fix) + sent[CAP + c : CAP + c + 1]
+            value = values[4 + c : 5 + c] + chosen(pick(line, CODE_LANE + c), fix)
+            value = value + sent[CAP + c : CAP + c + 1]
             x8[d * CAP + c] = wide(
                 advance(kept[c : c + 1], kept[CAP + c : CAP + c + 1], value, coefs)[2]
             )
@@ -402,53 +401,58 @@
     me = lax.axis_index("gx")
     before, after = around(me, peers)
     ky = masked_ky(stiff)
-    mine = corr[me] * (coefs[0] * coefs[2])
+    mine = corr[me] * coefs[0]
     for e in range(3):
-        d1, r2, d2 = advance(b[e], v1[e], v2[e], coefs)
+        d1, image, r2 = advance(b[e], v1[e], v2[e], coefs)
         part[e] = coefs[0] * b[e] + coefs[2] * d1
+        d1_out[e] = d1
+        ad1_out[e] = image
         r2_out[e] = r2
-        d2_out[e] = d2
         for side, row in enumerate((0, rows - 1)):
-            r2_out[e, row : row + 1, :] = r2_out[e, row : row + 1, :] + rim_row(mine, side, e)
-            d2_out[e, row : row + 1, :] = d2_out[e, row : row + 1, :] + rim_row(mine, side, e)
-    write_rim(rim, d2_out)
-
-    def rim_direction(d):
-        return advance(
-            tiles1[d, 0:8, 0:width],
-            tiles3[d, 0:8, 0:width],
-            tiles3[d, 8:16, 0:width] + corr[d],
-            coefs,
-        )[2]
-
-    fix = rim_coefs(edges, me) * (rim[...] - across(rim_direction(before), rim_direction(after)))
-    sq = dot = None
+            change = rim_row(mine, side, e)
+            ad1_out[e, row : row + 1, :] = ad1_out[e, row : row + 1, :] - change
+            r2_out[e, row : row + 1, :] = r2_out[e, row : row + 1, :] + coefs[2] * change
+    write_rim(rim, r2_out)
+
+    facing = jnp.where(
+        iota((8, width), 0) < 4, tiles3[before, 8:16, :], pltpu.roll(tiles3[after, 8:16, :], 4, 0)
+    )
+    others = advance(
+        across(tiles1[before, 0:8, :], tiles1[after, 0:8, :]),
+        across(tiles3[before, 0:8, :], tiles3[after, 0:8, :]),
+        facing + across(corr[before], corr[after]),
+        coefs,
+    )[2]
+    fix = rim_coefs(edges, me) * (rim[...] - others)
+    sums = None
     for e in range(3):
-        r2, d2 = r2_out[e], d2_out[e]
-        dd2[e] = inner_apply(d2, mass[...], stiff[0], ky)
+        r2 = r2_out[e]
+        ar2[e] = inner_apply(r2, mass[...], stiff[0], ky)
         for side, row in enumerate((0, rows - 1)):
-            dd2[e, row : row + 1, :] = dd2[e, row : row + 1, :] + rim_row(fix, side, e)
-        sq = r2 * r2 if sq is None else sq + r2 * r2
-        dot = d2 * dd2[e] if dot is None else dot + d2 * dd2[e]
-    rr2, dad2 = total(sq), total(dot)
+            ar2[e, row : row + 1, :] = ar2[e, row : row + 1, :] + rim_row(fix, side, e)
+        terms = [r2 * r2, r2 * ar2[e], r2 * ad1_out[e]]
+        sums = terms if sums is None else [s + t for s, t in zip(sums, terms)]
+    sums = [total(value) for value in sums]
 
     contact_products(pairs, live[0, live.shape[1] - 1], x8, y8, hessian)
-    line = packed_line([rr2, dad2 + contact_dot(x8, y8)])
+    line = packed_line([sums[0], sums[1] + contact_dot(x8, y8), sums[2]])
     line = jnp.concatenate([line, jnp.zeros((1, width - 128), F32)], axis=1)
     for d in range(peers):
         rows = [y8[d * CAP + c, 0:1, :] for c in range(CAP)]
         message[d] = jnp.concatenate([*rows, line], axis=0).astype(BF16)
 
 
-def finish_kernel(send, got4, part, r2, d2, dd2, solution, residual, cd2, back):
+def finish_kernel(send, got4, known, part, d1, ad1, r2, ar2, solution, residual, cr2, back):
     for d in range(got4.shape[0]):
         back[d] = got4[d].astype(F32)
-    scatter_blocks(send, back, [cd2])
+    scatter_blocks(send, back, [cr2])
     sums = line_sum(back, SUMS_ONE)
-    alpha2 = pick_packed(sums, 0) / pick_packed(sums, 1)
+    rr2, rar2, rad1 = [pick_packed(sums, k) for k in range(3)]
+    beta1 = rr2 / pick(known[...], 0)
+    alpha2 = rr2 / (rar2 + 2.0 * beta1 * rad1 + beta1 * beta1 * pick(known[...], 1))
     for e in range(3):
-        solution[e] = part[e] + alpha2 * d2[e]
-        residual[e] = r2[e] - alpha2 * (dd2[e] + from_panels(cd2, e))
+        solution[e] = part[e] + alpha2 * (r2[e] + beta1 * d1[e])
+        residual[e] = r2[e] - alpha2 * (ar2[e] + from_panels(cr2, e) + beta1 * ad1[e])
 
 
 def call(kernel, spaces, outs, scratch=(), mebibytes=16, name=None):
@@ -472,10 +476,10 @@
     assert send_list.shape[1] == peers * CAP and col_count == 4 * block_len and block_len == 128
     field = (right_side.shape, F32)
     first, second = ((peers, 16, width), BF16), ((peers, 8, width), BF16)
-    third, fourth = ((peers, 16, 4 * block_len), BF16), ((peers, 4, width), BF16)
+    third, fourth = ((peers, 16, width), BF16), ((peers, 4, width), BF16)
     held_shape, edges = ((peers, 8, width), F32), (peers, 8, block_len)
     panels = (3, 4, row_count, block_len)
-    tiles, wide_tiles, rims = (peers * CAP, 8, width), (peers, 16, 4 * block_len), (peers, 8, width)
+    tiles, wide_tiles, rims = (peers * CAP, 8, width), (peers, 16, width), (peers, 8, width)
     line = ((1, 128), F32)
 
     routes = jnp.concatenate([send_list, counts.reshape(1, 1)], axis=1)
@@ -499,7 +503,7 @@
         owner_kernel,
         "ssvv",
         [second, held_shape, ((8, width), F32), line],
-        [tiles, tiles, tiles, tiles, (peers, 16, width), rims, edges],
+        [tiles, tiles, tiles, tiles, wide_tiles, rims, edges],
         32,
         name="owner",
     )(pair_refs, routes, got1, hessian)
@@ -508,15 +512,15 @@
         middle_kernel,
         "svvvvvvv",
         [third, field, field, line],
-        [panels, panels, panels, (2, 8, width), (peers, 16, block_len), rims],
+        [panels, panels, panels, (2, 8, width), rims, rims],
         name="middle",
     )(routes, got2, own, known1, right_side, loc, masses, stiffness)
     got3 = swap(sent3)
-    sent4, part, r2, d2, dd2 = call(
+    sent4, part, d1, ad1, r2, ar2, known2 = call(
         last_kernel,
         "ssvvvvvvvvvvv",
-        [fourth, field, field, field, field],
-        [tiles, tiles, (peers, 16, width), wide_tiles, rims, (8, width), edges],
+        [fourth, field, field, field, field, field, line],
+        [tiles, tiles, wide_tiles, wide_tiles, rims, (8, width), edges],
         32,
         name="last",
     )(
@@ -524,8 +528,8 @@
         hessian,
     )
     got4 = swap(sent4)
-    return call(finish_kernel, "svvvvv", [field, field], [panels, (peers, 4, width)], name="finish")(
-        routes, got4, part, r2, d2, dd2
+    return call(finish_kernel, "svvvvvvv", [field, field], [panels, (peers, 4, width)], name="finish")(
+        routes, got4, known2, part, d1, ad1, r2, ar2
     )
 
 

time: 65.5 us -> 64.2 us (0.980)
  blocking collectives: 48.6 us -> 47.4 us
    all_to_all x4, blocking collectives: 48.6 us -> 47.4 us  [swap(): lax.all_to_all(message, 'gx', split_axis=0, concat_axis=0, tiled=True)]
where the time goes in v8:
time: 64.2 us; the launch traced here: 64 us
  blocking collectives  47.4 us (74%)
  Pallas kernels  14.1 us (22%)
  between operations  1.41 us (2%)
  local copies, waits for them, and re-layouts  0.97 us (2%)
    all_to_all x4, blocking collectives, swap(): lax.all_to_all(message, 'gx', split_axis=0, concat_axis=0, tiled=True)  47.4 us
    pallas_call x1, Pallas kernels, per_device(): call(owner_kernel, 'ssvv', [second, held_shape, ((8, width), F32), line],...  4.69 us
    pallas_call x1, Pallas kernels, per_device(): call(last_kernel, 'ssvvvvvvvvvvv', [fourth, field, field, field, field, f...  4.12 us
    pallas_call x1, Pallas kernels, per_device(): call(finish_kernel, 'svvvvvvv', [field, field], [panels, (peers, 4, width...  2.07 us
    pallas_call x1, Pallas kernels, per_device(): call(middle_kernel, 'svvvvvvv', [third, field, field, line], [panels, pan...  1.89 us
    pallas_call x1, Pallas kernels, per_device(): call(start_kernel, 'asvvv', [first, field], [panels, panels, (8, width),...  1.36 us

profile of v8, /device:TPU:0, one launch (start us, length us, event | category | flops | bytes accessed | tf_op | source)
XLA Modules:
  0.0 64.0 jit_solution(11795744838504346971)
XLA Ops:
  1.3 0.0 copy-start.4
  1.3 0.0 copy-start
  1.3 0.0 copy-start.1
  1.3 0.0 copy-start.2
  1.3 0.0 slice-start
  1.3 0.0 slice-start.1
  1.4 0.0 copy-start.3
  1.4 0.0 slice-start.2
  1.4 0.5 copy-done.4
  1.9 0.1 pad_add_fusion.send.live
  2.0 0.3 copy-done
  2.3 0.1 copy-done.1
  2.4 0.0 copy-done.2
  2.4 1.4 %start.1 = (bf16[16,16,384]{2,1,0:T(8,128)(2,1)S(1)}, f32[3,64,512]{2,1,0:T(8,128)S(1)}) custom-call(f32[1,128]{1,0:T(1,128)S(1)} %announce.3._, s32[1,49]{1,0:T(1,128)S(1)} %pad_add_fusion.send.live, f32[3,64,512]{2,1,0:T(8,128)S(1)} %copy-done, f32[64,512]{1,0:T(8,128)S(1)} %copy-done.2, f32[2,64,512]{2,1,0:T(8,128)S(1)} %copy-done.1), custom_call_target="tpu_custom_call" | custom-call | tf_op jit(solution)/shard_map/start/pallas_call | solution.py:494
  3.8 16.4 %all_to_all.20.got.got1 = bf16[16,16,384]{2,1,0:T(8,128)(2,1)S(1)} all-to-all(bf16[16,16,384]{2,1,0:T(8,128)(2,1)S(1)} %get-tuple-element.19), channel_id=1, replica_groups=mesh['groups'=2,'gx'=16] {'gx'}, dimensions={0} | all-to-all | bytes 393216 | tf_op jit(solution)/shard_map/all_to_all | solution.py:489
  20.2 0.0 slice-done
  20.2 0.0 slice-done.1
  20.2 0.0 copy-done.3
  20.2 0.0 slice-done.2
  20.2 4.7 %owner.1 = (bf16[16,8,384]{2,1,0:T(8,128)(2,1)S(1)}, f32[16,8,384]{2,1,0:T(8,128)S(1)}, f32[8,384]{1,0:T(8,128)S(1)}, f32[1,128]{1,0:T(1,128)S(1)}) custom-call(s32[2,36]{1,0:T(2,128)S(1)} %bitcast.5, s32[1,49]{1,0:T(1,128)S(1)} %pad_add_fusion.send.live, bf16[16,16,384]{2,1,0:T(8,128)(2,1)S(1)} %all_to_all.20.got.got1, bf16[36,384,384]{2,1,0:T(8,128)(2,1)S(1)} %bitcast.4), custom_call_target="tpu_custom_call" | custom-call | tf_op jit(solution)/shard_map/owner/pallas_call | solution.py:502
  24.9 10.0 %all_to_all.21.got2 = bf16[16,8,384]{2,1,0:T(8,128)(2,1)S(1)} all-to-all(bf16[16,8,384]{2,1,0:T(8,128)(2,1)S(1)} %get-tuple-element.20.sent2), channel_id=1, replica_groups=mesh['groups'=2,'gx'=16] {'gx'}, dimensions={0} | all-to-all | bytes 196608 | tf_op jit(solution)/shard_map/all_to_all | solution.py:489
  34.9 1.9 %middle.1 = (bf16[16,16,384]{2,1,0:T(8,128)(2,1)S(1)}, f32[3,64,512]{2,1,0:T(8,128)S(1)}, f32[3,64,512]{2,1,0:T(8,128)S(1)}, f32[1,128]{1,0:T(1,128)S(1)}) custom-call(s32[1,49]{1,0:T(1,128)S(1)} %pad_add_fusion.send.live, bf16[16,8,384]{2,1,0:T(8,128)(2,1)S(1)} %all_to_all.21.got2, f32[8,384]{1,0:T(8,128)S(1)} %get-tuple-element.21.own, ...), custom_call_target="tpu_custom_call" | custom-call | tf_op jit(solution)/shard_map/middle/pallas_call | solution.py:511
  36.8 11.6 %all_to_all.22.got3 = bf16[16,16,384]{2,1,0:T(8,128)(2,1)S(1)} all-to-all(bf16[16,16,384]{2,1,0:T(8,128)(2,1)S(1)} %get-tuple-element.24), channel_id=1, replica_groups=mesh['groups'=2,'gx'=16] {'gx'}, dimensions={0} | all-to-all | bytes 393216 | tf_op jit(solution)/shard_map/all_to_all | solution.py:489
  48.4 4.1 %last.1 = (bf16[16,4,384]{2,1,0:T(4,128)(2,1)S(1)}, f32[3,64,512]{2,1,0:T(8,128)S(1)}, f32[3,64,512]{2,1,0:T(8,128)S(1)}, f32[3,64,512]{2,1,0:T(8,128)S(1)}, f32...) custom-call(s32[2,36]{1,0:T(2,128)S(1)} %bitcast.6, s32[1,49]{1,0:T(1,128)S(1)} %pad_add_fusion.send.live, ...), custom_call_target="tpu_custom_call" | custom-call | tf_op jit(solution)/shard_map/last/pallas_call | solution.py:519
  52.5 9.3 %all_to_all.23.got4 = bf16[16,4,384]{2,1,0:T(4,128)(2,1)S(1)} all-to-all(bf16[16,4,384]{2,1,0:T(4,128)(2,1)S(1)} %get-tuple-element.29), channel_id=1, replica_groups=mesh['groups'=2,'gx'=16] {'gx'}, dimensions={0} | all-to-all | bytes 98304 | tf_op jit(solution)/shard_map/all_to_all | solution.py:489
  61.9 2.1 %finish.1 = (f32[3,64,512]{2,1,0:T(8,128)}, f32[3,64,512]{2,1,0:T(8,128)}) custom-call(s32[1,49]{1,0:T(1,128)S(1)} %pad_add_fusion.send.live, bf16[16,4,384]{2,1,0:T(4,128)(2,1)S(1)} %all_to_all.23.got4, f32[1,128]{1,0:T(1,128)S(1)} %get-tuple-element.30.known, f32[3,64,512]{2,1,0:T(8,128)S(1)} %get-tuple-element.31.part, ...), custom_call_target="tpu_custom_call" | custom-call | tf_op jit(solution)/shard_map/finish/pallas_call | solution.py:531
  (4 shorter events, 0.0 us)
Async XLA Ops:
  1.3 0.7 %copy-start.4 = (s32[1,48]{1,0:T(1,128)S(1)}, s32[1,48]{1,0:T(1,128)}, u32[]{:S(2)}) copy-start(s32[1,48]{1,0:T(1,128)} %param.11) | copy-start | bytes 580
  1.3 1.0 %copy-start = (f32[3,64,512]{2,1,0:T(8,128)S(1)}, f32[3,64,512]{2,1,0:T(8,128)}, u32[]{:S(2)}) copy-start(f32[3,64,512]{2,1,0:T(8,128)} %b.5) | copy-start | bytes 1179652
  1.3 1.1 %copy-start.1 = (f32[2,64,512]{2,1,0:T(8,128)S(1)}, f32[2,64,512]{2,1,0:T(8,128)}, u32[]{:S(2)}) copy-start(f32[2,64,512]{2,1,0:T(8,128)} %stiff.5) | copy-start | bytes 786436
  1.3 1.1 %copy-start.2 = (f32[64,512]{1,0:T(8,128)S(1)}, f32[64,512]{1,0:T(8,128)}, u32[]{:S(2)}) copy-start(f32[64,512]{1,0:T(8,128)} %mass.5) | copy-start | bytes 393220
  1.3 18.9 %slice-start = ((s8[10616832]{0:T(1024)(128)(4,1)}), s8[4194304]{0:T(1024)(128)(4,1)S(1)}, s32[]{:S(2)}) async-start(s8[10616832]{0:T(1024)(128)(4,1)} %bitcast.3), calls=%async_computation.4 | async-start | bytes 8388608
  1.3 18.9 %slice-start.1 = ((s8[10616832]{0:T(1024)(128)(4,1)}), s8[4194304]{0:T(1024)(128)(4,1)S(1)}, s32[]{:S(2)}) async-start(s8[10616832]{0:T(1024)(128)(4,1)} %bitcast.3), calls=%async_computation.5 | async-start | bytes 8388608
  1.4 18.9 %copy-start.3 = (s32[36,2]{0,1:T(2,128)S(1)}, s32[36,2]{0,1:T(2,128)}, u32[]{:S(2)}) copy-start(s32[36,2]{0,1:T(2,128)} %param.12) | copy-start | bytes 868
  1.4 18.8 %slice-start.2 = ((s8[10616832]{0:T(1024)(128)(4,1)}), s8[2228224]{0:T(1024)(128)(4,1)S(1)}, s32[]{:S(2)}) async-start(s8[10616832]{0:T(1024)(128)(4,1)} %bitcast.3), calls=%async_computation.6 | async-start | bytes 4456448

commit v9 on v8

--- a/solution.py
+++ b/solution.py
@@ -44,7 +44,8 @@
 
 def place_of(send, position, col_blocks):
     block = send[0, position]
-    return lax.div(block, jnp.int32(col_blocks)), lax.rem(block, jnp.int32(col_blocks))
+    shift = col_blocks.bit_length() - 1
+    return lax.shift_right_logical(block, jnp.int32(shift)), block & (col_blocks - 1)
 
 
 def scatter_blocks(send, message, panels):
@@ -63,7 +64,7 @@
                     ]
         return carry
 
-    lax.fori_loop(0, peers, one, 0, unroll=4)
+    lax.fori_loop(0, peers, one, 0, unroll=16)
 
 
 def to_panels(panels, e, value):
@@ -211,7 +212,7 @@
         message[d] = jnp.concatenate([rim[...], lower], axis=0).astype(BF16)
         return carry
 
-    lax.fori_loop(0, peers, one, 0, unroll=4)
+    lax.fori_loop(0, peers, one, 0, unroll=16)
 
 
 def contact_products(pairs, live_count, x8, y8, held):
@@ -263,7 +264,7 @@
         return energy + fix * diff, sums + line
 
     zero = jnp.zeros((8, width), F32)
-    energy, sums = lax.fori_loop(0, peers, one, (zero, jnp.zeros((1, block_len), F32)), unroll=4)
+    energy, sums = lax.fori_loop(0, peers, one, (zero, jnp.zeros((1, block_len), F32)), unroll=16)
     known[...] = line_of(
         [pick_packed(sums, 0), pick_packed(sums, 1) + 0.5 * total(energy)], known.shape[1]
     )
@@ -334,7 +335,7 @@
         message[d] = jnp.concatenate([common[0], lower], axis=0).astype(BF16)
         return carry
 
-    lax.fori_loop(0, peers, one, 0, unroll=4)
+    lax.fori_loop(0, peers, one, 0, unroll=16)
 
 
 def coefficients(known, sums, b_x, v1_x):
@@ -396,7 +397,7 @@
             )
         return carry
 
-    lax.fori_loop(0, peers, two, 0, unroll=4)
+    lax.fori_loop(0, peers, two, 0, unroll=16)
 
     me = lax.axis_index("gx")
     before, after = around(me, peers)
@@ -442,27 +443,43 @@
         message[d] = jnp.concatenate([*rows, line], axis=0).astype(BF16)
 
 
-def finish_kernel(send, got4, known, part, d1, ad1, r2, ar2, solution, residual, cr2, back):
+def finish_kernel(
+    send, got4, known, part, d1, ad1, r2, ar2, solution, residual, cr2, back, x, r3, sems
+):
     for d in range(got4.shape[0]):
         back[d] = got4[d].astype(F32)
-    scatter_blocks(send, back, [cr2])
     sums = line_sum(back, SUMS_ONE)
     rr2, rar2, rad1 = [pick_packed(sums, k) for k in range(3)]
     beta1 = rr2 / pick(known[...], 0)
     alpha2 = rr2 / (rar2 + 2.0 * beta1 * rad1 + beta1 * beta1 * pick(known[...], 1))
+    copies = []
+
+    def send_out(source, target):
+        copies.append(pltpu.make_async_copy(source, target, sems.at[len(copies)]))
+        copies[-1].start()
+
     for e in range(3):
-        solution[e] = part[e] + alpha2 * (r2[e] + beta1 * d1[e])
-        residual[e] = r2[e] - alpha2 * (ar2[e] + from_panels(cr2, e) + beta1 * ad1[e])
-
-
-def call(kernel, spaces, outs, scratch=(), mebibytes=16, name=None):
+        x[e] = part[e] + alpha2 * (r2[e] + beta1 * d1[e])
+        send_out(x.at[e], solution.at[e])
+    scatter_blocks(send, back, [cr2])
+    for e in range(3):
+        r3[e] = r2[e] - alpha2 * (ar2[e] + from_panels(cr2, e) + beta1 * ad1[e])
+        send_out(r3.at[e], residual.at[e])
+    for copy in copies:
+        copy.wait()
+
+
+def call(kernel, spaces, outs, scratch=(), mebibytes=16, semaphores=0, name=None):
     kinds = {"s": pltpu.SMEM, "v": pltpu.VMEM, "a": pl.ANY}
     return pl.pallas_call(
         kernel,
         out_shape=tuple(jax.ShapeDtypeStruct(shape, kind) for shape, kind in outs),
         in_specs=[pl.BlockSpec(memory_space=kinds[k]) for k in spaces],
-        out_specs=tuple(pl.BlockSpec(memory_space=pltpu.VMEM) for _ in outs),
-        scratch_shapes=[pltpu.VMEM(shape, F32) for shape in scratch],
+        out_specs=tuple(
+            pl.BlockSpec(memory_space=pl.ANY if semaphores else pltpu.VMEM) for _ in outs
+        ),
+        scratch_shapes=[pltpu.VMEM(shape, F32) for shape in scratch]
+        + [pltpu.SemaphoreType.DMA((semaphores,))] * bool(semaphores),
         compiler_params=pltpu.CompilerParams(vmem_limit_bytes=mebibytes * 2**20),
         name=name,
     )
@@ -528,7 +545,7 @@
         hessian,
     )
     got4 = swap(sent4)
-    return call(finish_kernel, "svvvvvvv", [field, field], [panels, (peers, 4, width)], name="finish")(
+    return call(finish_kernel, "svvvvvvv", [field, field], [panels, (peers, 4, width), field[0], field[0]], semaphores=6, name="finish")(
         routes, got4, known2, part, d1, ad1, r2, ar2
     )
 

time: 64.2 us -> 63 us (0.981)
  Pallas kernels: 14.1 us -> 12.9 us
where the time goes in v9:
time: 63 us; the launch traced here: 62.7 us
  blocking collectives  47.4 us (75%)
  Pallas kernels  12.9 us (20%)
  between operations  1.41 us (2%)
  local copies, waits for them, and re-layouts  0.97 us (2%)
    all_to_all x4, blocking collectives, swap(): lax.all_to_all(message, 'gx', split_axis=0, concat_axis=0, tiled=True)  47.4 us
    pallas_call x1, Pallas kernels, per_device(): call(owner_kernel, 'ssvv', [second, held_shape, ((8, width), F32), line],...  4.39 us
    pallas_call x1, Pallas kernels, per_device(): call(last_kernel, 'ssvvvvvvvvvvv', [fourth, field, field, field, field, f...  3.85 us
    pallas_call x1, Pallas kernels, per_device(): call(finish_kernel, 'svvvvvvv', [field, field], [panels, (peers, 4, width...  1.82 us
    pallas_call x1, Pallas kernels, per_device(): call(middle_kernel, 'svvvvvvv', [third, field, field, line], [panels, pan...  1.57 us

profile of v9, /device:TPU:0, one launch (start us, length us, event | category | flops | bytes accessed | tf_op | source)
XLA Modules:
  0.0 62.7 jit_solution(7460807939757252517)
XLA Ops:
  1.3 0.0 copy-start.4
  1.3 0.0 copy-start
  1.3 0.0 copy-start.1
  1.3 0.0 copy-start.2
  1.3 0.0 slice-start
  1.3 0.0 slice-start.1
  1.4 0.0 copy-start.3
  1.4 0.0 slice-start.2
  1.4 0.5 copy-done.4
  1.9 0.1 pad_add_fusion.send.live
  2.0 0.3 copy-done
  2.3 0.1 copy-done.1
  2.4 0.0 copy-done.2
  2.4 1.2 %start.1 = (bf16[16,16,384]{2,1,0:T(8,128)(2,1)S(1)}, f32[3,64,512]{2,1,0:T(8,128)S(1)}) custom-call(f32[1,128]{1,0:T(1,128)S(1)} %announce.3._, s32[1,49]{1,0:T(1,128)S(1)} %pad_add_fusion.send.live, f32[3,64,512]{2,1,0:T(8,128)S(1)} %copy-done, f32[64,512]{1,0:T(8,128)S(1)} %copy-done.2, f32[2,64,512]{2,1,0:T(8,128)S(1)} %copy-done.1), custom_call_target="tpu_custom_call" | custom-call | tf_op jit(solution)/shard_map/start/pallas_call | solution.py:511
  3.6 16.4 %all_to_all.20.got.got1 = bf16[16,16,384]{2,1,0:T(8,128)(2,1)S(1)} all-to-all(bf16[16,16,384]{2,1,0:T(8,128)(2,1)S(1)} %get-tuple-element.19), channel_id=1, replica_groups=mesh['groups'=2,'gx'=16] {'gx'}, dimensions={0} | all-to-all | bytes 393216 | tf_op jit(solution)/shard_map/all_to_all | solution.py:506
  20.1 0.0 slice-done
  20.1 0.0 slice-done.1
  20.1 0.0 copy-done.3
  20.1 0.0 slice-done.2
  20.1 4.4 %owner.1 = (bf16[16,8,384]{2,1,0:T(8,128)(2,1)S(1)}, f32[16,8,384]{2,1,0:T(8,128)S(1)}, f32[8,384]{1,0:T(8,128)S(1)}, f32[1,128]{1,0:T(1,128)S(1)}) custom-call(s32[2,36]{1,0:T(2,128)S(1)} %bitcast.5, s32[1,49]{1,0:T(1,128)S(1)} %pad_add_fusion.send.live, bf16[16,16,384]{2,1,0:T(8,128)(2,1)S(1)} %all_to_all.20.got.got1, bf16[36,384,384]{2,1,0:T(8,128)(2,1)S(1)} %bitcast.4), custom_call_target="tpu_custom_call" | custom-call | tf_op jit(solution)/shard_map/owner/pallas_call | solution.py:519
  24.5 10.0 %all_to_all.21.got2 = bf16[16,8,384]{2,1,0:T(8,128)(2,1)S(1)} all-to-all(bf16[16,8,384]{2,1,0:T(8,128)(2,1)S(1)} %get-tuple-element.20.sent2), channel_id=1, replica_groups=mesh['groups'=2,'gx'=16] {'gx'}, dimensions={0} | all-to-all | bytes 196608 | tf_op jit(solution)/shard_map/all_to_all | solution.py:506
  34.5 1.6 %middle.1 = (bf16[16,16,384]{2,1,0:T(8,128)(2,1)S(1)}, f32[3,64,512]{2,1,0:T(8,128)S(1)}, f32[3,64,512]{2,1,0:T(8,128)S(1)}, f32[1,128]{1,0:T(1,128)S(1)}) custom-call(s32[1,49]{1,0:T(1,128)S(1)} %pad_add_fusion.send.live, bf16[16,8,384]{2,1,0:T(8,128)(2,1)S(1)} %all_to_all.21.got2, f32[8,384]{1,0:T(8,128)S(1)} %get-tuple-element.21.own, ...), custom_call_target="tpu_custom_call" | custom-call | tf_op jit(solution)/shard_map/middle/pallas_call | solution.py:528
  36.1 11.6 %all_to_all.22.got3 = bf16[16,16,384]{2,1,0:T(8,128)(2,1)S(1)} all-to-all(bf16[16,16,384]{2,1,0:T(8,128)(2,1)S(1)} %get-tuple-element.24), channel_id=1, replica_groups=mesh['groups'=2,'gx'=16] {'gx'}, dimensions={0} | all-to-all | bytes 393216 | tf_op jit(solution)/shard_map/all_to_all | solution.py:506
  47.7 3.9 %last.1 = (bf16[16,4,384]{2,1,0:T(4,128)(2,1)S(1)}, f32[3,64,512]{2,1,0:T(8,128)S(1)}, f32[3,64,512]{2,1,0:T(8,128)S(1)}, f32[3,64,512]{2,1,0:T(8,128)S(1)}, f32...) custom-call(s32[2,36]{1,0:T(2,128)S(1)} %bitcast.6, s32[1,49]{1,0:T(1,128)S(1)} %pad_add_fusion.send.live, ...), custom_call_target="tpu_custom_call" | custom-call | tf_op jit(solution)/shard_map/last/pallas_call | solution.py:536
  51.5 9.3 %all_to_all.23.got4 = bf16[16,4,384]{2,1,0:T(4,128)(2,1)S(1)} all-to-all(bf16[16,4,384]{2,1,0:T(4,128)(2,1)S(1)} %get-tuple-element.29), channel_id=1, replica_groups=mesh['groups'=2,'gx'=16] {'gx'}, dimensions={0} | all-to-all | bytes 98304 | tf_op jit(solution)/shard_map/all_to_all | solution.py:506
  60.9 1.8 %finish.1 = (f32[3,64,512]{2,1,0:T(8,128)}, f32[3,64,512]{2,1,0:T(8,128)}) custom-call(s32[1,49]{1,0:T(1,128)S(1)} %pad_add_fusion.send.live, bf16[16,4,384]{2,1,0:T(4,128)(2,1)S(1)} %all_to_all.23.got4, f32[1,128]{1,0:T(1,128)S(1)} %get-tuple-element.30.known, f32[3,64,512]{2,1,0:T(8,128)S(1)} %get-tuple-element.31.part, ...), custom_call_target="tpu_custom_call" | custom-call | tf_op jit(solution)/shard_map/finish/pallas_call | solution.py:548
  (4 shorter events, 0.0 us)
Async XLA Ops:
  1.3 0.7 %copy-start.4 = (s32[1,48]{1,0:T(1,128)S(1)}, s32[1,48]{1,0:T(1,128)}, u32[]{:S(2)}) copy-start(s32[1,48]{1,0:T(1,128)} %param.11) | copy-start | bytes 580
  1.3 1.0 %copy-start = (f32[3,64,512]{2,1,0:T(8,128)S(1)}, f32[3,64,512]{2,1,0:T(8,128)}, u32[]{:S(2)}) copy-start(f32[3,64,512]{2,1,0:T(8,128)} %b.5) | copy-start | bytes 1179652
  1.3 1.1 %copy-start.1 = (f32[2,64,512]{2,1,0:T(8,128)S(1)}, f32[2,64,512]{2,1,0:T(8,128)}, u32[]{:S(2)}) copy-start(f32[2,64,512]{2,1,0:T(8,128)} %stiff.5) | copy-start | bytes 786436
  1.3 1.1 %copy-start.2 = (f32[64,512]{1,0:T(8,128)S(1)}, f32[64,512]{1,0:T(8,128)}, u32[]{:S(2)}) copy-start(f32[64,512]{1,0:T(8,128)} %mass.5) | copy-start | bytes 393220
  1.3 18.7 %slice-start = ((s8[10616832]{0:T(1024)(128)(4,1)}), s8[4194304]{0:T(1024)(128)(4,1)S(1)}, s32[]{:S(2)}) async-start(s8[10616832]{0:T(1024)(128)(4,1)} %bitcast.3), calls=%async_computation.4 | async-start | bytes 8388608
  1.3 18.7 %slice-start.1 = ((s8[10616832]{0:T(1024)(128)(4,1)}), s8[4194304]{0:T(1024)(128)(4,1)S(1)}, s32[]{:S(2)}) async-start(s8[10616832]{0:T(1024)(128)(4,1)} %bitcast.3), calls=%async_computation.5 | async-start | bytes 8388608
  1.4 18.7 %copy-start.3 = (s32[36,2]{0,1:T(2,128)S(1)}, s32[36,2]{0,1:T(2,128)}, u32[]{:S(2)}) copy-start(s32[36,2]{0,1:T(2,128)} %param.12) | copy-start | bytes 868
  1.4 18.7 %slice-start.2 = ((s8[10616832]{0:T(1024)(128)(4,1)}), s8[2228224]{0:T(1024)(128)(4,1)S(1)}, s32[]{:S(2)}) async-start(s8[10616832]{0:T(1024)(128)(4,1)} %bitcast.3), calls=%async_computation.6 | async-start | bytes 4456448

commit v10 on v9

--- a/solution.py
+++ b/solution.py
@@ -217,16 +217,27 @@
 
 def contact_products(pairs, live_count, x8, y8, held):
     y8[...] = jnp.zeros_like(y8)
-    for h in range(held.shape[0]):
-        a, b = pairs[0, h], pairs[1, h]
-        delta = x8[a] - x8[b]
-        delta = jnp.where(h < live_count, delta, 0.0)
-        coarse = delta.astype(jnp.bfloat16).astype(F32)
-        both = jnp.concatenate([coarse, delta - coarse], axis=0).astype(jnp.bfloat16)
-        product = jnp.dot(both, held[h], preferred_element_type=F32)
-        y = product[0:8] + product[8:16]
-        y8[a] = y8[a] + y
-        y8[b] = y8[b] - y
+    groups, depth, width = held.shape
+    slots = depth // width
+    sub = iota((8, width), 0)
+    zero = jnp.zeros((8, width), F32)
+    for g in range(groups):
+        ends, rows = [], []
+        for k in range(slots):
+            h = g * slots + k
+            a, b = pairs[0, h], pairs[1, h]
+            delta = jnp.where(h < live_count, x8[a] - x8[b], 0.0)
+            coarse = rounded(delta)
+            value = jnp.where(sub < 4, coarse, delta - coarse)
+            rows.append(jnp.concatenate([value if j == k else zero for j in range(slots)], axis=1))
+            ends.append((a, b))
+        left = jnp.concatenate(rows, axis=0).astype(BF16)
+        product = jnp.dot(left, held[g], preferred_element_type=F32)
+        for k, (a, b) in enumerate(ends):
+            y = product[8 * k : 8 * k + 8]
+            y = y + pltpu.roll(y, 4, 0)
+            y8[a] = y8[a] + y
+            y8[b] = y8[b] - y
 
 
 def wide(row):
@@ -501,6 +512,9 @@
 
     routes = jnp.concatenate([send_list, counts.reshape(1, 1)], axis=1)
     pair_refs = pair_refs.T
+    slots = hessian.shape[0]
+    grouped = 2 if slots % 2 == 0 else 1
+    hessian = hessian.reshape(slots // grouped, grouped * width, width)
 
     def swap(message):
         return lax.all_to_all(message, "gx", split_axis=0, concat_axis=0, tiled=True)

time: 63 us -> 62.6 us (level)
  no operation moved by 1% of the time
where the time goes in v10:
time: 62.6 us; the launch traced here: 62.3 us
  blocking collectives  47.4 us (76%)
  Pallas kernels  12.5 us (20%)
  between operations  1.41 us (2%)
  local copies, waits for them, and re-layouts  0.97 us (2%)
    all_to_all x4, blocking collectives, swap(): lax.all_to_all(message, 'gx', split_axis=0, concat_axis=0, tiled=True)  47.4 us
    pallas_call x1, Pallas kernels, per_device(): call(owner_kernel, 'ssvv', [second, held_shape, ((8, width), F32), line],...  4.13 us
    pallas_call x1, Pallas kernels, per_device(): call(last_kernel, 'ssvvvvvvvvvvv', [fourth, field, field, field, field, f...  3.73 us
    pallas_call x1, Pallas kernels, per_device(): call(finish_kernel, 'svvvvvvv', [field, field], [panels, (peers, 4, width...  1.82 us
    pallas_call x1, Pallas kernels, per_device(): call(middle_kernel, 'svvvvvvv', [third, field, field, line], [panels, pan...  1.57 us

profile of v10, /device:TPU:0, one launch (start us, length us, event | category | flops | bytes accessed | tf_op | source)
XLA Modules:
  0.0 62.3 jit_solution(3006596732815134175)
XLA Ops:
  1.3 0.0 copy-start.4
  1.3 0.0 copy-start
  1.3 0.0 copy-start.1
  1.3 0.0 copy-start.2
  1.3 0.0 slice-start
  1.3 0.0 slice-start.1
  1.4 0.0 copy-start.3
  1.4 0.0 slice-start.2
  1.4 0.5 copy-done.4
  1.9 0.1 pad_add_fusion.send.live
  2.0 0.3 copy-done
  2.3 0.1 copy-done.1
  2.4 0.0 copy-done.2
  2.4 1.2 %start.1 = (bf16[16,16,384]{2,1,0:T(8,128)(2,1)S(1)}, f32[3,64,512]{2,1,0:T(8,128)S(1)}) custom-call(f32[1,128]{1,0:T(1,128)S(1)} %announce.3._, s32[1,49]{1,0:T(1,128)S(1)} %pad_add_fusion.send.live, f32[3,64,512]{2,1,0:T(8,128)S(1)} %copy-done, f32[64,512]{1,0:T(8,128)S(1)} %copy-done.2, f32[2,64,512]{2,1,0:T(8,128)S(1)} %copy-done.1), custom_call_target="tpu_custom_call" | custom-call | tf_op jit(solution)/shard_map/start/pallas_call | solution.py:525
  3.6 16.4 %all_to_all.20.got.got1 = bf16[16,16,384]{2,1,0:T(8,128)(2,1)S(1)} all-to-all(bf16[16,16,384]{2,1,0:T(8,128)(2,1)S(1)} %get-tuple-element.19), channel_id=1, replica_groups=mesh['groups'=2,'gx'=16] {'gx'}, dimensions={0} | all-to-all | bytes 393216 | tf_op jit(solution)/shard_map/all_to_all | solution.py:520
  20.1 0.0 slice-done
  20.1 0.0 slice-done.1
  20.1 0.0 copy-done.3
  20.1 0.0 slice-done.2
  20.1 4.1 %owner.1 = (bf16[16,8,384]{2,1,0:T(8,128)(2,1)S(1)}, f32[16,8,384]{2,1,0:T(8,128)S(1)}, f32[8,384]{1,0:T(8,128)S(1)}, f32[1,128]{1,0:T(1,128)S(1)}) custom-call(s32[2,36]{1,0:T(2,128)S(1)} %bitcast.10, s32[1,49]{1,0:T(1,128)S(1)} %pad_add_fusion.send.live, bf16[16,16,384]{2,1,0:T(8,128)(2,1)S(1)} %all_to_all.20.got.got1, bf16[18,768,384]{2,1,0:T(8,128)(2,1)S(1)} %bitcast.8), custom_call_target="tpu_custom_call" | custom-call | tf_op jit(solution)/shard_map/owner/pallas_call | solution.py:533
  24.2 10.0 %all_to_all.21.got2 = bf16[16,8,384]{2,1,0:T(8,128)(2,1)S(1)} all-to-all(bf16[16,8,384]{2,1,0:T(8,128)(2,1)S(1)} %get-tuple-element.20.sent2), channel_id=1, replica_groups=mesh['groups'=2,'gx'=16] {'gx'}, dimensions={0} | all-to-all | bytes 196608 | tf_op jit(solution)/shard_map/all_to_all | solution.py:520
  34.2 1.6 %middle.1 = (bf16[16,16,384]{2,1,0:T(8,128)(2,1)S(1)}, f32[3,64,512]{2,1,0:T(8,128)S(1)}, f32[3,64,512]{2,1,0:T(8,128)S(1)}, f32[1,128]{1,0:T(1,128)S(1)}) custom-call(s32[1,49]{1,0:T(1,128)S(1)} %pad_add_fusion.send.live, bf16[16,8,384]{2,1,0:T(8,128)(2,1)S(1)} %all_to_all.21.got2, f32[8,384]{1,0:T(8,128)S(1)} %get-tuple-element.21.own, ...), custom_call_target="tpu_custom_call" | custom-call | tf_op jit(solution)/shard_map/middle/pallas_call | solution.py:542
  35.8 11.6 %all_to_all.22.got3 = bf16[16,16,384]{2,1,0:T(8,128)(2,1)S(1)} all-to-all(bf16[16,16,384]{2,1,0:T(8,128)(2,1)S(1)} %get-tuple-element.24), channel_id=1, replica_groups=mesh['groups'=2,'gx'=16] {'gx'}, dimensions={0} | all-to-all | bytes 393216 | tf_op jit(solution)/shard_map/all_to_all | solution.py:520
  47.4 3.7 %last.1 = (bf16[16,4,384]{2,1,0:T(4,128)(2,1)S(1)}, f32[3,64,512]{2,1,0:T(8,128)S(1)}, f32[3,64,512]{2,1,0:T(8,128)S(1)}, f32[3,64,512]{2,1,0:T(8,128)S(1)}, f32...) custom-call(s32[2,36]{1,0:T(2,128)S(1)} %bitcast.11, s32[1,49]{1,0:T(1,128)S(1)} %pad_add_fusion.send.live, ...), custom_call_target="tpu_custom_call" | custom-call | tf_op jit(solution)/shard_map/last/pallas_call | solution.py:550
  51.1 9.3 %all_to_all.23.got4 = bf16[16,4,384]{2,1,0:T(4,128)(2,1)S(1)} all-to-all(bf16[16,4,384]{2,1,0:T(4,128)(2,1)S(1)} %get-tuple-element.29), channel_id=1, replica_groups=mesh['groups'=2,'gx'=16] {'gx'}, dimensions={0} | all-to-all | bytes 98304 | tf_op jit(solution)/shard_map/all_to_all | solution.py:520
  60.5 1.8 %finish.1 = (f32[3,64,512]{2,1,0:T(8,128)}, f32[3,64,512]{2,1,0:T(8,128)}) custom-call(s32[1,49]{1,0:T(1,128)S(1)} %pad_add_fusion.send.live, bf16[16,4,384]{2,1,0:T(4,128)(2,1)S(1)} %all_to_all.23.got4, f32[1,128]{1,0:T(1,128)S(1)} %get-tuple-element.30.known, f32[3,64,512]{2,1,0:T(8,128)S(1)} %get-tuple-element.31.part, ...), custom_call_target="tpu_custom_call" | custom-call | tf_op jit(solution)/shard_map/finish/pallas_call | solution.py:562
  (4 shorter events, 0.0 us)
Async XLA Ops:
  1.3 0.7 %copy-start.4 = (s32[1,48]{1,0:T(1,128)S(1)}, s32[1,48]{1,0:T(1,128)}, u32[]{:S(2)}) copy-start(s32[1,48]{1,0:T(1,128)} %param.11) | copy-start | bytes 580
  1.3 1.0 %copy-start = (f32[3,64,512]{2,1,0:T(8,128)S(1)}, f32[3,64,512]{2,1,0:T(8,128)}, u32[]{:S(2)}) copy-start(f32[3,64,512]{2,1,0:T(8,128)} %b.5) | copy-start | bytes 1179652
  1.3 1.1 %copy-start.1 = (f32[2,64,512]{2,1,0:T(8,128)S(1)}, f32[2,64,512]{2,1,0:T(8,128)}, u32[]{:S(2)}) copy-start(f32[2,64,512]{2,1,0:T(8,128)} %stiff.5) | copy-start | bytes 786436
  1.3 1.1 %copy-start.2 = (f32[64,512]{1,0:T(8,128)S(1)}, f32[64,512]{1,0:T(8,128)}, u32[]{:S(2)}) copy-start(f32[64,512]{1,0:T(8,128)} %mass.5) | copy-start | bytes 393220
  1.3 18.7 %slice-start = ((s8[10616832]{0:T(1024)(128)(4,1)}), s8[4194304]{0:T(1024)(128)(4,1)S(1)}, s32[]{:S(2)}) async-start(s8[10616832]{0:T(1024)(128)(4,1)} %bitcast.6), calls=%async_computation.4 | async-start | bytes 8388608
  1.3 18.7 %slice-start.1 = ((s8[10616832]{0:T(1024)(128)(4,1)}), s8[4194304]{0:T(1024)(128)(4,1)S(1)}, s32[]{:S(2)}) async-start(s8[10616832]{0:T(1024)(128)(4,1)} %bitcast.6), calls=%async_computation.5 | async-start | bytes 8388608
  1.4 18.7 %copy-start.3 = (s32[36,2]{0,1:T(2,128)S(1)}, s32[36,2]{0,1:T(2,128)}, u32[]{:S(2)}) copy-start(s32[36,2]{0,1:T(2,128)} %param.12) | copy-start | bytes 868
  1.4 18.7 %slice-start.2 = ((s8[10616832]{0:T(1024)(128)(4,1)}), s8[2228224]{0:T(1024)(128)(4,1)S(1)}, s32[]{:S(2)}) async-start(s8[10616832]{0:T(1024)(128)(4,1)} %bitcast.6), calls=%async_computation.6 | async-start | bytes 4456448

commit v11 on v10

--- a/solution.py
+++ b/solution.py
@@ -167,10 +167,10 @@
     return thrice(jnp.where(iota(here.shape, 0) < 4, other, here))
 
 
-def chosen(code, tile):
-    return jnp.sum(
-        jnp.where(iota(tile.shape, 0).astype(F32) == code, tile, 0.0), axis=0, keepdims=True
-    )
+def spread_sum(tile):
+    for step in (4, 2, 1):
+        tile = tile + pltpu.roll(tile, step, 0)
+    return tile
 
 
 def announce_kernel(hessian, _, token):
@@ -252,12 +252,13 @@
 
 
 def owner_kernel(
-    pairs, live, got, hessian, message, held, own, known, x8, y8, z8, f8, tiles, corr, edges
+    pairs, live, got, hessian, message, held, own, known, marks, exact, x8, y8, z8, f8, tiles, corr, edges
 ):
     peers, _, _ = got.shape
     width = x8.shape[2]
     block_len = width // 3
     unpack_first(got, tiles, edges)
+    sub, sub_one = iota((8, width), 0), iota((8, block_len), 0).astype(F32)
 
     def one(d, carry):
         energy, sums = carry
@@ -271,7 +272,9 @@
         for c in range(CAP):
             p = d * CAP + c
             x8[p] = wide(body[c : c + 1])
-            f8[p] = wide(body[CAP + c : CAP + c + 1] + chosen(pick(line, CODE_LANE + c), fix))
+            mark = jnp.where(sub_one == pick(line, CODE_LANE + c), 1.0, 0.0)
+            marks[p] = mark
+            f8[p] = spread_sum(jnp.where(sub == CAP + c, body, 0.0) + thrice(mark) * fix)
         return energy + fix * diff, sums + line
 
     zero = jnp.zeros((8, width), F32)
@@ -296,6 +299,7 @@
             tile = jnp.where(sub == CAP + c, z8[d * CAP + c], tile)
             kept = jnp.where(sub == CAP + c, x8[d * CAP + c], kept)
         message[d] = tile.astype(BF16)
+        exact[d] = tile
         held[d] = kept
 
 
@@ -367,7 +371,7 @@
 
 
 def last_kernel(
-    pairs, live, got1, got3, held, sent2, known, b, v1, v2, mass, stiff, hessian,
+    pairs, live, got1, got3, held, marks, exact, sent2, known, b, v1, v2, mass, stiff, hessian,
     message, part, d1_out, ad1_out, r2_out, ar2, known_out,
     x8, y8, tiles1, tiles3, corr, rim, edges,
 ):
@@ -396,19 +400,18 @@
     coefs, known_line = coefficients(known[...], sums, total(b_x), total(v1_x))
     known_out[...] = known_line
 
+    sub = iota((8, width), 0)
+
     def two(d, carry):
-        line = tiles1[d, 15:16, 128:256]
-        fix, values = corr[d], tiles3[d, 8:16, :]
-        kept, sent = held[d], sent2[d].astype(F32)
-        for c in range(CAP):
-            value = values[4 + c : 5 + c] + chosen(pick(line, CODE_LANE + c), fix)
-            value = value + sent[CAP + c : CAP + c + 1]
-            x8[d * CAP + c] = wide(
-                advance(kept[c : c + 1], kept[CAP + c : CAP + c + 1], value, coefs)[2]
-            )
+        sent = sent2[d].astype(F32)
+        second = pltpu.roll(tiles3[d, 8:16, :], 4, 0) + pltpu.roll(sent, 8 - CAP, 0)
+        for c in range(CAP):
+            p = d * CAP + c
+            x8[p] = spread_sum(jnp.where(sub == c, second, 0.0) + thrice(marks[p]) * corr[d])
         return carry
 
     lax.fori_loop(0, peers, two, 0, unroll=16)
+    contact_products(pairs, live[0, live.shape[1] - 1], x8, y8, hessian)
 
     me = lax.axis_index("gx")
     before, after = around(me, peers)
@@ -446,12 +449,23 @@
         sums = terms if sums is None else [s + t for s, t in zip(sums, terms)]
     sums = [total(value) for value in sums]
 
-    contact_products(pairs, live[0, live.shape[1] - 1], x8, y8, hessian)
-    line = packed_line([sums[0], sums[1] + contact_dot(x8, y8), sums[2]])
+    p_coef, q_coef = coefs[0] + coefs[2] * (1.0 + coefs[1]), coefs[0] * coefs[2]
+    dot = jnp.zeros((8, width), F32)
+    for d in range(peers):
+        kept, known_c = held[d], exact[d]
+        v2_o = jnp.zeros((8, width), F32)
+        cv2_o = v2_o
+        for c in range(CAP):
+            v2_o = jnp.where(sub == c, x8[d * CAP + c], v2_o)
+            cv2_o = jnp.where(sub == c, y8[d * CAP + c], cv2_o)
+        r2_o = kept - p_coef * pltpu.roll(kept, 8 - CAP, 0) + q_coef * v2_o
+        cr2_o = known_c - p_coef * pltpu.roll(known_c, 8 - CAP, 0) + q_coef * cv2_o
+        dot = dot + jnp.where(sub < CAP, r2_o * cr2_o, 0.0)
+        corr[d] = cr2_o
+    line = packed_line([sums[0], sums[1] + total(dot), sums[2]])
     line = jnp.concatenate([line, jnp.zeros((1, width - 128), F32)], axis=1)
     for d in range(peers):
-        rows = [y8[d * CAP + c, 0:1, :] for c in range(CAP)]
-        message[d] = jnp.concatenate([*rows, line], axis=0).astype(BF16)
+        message[d] = jnp.concatenate([corr[d, 0:CAP, :], line], axis=0).astype(BF16)
 
 
 def finish_kernel(
@@ -530,10 +544,10 @@
         name="start",
     )(token, routes, right_side, masses, stiffness)
     got1 = swap(sent1)
-    sent2, held, own, known1 = call(
+    sent2, held, own, known1, marks, exact = call(
         owner_kernel,
         "ssvv",
-        [second, held_shape, ((8, width), F32), line],
+        [second, held_shape, ((8, width), F32), line, ((peers * CAP, 8, block_len), F32), held_shape],
         [tiles, tiles, tiles, tiles, wide_tiles, rims, edges],
         32,
         name="owner",
@@ -549,13 +563,13 @@
     got3 = swap(sent3)
     sent4, part, d1, ad1, r2, ar2, known2 = call(
         last_kernel,
-        "ssvvvvvvvvvvv",
+        "ssvvvvvvvvvvvvv",
         [fourth, field, field, field, field, field, line],
         [tiles, tiles, wide_tiles, wide_tiles, rims, (8, width), edges],
         32,
         name="last",
     )(
-        pair_refs, routes, got1, got3, held, sent2, known, right_side, v1, v2, masses, stiffness,
+        pair_refs, routes, got1, got3, held, marks, exact, sent2, known, right_side, v1, v2, masses, stiffness,
         hessian,
     )
     got4 = swap(sent4)

time: 62.6 us -> 62 us (level)
  no operation moved by 1% of the time
where the time goes in v11:
time: 62 us; the launch traced here: 61.7 us
  blocking collectives  47.4 us (76%)
  Pallas kernels  11.9 us (19%)
  between operations  1.41 us (2%)
  local copies, waits for them, and re-layouts  0.97 us (2%)
    all_to_all x4, blocking collectives, swap(): lax.all_to_all(message, 'gx', split_axis=0, concat_axis=0, tiled=True)  47.4 us
    pallas_call x1, Pallas kernels, per_device(): call(owner_kernel, 'ssvv', [second, held_shape, ((8, width), F32), line,...  4.15 us
    pallas_call x1, Pallas kernels, per_device(): call(last_kernel, 'ssvvvvvvvvvvvvv', [fourth, field, field, field, field,...  3.1 us
    pallas_call x1, Pallas kernels, per_device(): call(finish_kernel, 'svvvvvvv', [field, field], [panels, (peers, 4, width...  1.82 us
    pallas_call x1, Pallas kernels, per_device(): call(middle_kernel, 'svvvvvvv', [third, field, field, line], [panels, pan...  1.57 us

profile of v11, /device:TPU:0, one launch (start us, length us, event | category | flops | bytes accessed | tf_op | source)
XLA Modules:
  0.0 61.7 jit_solution(14683171061805575404)
XLA Ops:
  1.3 0.0 copy-start.4
  1.3 0.0 copy-start
  1.3 0.0 copy-start.1
  1.3 0.0 copy-start.2
  1.3 0.0 slice-start
  1.3 0.0 slice-start.1
  1.4 0.0 copy-start.3
  1.4 0.0 slice-start.2
  1.4 0.5 copy-done.4
  1.9 0.1 pad_add_fusion.send.live
  2.0 0.3 copy-done
  2.3 0.1 copy-done.1
  2.4 0.0 copy-done.2
  2.4 1.2 %start.1 = (bf16[16,16,384]{2,1,0:T(8,128)(2,1)S(1)}, f32[3,64,512]{2,1,0:T(8,128)S(1)}) custom-call(f32[1,128]{1,0:T(1,128)S(1)} %announce.3._, s32[1,49]{1,0:T(1,128)S(1)} %pad_add_fusion.send.live, f32[3,64,512]{2,1,0:T(8,128)S(1)} %copy-done, f32[64,512]{1,0:T(8,128)S(1)} %copy-done.2, f32[2,64,512]{2,1,0:T(8,128)S(1)} %copy-done.1), custom_call_target="tpu_custom_call" | custom-call | tf_op jit(solution)/shard_map/start/pallas_call | solution.py:539
  3.6 16.4 %all_to_all.20.got.got1 = bf16[16,16,384]{2,1,0:T(8,128)(2,1)S(1)} all-to-all(bf16[16,16,384]{2,1,0:T(8,128)(2,1)S(1)} %get-tuple-element.21), channel_id=1, replica_groups=mesh['groups'=2,'gx'=16] {'gx'}, dimensions={0} | all-to-all | bytes 393216 | tf_op jit(solution)/shard_map/all_to_all | solution.py:534
  20.1 0.0 slice-done
  20.1 0.0 slice-done.1
  20.1 0.0 copy-done.3
  20.1 0.0 slice-done.2
  20.1 4.2 %owner.1 = (bf16[16,8,384]{2,1,0:T(8,128)(2,1)S(1)}, f32[16,8,384]{2,1,0:T(8,128)S(1)}, f32[8,384]{1,0:T(8,128)S(1)}, f32[1,128]{1,0:T(1,128)S(1)}, f32[48,8,128...) custom-call(s32[2,36]{1,0:T(2,128)S(1)} %bitcast.10, s32[1,49]{1,0:T(1,128)S(1)} %pad_add_fusion.send.live, ...), custom_call_target="tpu_custom_call" | custom-call | tf_op jit(solution)/shard_map/owner/pallas_call | solution.py:547
  24.3 10.0 %all_to_all.21.got2 = bf16[16,8,384]{2,1,0:T(8,128)(2,1)S(1)} all-to-all(bf16[16,8,384]{2,1,0:T(8,128)(2,1)S(1)} %get-tuple-element.22.sent2), channel_id=1, replica_groups=mesh['groups'=2,'gx'=16] {'gx'}, dimensions={0} | all-to-all | bytes 196608 | tf_op jit(solution)/shard_map/all_to_all | solution.py:534
  34.3 1.6 %middle.1 = (bf16[16,16,384]{2,1,0:T(8,128)(2,1)S(1)}, f32[3,64,512]{2,1,0:T(8,128)S(1)}, f32[3,64,512]{2,1,0:T(8,128)S(1)}, f32[1,128]{1,0:T(1,128)S(1)}) custom-call(s32[1,49]{1,0:T(1,128)S(1)} %pad_add_fusion.send.live, bf16[16,8,384]{2,1,0:T(8,128)(2,1)S(1)} %all_to_all.21.got2, f32[8,384]{1,0:T(8,128)S(1)} %get-tuple-element.23.own, ...), custom_call_target="tpu_custom_call" | custom-call | tf_op jit(solution)/shard_map/middle/pallas_call | solution.py:556
  35.8 11.6 %all_to_all.22.got3 = bf16[16,16,384]{2,1,0:T(8,128)(2,1)S(1)} all-to-all(bf16[16,16,384]{2,1,0:T(8,128)(2,1)S(1)} %get-tuple-element.26), channel_id=1, replica_groups=mesh['groups'=2,'gx'=16] {'gx'}, dimensions={0} | all-to-all | bytes 393216 | tf_op jit(solution)/shard_map/all_to_all | solution.py:534
  47.4 3.1 %last.1 = (bf16[16,4,384]{2,1,0:T(4,128)(2,1)S(1)}, f32[3,64,512]{2,1,0:T(8,128)S(1)}, f32[3,64,512]{2,1,0:T(8,128)S(1)}, f32[3,64,512]{2,1,0:T(8,128)S(1)}, f32...) custom-call(s32[2,36]{1,0:T(2,128)S(1)} %bitcast.11, s32[1,49]{1,0:T(1,128)S(1)} %pad_add_fusion.send.live, ...), custom_call_target="tpu_custom_call" | custom-call | tf_op jit(solution)/shard_map/last/pallas_call | solution.py:564
  50.5 9.3 %all_to_all.23.got4 = bf16[16,4,384]{2,1,0:T(4,128)(2,1)S(1)} all-to-all(bf16[16,4,384]{2,1,0:T(4,128)(2,1)S(1)} %get-tuple-element.33), channel_id=1, replica_groups=mesh['groups'=2,'gx'=16] {'gx'}, dimensions={0} | all-to-all | bytes 98304 | tf_op jit(solution)/shard_map/all_to_all | solution.py:534
  59.9 1.8 %finish.1 = (f32[3,64,512]{2,1,0:T(8,128)}, f32[3,64,512]{2,1,0:T(8,128)}) custom-call(s32[1,49]{1,0:T(1,128)S(1)} %pad_add_fusion.send.live, bf16[16,4,384]{2,1,0:T(4,128)(2,1)S(1)} %all_to_all.23.got4, f32[1,128]{1,0:T(1,128)S(1)} %get-tuple-element.34.known, f32[3,64,512]{2,1,0:T(8,128)S(1)} %get-tuple-element.35.part, ...), custom_call_target="tpu_custom_call" | custom-call | tf_op jit(solution)/shard_map/finish/pallas_call | solution.py:576
  (4 shorter events, 0.0 us)
Async XLA Ops:
  1.3 0.7 %copy-start.4 = (s32[1,48]{1,0:T(1,128)S(1)}, s32[1,48]{1,0:T(1,128)}, u32[]{:S(2)}) copy-start(s32[1,48]{1,0:T(1,128)} %param.11) | copy-start | bytes 580
  1.3 1.0 %copy-start = (f32[3,64,512]{2,1,0:T(8,128)S(1)}, f32[3,64,512]{2,1,0:T(8,128)}, u32[]{:S(2)}) copy-start(f32[3,64,512]{2,1,0:T(8,128)} %b.5) | copy-start | bytes 1179652
  1.3 1.1 %copy-start.1 = (f32[2,64,512]{2,1,0:T(8,128)S(1)}, f32[2,64,512]{2,1,0:T(8,128)}, u32[]{:S(2)}) copy-start(f32[2,64,512]{2,1,0:T(8,128)} %stiff.5) | copy-start | bytes 786436
  1.3 1.1 %copy-start.2 = (f32[64,512]{1,0:T(8,128)S(1)}, f32[64,512]{1,0:T(8,128)}, u32[]{:S(2)}) copy-start(f32[64,512]{1,0:T(8,128)} %mass.5) | copy-start | bytes 393220
  1.3 18.7 %slice-start = ((s8[10616832]{0:T(1024)(128)(4,1)}), s8[4194304]{0:T(1024)(128)(4,1)S(1)}, s32[]{:S(2)}) async-start(s8[10616832]{0:T(1024)(128)(4,1)} %bitcast.6), calls=%async_computation.4 | async-start | bytes 8388608
  1.3 18.7 %slice-start.1 = ((s8[10616832]{0:T(1024)(128)(4,1)}), s8[4194304]{0:T(1024)(128)(4,1)S(1)}, s32[]{:S(2)}) async-start(s8[10616832]{0:T(1024)(128)(4,1)} %bitcast.6), calls=%async_computation.5 | async-start | bytes 8388608
  1.4 18.7 %copy-start.3 = (s32[36,2]{0,1:T(2,128)S(1)}, s32[36,2]{0,1:T(2,128)}, u32[]{:S(2)}) copy-start(s32[36,2]{0,1:T(2,128)} %param.12) | copy-start | bytes 868
  1.4 18.7 %slice-start.2 = ((s8[10616832]{0:T(1024)(128)(4,1)}), s8[2228224]{0:T(1024)(128)(4,1)S(1)}, s32[]{:S(2)}) async-start(s8[10616832]{0:T(1024)(128)(4,1)} %bitcast.6), calls=%async_computation.6 | async-start | bytes 4456448
